TPU v7x, 32 devices: a whole 2x2x4 slice. The times are simulated.
32 devices in a mesh: row: 8 (over z, x), col: 4 (over y, core).
Axes of the slice: x: 2, y: 2, z: 4, core: 2. Of those that a mesh axis runs over, the one named last changes fastest.
Arguments:
- attn: bfloat16 [2048, 16384], P('col', 'row'), may hold values from -6 to 6
- grad_out: bfloat16 [2048, 16384], P('row', 'col'), may hold values from -0.119628906 to 0.119628906
- weight: bfloat16 [16384, 16384], P('row', 'col'), may hold values from -2.09375 to 2.09375
- momentum: bfloat16 [16384, 16384], P('row', 'col'), may hold values from -3 to 3
Outputs:
- grad_in: bfloat16 [2048, 16384], P('col', 'row')
- new_weight: bfloat16 [16384, 16384], P('row', 'col')
- new_momentum: bfloat16 [16384, 16384], P('row', 'col')
All inputs are finite; a program needn't handle non-finite values.
Results may differ from a plain program's by a relative error of at most 0.014.
Values may be sent and summed in bfloat16 or wider, within the bound.
No kernel may reach another device: no remote copies, remote signals or barrier semaphores. Data moves between devices by JAX's collectives and lax.ppermute only.
A program may use at most 192 MiB of HBM per device.

v0:
```python
import jax
import jax.numpy as jnp
from jax import lax
from jax.sharding import PartitionSpec as P


def shards(attn, grad_out, weight, momentum):
    contract_rows = (((0,), (0,)), ((), ()))
    contract_cols = (((1,), (1,)), ((), ()))
    grads_all = lax.all_gather(grad_out, "row", axis=0, tiled=True)
    rows_here = grads_all
    grad_w = lax.dot_general(
        lax.all_gather(attn, "col", axis=0, tiled=True),
        rows_here,
        contract_rows,
        preferred_element_type=jnp.float32,
    )
    rows_here = grads_all
    grad_in = lax.psum_scatter(
        lax.dot_general(
            rows_here, weight, contract_cols, preferred_element_type=jnp.float32
        ).astype(jnp.bfloat16),
        "col",
        scatter_dimension=0,
        tiled=True,
    )
    mom = 0.9 * momentum.astype(jnp.float32) + grad_w
    new_weight = (weight.astype(jnp.float32) - 0.25 * mom).astype(jnp.bfloat16)
    return (grad_in, new_weight, mom.astype(jnp.bfloat16))


def solution(mesh):
    in_specs = (P("col", "row"), P("row", "col"), P("row", "col"), P("row", "col"))
    out_specs = (P("col", "row"), P("row", "col"), P("row", "col"))
    return jax.shard_map(shards, mesh=mesh, in_specs=in_specs, out_specs=out_specs, check_vma=False)
```

profile of v0, /device:TPU:5, one launch (start us, length us, event | category | flops | bytes accessed | tf_op | source)
XLA Modules:
  0.0 377.5 jit_solution(1027493951913663154)
XLA Ops:
  7.2 0.0 all-gather.3.cloned.1.call-start
  7.2 0.7 all-gather.3.cloned.1.call-update
  7.9 0.0 all-gather.5.cloned.1.call-start
  7.9 0.7 all-gather.5.cloned.1.call-update
  8.6 0.0 reduce-scatter.2.cloned.1.call-start
  8.7 229.9 %all-gather.3.cloned.1.call-done = bf16[2048,4096]{1,0:T(8,128)(2,1)} async-done(((bf16[256,4096]{1,0:T(8,128)(2,1)}), bf16[2048,4096]{1,0:T(8,128)(2,1)}) %all-gather.3.cloned.1.call-update) | async-done | bytes 16777232 | tf_op jit(solution)/shard_map/all_gather | solution.py:10
  238.6 42.6 %convolution_convert_fusion = bf16[2048,2048]{1,0:T(8,128)(2,1)} fusion(bf16[2048,4096]{1,0:T(8,128)(2,1)} %all-gather.3.cloned.1.call-done, bf16[2048,4096]{1,0:T(8,128)(2,1)} %param.6), kind=kOutput, calls=%fused_computation.3 | convolution fusion | flops 34363932672 | bytes 41943040 | tf_op jit(solution)/shard_map/dot_general | solution.py:20
  281.1 0.0 reduce-scatter.2.cloned.1.call-update
  281.1 15.1 %all-gather.5.cloned.1.call-done = bf16[2048,2048]{1,0:T(8,128)(2,1)} async-done(((bf16[512,2048]{1,0:T(8,128)(2,1)}), bf16[2048,2048]{1,0:T(8,128)(2,1)}) %all-gather.5.cloned.1.call-update) | async-done | bytes 8388624 | tf_op jit(solution)/shard_map/all_gather | solution.py:13
  296.3 53.1 %fusion = (bf16[2048,4096]{1,0:T(8,128)(2,1)}, bf16[2048,4096]{1,0:T(8,128)(2,1)}) fusion(bf16[2048,4096]{1,0:T(8,128)(2,1)} %param.7, bf16[2048,4096]{1,0:T(8,128)(2,1)} %param.6, bf16[2048,2048]{1,0:T(8,128)(2,1)} %all-gather.5.cloned.1.call-done, bf16[2048,4096]{1,0:T(8,128)(2,1)} %all-gather.3.cloned.1.call-done), kind=kOutput, calls=%fused_computation.2 | convolution fusion | flops 34426847232 | bytes 92274688 | tf_op jit(solution)/shard_map/dot_general | solution.py:12
  349.4 21.6 %reduce-scatter.2.cloned.1.call-done = bf16[512,2048]{1,0:T(8,128)(2,1)} async-done(((bf16[2048,2048]{1,0:T(8,128)(2,1)}), bf16[512,2048]{1,0:T(8,128)(2,1)}) %reduce-scatter.2.cloned.1.call-update) | async-done | bytes 2097168 | tf_op jit(solution)/shard_map/reduce_scatter | solution.py:19
Async XLA Ops:
  7.2 231.4 %all-gather.3.cloned.1.call-start = ((), (), s32[]{:S(2)}) async-start(), calls=%async_computation.1 | async-start | bytes 18874368 | tf_op jit(solution)/shard_map/all_gather | solution.py:10
  7.9 288.4 %all-gather.5.cloned.1.call-start = ((), (), s32[]{:S(2)}) async-start(), calls=%async_computation.3 | async-start | bytes 10485760 | tf_op jit(solution)/shard_map/all_gather | solution.py:13
  8.6 362.3 %reduce-scatter.2.cloned.1.call-start = ((), (), s32[]{:S(2)}) async-start(), calls=%async_computation.2 | async-start | bytes 10485760 | tf_op jit(solution)/shard_map/reduce_scatter | solution.py:19
Sparse Core Ops, SparseCore 0:
  10.1 228.3 all-gather.2
  240.1 56.1 all-gather.4
  299.5 71.4 reduce-scatter.1
where the time goes:
time: 380 us; the launch traced here: 377 us
  waiting for transfers between devices  268 us (71%)
  matrix products  95.6 us (25%)
  between operations  13.7 us (4%)
    all_gather x1, waiting for transfers between devices, shards(): grads_all = lax.all_gather(grad_out, 'row', axis=0, tiled=True)  230 us
    dot_general x1, matrix products, shards(): lax.dot_general(lax.all_gather(attn, 'col', axis=0, tiled=True), rows_her...  53.1 us
    dot_general x1, matrix products, shards(): lax.dot_general(rows_here, weight, contract_cols, preferred_element_type=...  42.6 us
    reduce_scatter x1, waiting for transfers between devices, shards(): lax.psum_scatter(lax.dot_general(rows_here, weight, contract_cols, prefer...  21.6 us
    all_gather x1, waiting for transfers between devices, shards(): lax.all_gather(attn, 'col', axis=0, tiled=True)  15.1 us
  transfers between devices with their start and end apart: 3, of which 3 were waited for; matrix products, arithmetic and copies ran while one was open for 25% of the time, Pallas kernels for 0%

commit v1 on v0

v1 whole, which is shorter than its diff:
```python
import functools

import jax
import jax.numpy as jnp
import numpy as np
from jax import lax
from jax.experimental import pallas as pl
from jax.experimental.pallas import tpu as pltpu
from jax.sharding import PartitionSpec as P

BF16 = jnp.bfloat16
F32 = jnp.float32
NT = (((1,), (1,)), ((), ()))
TN = (((0,), (0,)), ((), ()))
VMEM_BYTES = 60 << 20


def snake(n):
    return list(range(0, n, 2)) + list(range(n - 1 - (n % 2), 0, -2))


def tie(*xs):
    return lax.optimization_barrier(xs)


def fit(size, want):
    while size % want:
        want //= 2
    return want


def call(kernel, grid, in_specs, out_specs, out_shape, scalars=(), scratch=(), aliases=None, flops=0, bytes_accessed=0):
    return pl.pallas_call(
        kernel,
        grid_spec=pltpu.PrefetchScalarGridSpec(
            num_scalar_prefetch=len(scalars), grid=grid, in_specs=in_specs, out_specs=out_specs, scratch_shapes=scratch
        ),
        out_shape=out_shape,
        input_output_aliases=aliases or {},
        compiler_params=pltpu.CompilerParams(vmem_limit_bytes=VMEM_BYTES),
        cost_estimate=pl.CostEstimate(flops=flops, bytes_accessed=bytes_accessed, transcendentals=0),
    )


def tokens_of(refs, parts):
    halves = [refs[i : i + parts] for i in range(0, len(refs), parts)]
    rows = [h[0][...] if parts == 1 else jnp.concatenate([r[...] for r in h], axis=1) for h in halves]
    return jnp.concatenate(rows)


def grad_in_kernel(*refs, n, parts):
    total = lax.dot_general(tokens_of(refs[:n], parts), refs[n][...], NT, preferred_element_type=F32)
    refs[-1][...] = total.astype(BF16)


def grad_in_sorted_kernel(me, take, *refs, n, parts, n_out, half):
    total = lax.dot_general(tokens_of(refs[:n], parts), refs[n][...], NT, preferred_element_type=F32).astype(BF16)
    for s in range(n_out):
        upper = take[me[0] * n_out + s] > 0
        refs[n + 1 + s][...] = jnp.where(upper, total[half:], total[:half])


def grad_in_part(pieces, weight, take=None, me=None, tile=512):
    parts, half = len(pieces[0]), pieces[0][0].shape[0]
    feats, cols = weight.shape
    rows = half * len(pieces)
    tile = fit(feats, tile)
    flat = [x for p in pieces for x in p]
    specs = [pl.BlockSpec(x.shape, lambda i, *_: (0, 0)) for x in flat]
    specs.append(pl.BlockSpec((tile, cols), lambda i, *_: (i, 0)))
    cost = dict(flops=2 * rows * feats * cols, bytes_accessed=2 * (rows * cols + feats * cols + rows * feats))
    if take is None:
        kernel = functools.partial(grad_in_kernel, n=len(flat), parts=parts)
        out = pl.BlockSpec((rows, tile), lambda i: (0, i))
        return call(kernel, (feats // tile,), specs, out, jax.ShapeDtypeStruct((rows, feats), BF16), **cost)(*flat, weight)
    n_out = take.shape[1]
    kernel = functools.partial(grad_in_sorted_kernel, n=len(flat), parts=parts, n_out=n_out, half=half)
    outs = [pl.BlockSpec((half, tile), lambda i, *_: (0, i))] * n_out
    shapes = [jax.ShapeDtypeStruct((half, feats), BF16)] * n_out
    return call(kernel, (feats // tile,), specs, outs, shapes, scalars=(me, take), **cost)(
        me, jnp.asarray(take.reshape(-1), jnp.int32), *flat, weight
    )


def assemble(dst, refs):
    at = 0
    for r in refs:
        dst[at : at + r.shape[0], :] = r[...]
        at += r.shape[0]


def pass_kernel(_, __, *refs, n, n_grads, last, n_old, rows):
    attn, grads, rest = refs[:n], refs[n : n + n_grads], refs[n + n_grads :]
    if last:
        acc_ref, w_ref = rest[:2]
        new_w, new_m, attn_s, grad_s = rest[2 + n_old :]
    else:
        m_ref, out, attn_s, grad_s = rest

    @pl.when(pl.program_id(0) == 0)
    def _():
        assemble(attn_s, attn)

    assemble(grad_s, grads)
    for c in range(0, attn_s.shape[1], rows):
        here = slice(c, c + rows)
        add = lax.dot_general(attn_s[:, here], grad_s[...], TN, preferred_element_type=F32)
        if last:
            mom = acc_ref[here].astype(F32) + add
            new_w[here] = (w_ref[here].astype(F32) - 0.25 * mom).astype(BF16)
            new_m[here] = mom.astype(BF16)
        else:
            out[here] = (0.9 * m_ref[here].astype(F32) + add).astype(out.dtype)


def token_pass(me, order, attn_all, pieces, wides, first_col=0, n_cols=None, old=(), out_dtype=None, tile=512):
    last = len(wides) == 2
    n = len(pieces)
    half = pieces[0][0].shape[0]
    feats, cols = wides[0].shape
    n_cols = n_cols or cols
    tile = fit(n_cols, tile)
    base = first_col // tile
    specs = [pl.BlockSpec((half, feats), lambda j, me, o, i=i: (o[me[0] * n + i], 0)) for i in range(n)]
    specs += [pl.BlockSpec((half, tile), lambda j, *_, c=(first_col - at) // tile: (0, j + c)) for _, at in pieces]
    wide = pl.BlockSpec((feats, tile), lambda j, *_: (0, j + base))
    specs += [wide] * len(wides) + [pl.BlockSpec(memory_space=pl.ANY)] * len(old)
    shape = jax.ShapeDtypeStruct((feats, cols), BF16 if last else out_dtype)
    return call(
        functools.partial(pass_kernel, n=n, n_grads=n, last=last, n_old=len(old), rows=fit(feats, 512)),
        (n_cols // tile,),
        specs,
        [wide, wide] if last else wide,
        [shape, shape] if last else shape,
        scalars=(me, order),
        scratch=[pltpu.VMEM((n * half, feats), BF16), pltpu.VMEM((n * half, tile), BF16)],
        aliases={2 + 2 * n + 2 + i: i for i in range(len(old))},
        flops=2 * n * half * feats * n_cols,
        bytes_accessed=8 * feats * n_cols,
    )(me, jnp.asarray(order.reshape(-1), jnp.int32), *([attn_all] * n), *[x for x, _ in pieces], *wides, *old)


def pair_sum_kernel(_, __, mine, other, out):
    out[...] = (mine[...].astype(F32) + other[...].astype(F32)).astype(BF16)


def pair_sum(me, which, mine, other, half):
    n, width = which.shape[1], mine.shape[1]
    picked = pl.BlockSpec((half, width), lambda i, me, w: (w[me[0] * n + i], 0))
    return call(
        pair_sum_kernel,
        (n,),
        [picked, picked],
        pl.BlockSpec((half, width), lambda i, *_: (i, 0)),
        jax.ShapeDtypeStruct((n * half, width), BF16),
        scalars=(me, which),
        bytes_accessed=6 * n * half * width,
    )(me, jnp.asarray(which.reshape(-1), jnp.int32), mine, other)


def place_kernel(me, _, valid, __, *refs, spans, total_slots):
    out, i = refs[-1], pl.program_id(0)
    flag = valid[me[0] * total_slots + i]
    at = 0
    for first, slots, n in spans:
        mine = refs[at : at + n]
        at += n

        @pl.when((flag == 1) & (i >= first) & (i < first + slots))
        def _():
            total = mine[0][...].astype(F32)
            for r in mine[1:]:
                total = total + r[...].astype(F32)
            out[...] = total.astype(BF16)

    if len(refs) > at + 1:

        @pl.when(flag == 2)
        def _():
            out[...] = refs[at][...]


def place(me, groups, out, shape, half):
    which = np.concatenate([g[0][0] for g in groups], axis=1)
    valid = np.concatenate([g[0][1] for g in groups], axis=1)
    where = np.concatenate([g[0][2] for g in groups], axis=1)
    n = which.shape[1]
    for d in range(len(valid)):
        real = np.flatnonzero(valid[d])
        if len(real) == 0:
            valid[d], where[d] = 2, 0
            continue
        for s in range(n):
            before = real[real <= s]
            where[d, s] = where[d, before[-1] if len(before) else real[0]]
    width = shape[1]
    specs, args, spans, first = [], [], [], 0
    for tables, picked, received in groups:
        slots = tables[0].shape[1]
        at = lambda i, f=first, s=slots: jnp.clip(i, f, f + s - 1)
        specs += [pl.BlockSpec((half, width), lambda i, me, w, v, p, at=at: (w[me[0] * n + at(i)], 0)) for _ in picked]
        specs += [pl.BlockSpec((half, width), lambda i, me, w, v, p, at=at, f=first: (at(i) - f, 0)) for _ in received]
        args += [*picked, *received]
        spans.append((first, slots, len(picked) + len(received)))
        first += slots
    spec = pl.BlockSpec((half, width), lambda i, me, w, v, p: (p[me[0] * n + i], 0))
    aliases = {}
    if out is not None:
        specs.append(spec if (valid == 2).any() else pl.BlockSpec(memory_space=pl.ANY))
        args.append(out)
        aliases = {4 + len(args) - 1: 0}
    kernel = functools.partial(place_kernel, spans=spans, total_slots=n)
    if out is not None and not (valid == 2).any():
        inner = kernel
        kernel = lambda *refs: inner(*refs[:-2], refs[-1])
    return call(
        kernel,
        (n,),
        specs,
        spec,
        jax.ShapeDtypeStruct(shape, BF16),
        scalars=(me, which, valid, where),
        aliases=aliases,
        bytes_accessed=8 * n * half * width,
    )(me, *[jnp.asarray(t.reshape(-1), jnp.int32) for t in (which, valid, where)], *args)


def body(n_row, n_col, attn, grad_out, weight, momentum):
    ring = np.array(snake(n_row))
    pos = np.argsort(ring)
    right = [(int(ring[i]), int(ring[(i + 1) % n_row])) for i in range(n_row)]
    left = [(b, a) for a, b in right]
    block, cols = grad_out.shape
    half = block // 2
    per_owner = n_row // n_col
    n_y = n_col // 2
    devices = [(r, c) for r in range(n_row) for c in range(n_col)]
    me = (lax.axis_index("row") * n_col + lax.axis_index("col")).astype(jnp.int32).reshape(1)
    out_shape = (per_owner * block, weight.shape[0])

    arrives = np.zeros((n_row, n_row, 2), np.int32)
    for r in range(n_row):
        for k in range(n_row):
            arrives[r, k, 0] = 2 * ring[(pos[r] - k) % n_row]
            arrives[r, k, 1] = 2 * ring[(pos[r] + k) % n_row] + 1

    def order_of(steps):
        return np.stack([arrives[r, np.array(steps)].reshape(-1) for r, _ in devices])

    def tables_of(steps):
        halves = arrives[:, np.array(steps), :].reshape(n_row, -1)
        owner = halves // (2 * per_owner)
        slots = max(int(np.sum(owner[r] == c)) for r, c in devices)
        which, valid, where = (np.zeros((n_row * n_col, slots), np.int32) for _ in range(3))
        for d, (r, c) in enumerate(devices):
            own = np.flatnonzero(owner[r] == c)
            spots = list(halves[r, own] % (2 * per_owner))
            spots += [s for s in range(2 * per_owner) if s not in spots]
            which[d, : len(own)] = own
            valid[d, : len(own)] = 1
            where[d] = spots[:slots]
        return which, valid, where

    def route(valid, shift):
        to = [(r, (c + shift) % n_col) for r, c in devices]
        return [(d, r * n_col + c) for d, (r, c) in enumerate(to) if valid[r * n_col + c].any()]

    def shifted(table, shift):
        return np.stack([table[r * n_col + (c + shift) % n_col] for r, c in devices])

    def reduce_in_pairs(steps, part):
        tables = tables_of(steps)
        (other,) = yield [lax.ppermute(part, "col", [(c, c ^ 1) for c in range(n_col)])]
        received = []
        for s in range(2, n_col, 2):
            sent = pair_sum(me, shifted(tables[0], s), part, other, half)
            received.append(lax.ppermute(sent, ("row", "col"), route(tables[1], s)))
        received = yield received
        done.append((tables, [part, other], received))

    def reduce_direct(step, parts):
        tables = tables_of([step])
        received = yield [lax.ppermute(parts[s], ("row", "col"), route(tables[1], s)) for s in range(1, n_col)]
        done.append((tables, [], [parts[0], *received]))

    def sorted_part(step):
        which = tables_of([step])[0]
        take = np.concatenate([shifted(which, s) for s in range(n_col)], axis=1)
        return grad_in_part(pieces_of([step]), weight, take, me)

    attn_all = lax.all_gather(attn, "col", axis=0, tiled=True)
    arrived = {0: (grad_out[:half], grad_out[half:])}
    pieces_of = lambda steps: [(x,) for k in steps for x in arrived[k]]
    whole_pieces = lambda steps: [(x, 0) for k in steps for x in arrived[k]]

    top = n_row - 1
    mid = n_row // 2
    early = list(range(0, mid - 1))
    late = list(range(mid - 1, n_row))
    at_work = {
        2: [("pairs", [0, 1])],
        mid: [("pairs", list(range(2, mid)))],
        mid + 1: [("first",)],
        top - 1: [("pairs", list(range(mid, top - 1)))],
        top: [("direct", top - 1)],
    }
    done, moving = [], []
    grad_in = None
    acc = None

    def turn(on_link, work):
        nonlocal moving
        flights = [f for _, f in moving]
        on_link, work, flights = tie(on_link, work, flights)
        moving = [[g, f] for (g, _), f in zip(moving, flights)]
        return on_link, work

    def advance():
        nonlocal moving
        still = []
        for g, f in moving:
            try:
                still.append([g, g.send(f)])
            except StopIteration:
                pass
        moving = still

    for k in range(1, n_row):
        a, b = arrived[k - 1]
        nxt = (lax.ppermute(a, "row", right), lax.ppermute(b, "row", left))
        jobs = at_work.get(k, [])
        results = []
        for job in jobs:
            if job[0] == "pairs":
                results.append([grad_in_part(pieces_of(job[1]), weight)])
            elif job[0] == "direct":
                results.append(sorted_part(job[1]))
            else:
                results.append([token_pass(me, order_of(early), attn_all, whole_pieces(early), (momentum,), out_dtype=BF16)])
        arrived[k], results = turn(nxt, results)
        advance()
        for job, result in zip(jobs, results):
            if job[0] == "first":
                acc = result[0]
                continue
            g = reduce_in_pairs(job[1], result[0]) if job[0] == "pairs" else reduce_direct(job[1], result)
            moving.append([g, next(g)])
    parts = sorted_part(top)
    if done:
        grad_in = place(me, done, None, out_shape, half)
        done.clear()
    parts, acc = tie(parts, acc)
    g = reduce_direct(top, parts)
    moving.append([g, next(g)])
    new_w, new_m = token_pass(me, order_of(late), attn_all, whole_pieces(late), (acc, weight))
    _, (new_w, new_m) = turn((), (new_w, new_m))
    while moving:
        advance()
    grad_in = place(me, done, grad_in, out_shape, half)
    return grad_in, new_w, new_m


def solution(mesh):
    n_row, n_col = mesh.shape["row"], mesh.shape["col"]
    spec, act = P("row", "col"), P("col", "row")

    def shards(attn, grad_out, weight, momentum):
        return body(n_row, n_col, attn, grad_out, weight, momentum)

    return jax.shard_map(shards, mesh=mesh, in_specs=(act, spec, spec, spec), out_specs=(act, spec, spec), check_vma=False)
```

time: 380 us -> 308 us (0.81)
  waiting for transfers between devices: 268 us -> 98.7 us
  Pallas kernels: 0 us -> 147 us
  matrix products: 95.6 us -> 0 us
  starting transfers between devices: 0.11 us -> 39.9 us
  local copies, waits for them, and re-layouts: 0 us -> 6.9 us
    all_gather x2 -> x1, waiting for transfers between devices: 245 us -> 0.01 us  [body(): attn_all = lax.all_gather(attn, 'col', axis=0, tiled=True)]
    pallas_call x0 -> x12, Pallas kernels: none -> 147 us  [the longest x2 60.4 us: token_pass(): call(functools.partial(pass_kernel, n=n, n_grads=n, last=last, n_old=len(...]
    ppermute x0 -> x26, waiting for transfers between devices: none -> 98 us  [the longest x14 84.3 us: body(): nxt = (lax.ppermute(a, 'row', right), lax.ppermute(b, 'row', left))]
    dot_general x2 -> x0, matrix products: 95.6 us -> none  [the longest x1 53.1 us: shards(): lax.dot_general(lax.all_gather(attn, 'col', axis=0, tiled=True), rows_her...]
    ppermute x0 -> x26, starting transfers between devices: none -> 39.9 us  [the longest x6 15.9 us: reduce_direct(): lax.ppermute(parts[s], ('row', 'col'), route(tables[1], s))]
    reduce_scatter x1 -> x0, waiting for transfers between devices: 21.6 us -> none  [shards(): lax.psum_scatter(lax.dot_general(rows_here, weight, contract_cols, prefer...]
    unnamed x0 -> x32, local copies, waits for them, and re-layouts: none -> 5.15 us
  transfers between devices with their start and end apart: 3 -> 27, of which waited for: 3 -> 15; matrix products, arithmetic and copies ran while one was open for 25% -> 1% of each run, Pallas kernels for 0% -> 45%
where the time goes in v1:
time: 308 us; the launch traced here: 306 us
  Pallas kernels  147 us (48%)
  waiting for transfers between devices  98.7 us (32%)
  starting transfers between devices  39.9 us (13%)
  between operations  14.2 us (5%)
  local copies, waits for them, and re-layouts  6.9 us (2%)
    ppermute x14, waiting for transfers between devices, body(): nxt = (lax.ppermute(a, 'row', right), lax.ppermute(b, 'row', left))  84.3 us
    pallas_call x2, Pallas kernels, token_pass(): call(functools.partial(pass_kernel, n=n, n_grads=n, last=last, n_old=len(...  60.4 us
    pallas_call x3, Pallas kernels, grad_in_part(): call(kernel, (feats // tile,), specs, out, jax.ShapeDtypeStruct((rows, fe...  41.3 us
    pallas_call x2, Pallas kernels, grad_in_part(): call(kernel, (feats // tile,), specs, outs, shapes, scalars=(me, take), *...  22 us
    ppermute x6, starting transfers between devices, reduce_direct(): lax.ppermute(parts[s], ('row', 'col'), route(tables[1], s))  15.9 us
    ppermute x3, waiting for transfers between devices, reduce_in_pairs(): received.append(lax.ppermute(sent, ('row', 'col'), route(tables[1], s)))  13.7 us
    pallas_call x2, Pallas kernels, place(): call(kernel, (n,), specs, spec, jax.ShapeDtypeStruct(shape, BF16), scalar...  12.5 us
    pallas_call x3, Pallas kernels, pair_sum(): call(pair_sum_kernel, (n,), [picked, picked], pl.BlockSpec((half, width),...  10.4 us
  transfers between devices with their start and end apart: 27, of which 15 were waited for; matrix products, arithmetic and copies ran while one was open for 1% of the time, Pallas kernels for 45%

profile of v1, /device:TPU:5, one launch (start us, length us, event | category | flops | bytes accessed | tf_op | source)
XLA Modules:
  0.0 306.3 jit_solution(1952582175633000063)
XLA Ops:
  7.9 1.8 fusion
  11.2 22.7 %collective-permute-done.1.refs_3_.refs_9_ = bf16[128,4096]{1,0:T(8,128)(2,1)S(1)} collective-permute-done((bf16[128,4096]{1,0:T(8,128)(2,1)S(1)}, bf16[128,4096]{1,0:T(8,128)(2,1)S(1)}, u32[]{:S(2)}, u32[]{:S(2)}) %collective-permute-start.1) | collective-permute-done | bytes 1048608 | tf_op jit(solution)/shard_map/ppermute | solution.py:330
  36.2 13.8 %shard_map.184.mine.refs_0_ = bf16[512,2048]{1,0:T(8,128)(2,1)} custom-call(bf16[128,4096]{1,0:T(8,128)(2,1)} %copy-done.5, bf16[128,4096]{1,0:T(8,128)(2,1)} %copy-done.4, bf16[128,4096]{1,0:T(8,128)(2,1)} %collective-permute-done.refs_2_.refs_8_, bf16[128,4096]{1,0:T(8,128)(2,1)} %copy-done.10, bf16[2048,4096]{1,0:T(8,128)(2,1)} %refs_21_.1), custom_call_target="tpu_custom_call" | custom-call | flops 8589934592 | bytes 23068672 | tf_op jit(solution)/shard_map/pallas_call | solution.py:75
  50.0 7.8 %collective-permute-done.2.refs_0_.refs_10_ = bf16[128,4096]{1,0:T(8,128)(2,1)} collective-permute-done((bf16[128,4096]{1,0:T(8,128)(2,1)}, bf16[128,4096]{1,0:T(8,128)(2,1)}, u32[]{:S(2)}, u32[]{:S(2)}) %collective-permute-start.2) | collective-permute-done | bytes 1048608 | tf_op jit(solution)/shard_map/ppermute | solution.py:330
  57.9 2.9 collective-permute-start.6
  62.3 23.6 %collective-permute-done.4.refs_2_.refs_10_ = bf16[128,4096]{1,0:T(8,128)(2,1)S(1)} collective-permute-done((bf16[128,4096]{1,0:T(8,128)(2,1)}, bf16[128,4096]{1,0:T(8,128)(2,1)S(1)}, u32[]{:S(2)}, u32[]{:S(2)}) %collective-permute-start.4) | collective-permute-done | bytes 1048608 | tf_op jit(solution)/shard_map/ppermute | solution.py:330
  88.3 3.7 %shard_map.186 = bf16[384,2048]{1,0:T(8,128)(2,1)} custom-call(s32[1]{0:T(128)} %bitcast._.me.refs_0_, s32[96]{0:T(128)} %constant.37.clone.__, bf16[512,2048]{1,0:T(8,128)(2,1)} %shard_map.184.mine.refs_0_, bf16[512,2048]{1,0:T(8,128)(2,1)} %copy-done.1), custom_call_target="tpu_custom_call" | custom-call | bytes 4718592 | tf_op jit(solution)/shard_map/pallas_call | solution.py:150
  92.0 3.3 %collective-permute-start.9 = (bf16[384,2048]{1,0:T(8,128)(2,1)}, bf16[384,2048]{1,0:T(8,128)(2,1)}, u32[]{:S(2)}, u32[]{:S(2)}) collective-permute-start(bf16[384,2048]{1,0:T(8,128)(2,1)} %shard_map.186), channel_id=1, source_target_pairs={{2,0},{3,1},{6,4},{7,5},{8,10},{10,8},{11,9},{12,14},{14,12},{15,1... | collective-permute-start | bytes 4718600 | tf_op jit(solution)/shard_map/ppermute | solution.py:277
  96.7 13.8 %shard_map.185.mine.refs_3_ = bf16[512,2048]{1,0:T(8,128)(2,1)} custom-call(bf16[128,4096]{1,0:T(8,128)(2,1)} %collective-permute-done.2.refs_0_.refs_10_, bf16[128,4096]{1,0:T(8,128)(2,1)} %collective-permute-done.3.refs_1_.refs_11_, bf16[128,4096]{1,0:T(8,128)(2,1)} %copy-done.7, bf16[128,4096]{1,0:T(8,128)(2,1)} %collective-permute-done.5.refs_3_.refs_11_, ...), custom_call_target="tpu_custom_call" | custom-call | flops 8589934592 | bytes 23068672 | tf_op jit(solution)/shard_map/pallas_call | solution.py:75
  110.5 8.3 %collective-permute-done.7.refs_0_.refs_12_ = bf16[128,4096]{1,0:T(8,128)(2,1)S(1)} collective-permute-done((bf16[128,4096]{1,0:T(8,128)(2,1)S(1)}, bf16[128,4096]{1,0:T(8,128)(2,1)S(1)}, u32[]{:S(2)}, u32[]{:S(2)}) %collective-permute-start.7) | collective-permute-done | bytes 1048608 | tf_op jit(solution)/shard_map/ppermute | solution.py:330
  118.8 2.1 collective-permute-done.8.refs_1_.refs_13_
  121.9 5.1 %collective-permute-done.9.refs_2_ = bf16[384,2048]{1,0:T(8,128)(2,1)} collective-permute-done((bf16[384,2048]{1,0:T(8,128)(2,1)}, bf16[384,2048]{1,0:T(8,128)(2,1)}, u32[]{:S(2)}, u32[]{:S(2)}) %collective-permute-start.9) | collective-permute-done | bytes 1572896 | tf_op jit(solution)/shard_map/ppermute | solution.py:277
  127.0 2.0 collective-permute-start.12
  130.5 23.0 %shard_map.187.refs_20_ = bf16[2048,4096]{1,0:T(8,128)(2,1)} custom-call(s32[1]{0:T(128)} %bitcast._.me.refs_0_, s32[192]{0:T(256)} %constant.38.clone.__, bf16[2048,2048]{1,0:T(8,128)(2,1)} %all-gather.2.cloned.1.call-done.refs_0_.refs_1_.refs_2_.refs_3_.refs_4_.refs_5_.refs_6_.refs_7_.refs_8_.refs_9_, ...), custom_call_target="tpu_custom_call" | custom-call | flops 12884901888 | bytes 67108864 | tf_op jit(solution)/shard_map/pallas_call | solution.py:129
  153.9 3.2 %collective-permute-done.11.refs_3_.refs_15_ = bf16[128,4096]{1,0:T(8,128)(2,1)} collective-permute-done((bf16[128,4096]{1,0:T(8,128)(2,1)}, bf16[128,4096]{1,0:T(8,128)(2,1)}, u32[]{:S(2)}, u32[]{:S(2)}) %collective-permute-start.11) | collective-permute-done | bytes 1048608 | tf_op jit(solution)/shard_map/ppermute | solution.py:330
  158.5 3.0 shard_map.189
  161.4 2.2 collective-permute-start.15
  165.2 13.8 %shard_map.188.mine.refs_4_ = bf16[512,2048]{1,0:T(8,128)(2,1)} custom-call(bf16[128,4096]{1,0:T(8,128)(2,1)} %copy-done.8, bf16[128,4096]{1,0:T(8,128)(2,1)} %copy-done.9, bf16[128,4096]{1,0:T(8,128)(2,1)} %collective-permute-done.10.refs_2_.refs_14_, bf16[128,4096]{1,0:T(8,128)(2,1)} %collective-permute-done.11.refs_3_.refs_15_, bf16[2048,4096]{1,0:T(8,128)(2,1)} %refs_21_.1), custom_call_target="tpu_custom_call" | custom-call | flops 8589934592 | bytes 23068672 | tf_op jit(solution)/shard_map/pallas_call | solution.py:75
  178.9 8.6 %collective-permute-done.15.refs_5_ = bf16[256,2048]{1,0:T(8,128)(2,1)S(1)} collective-permute-done((bf16[256,2048]{1,0:T(8,128)(2,1)}, bf16[256,2048]{1,0:T(8,128)(2,1)S(1)}, u32[]{:S(2)}, u32[]{:S(2)}) %collective-permute-start.15) | collective-permute-done | bytes 1048608 | tf_op jit(solution)/shard_map/ppermute | solution.py:277
  188.9 1.7 collective-permute-start.18
  192.1 11.0 %shard_map.190 = (bf16[128,2048]{1,0:T(8,128)(2,1)}, bf16[128,2048]{1,0:T(8,128)(2,1)}, bf16[128,2048]{1,0:T(8,128)(2,1)}, bf16[128,2048]{1,0:T(8,128)(2,1)}) custom-call(s32[1]{0:T(128)} %bitcast._.me.refs_0_, s32[128]{0:T(128)} %constant.40.clone.take, bf16[128,4096]{1,0:T(8,128)(2,1)} %copy-done.3, ...), custom_call_target="tpu_custom_call" | custom-call | flops 4294967296 | bytes 19922944 | tf_op jit(solution)/shard_map/pallas_call | solution.py:80
  203.0 12.4 %collective-permute-done.16.refs_0_.refs_18_ = bf16[128,4096]{1,0:T(8,128)(2,1)} collective-permute-done((bf16[128,4096]{1,0:T(8,128)(2,1)S(1)}, bf16[128,4096]{1,0:T(8,128)(2,1)}, u32[]{:S(2)}, u32[]{:S(2)}) %collective-permute-start.16) | collective-permute-done | bytes 1048608 | tf_op jit(solution)/shard_map/ppermute | solution.py:330
  216.4 5.6 %collective-permute-start.21 = (bf16[128,2048]{1,0:T(8,128)(2,1)}, bf16[128,2048]{1,0:T(8,128)(2,1)S(1)}, u32[]{:S(2)}, u32[]{:S(2)}) collective-permute-start(bf16[128,2048]{1,0:T(8,128)(2,1)} %get-tuple-element.87), channel_id=1, source_target_pairs={{0,2},{3,1},{4,6},{7,5},{9,11},{10,8},{13,15},{14,12},{17,19},{18,... | collective-permute-start | bytes 1572872 | tf_op jit(solution)/shard_map/ppermute | solution.py:283
  222.0 5.8 %shard_map.194.refs_15_ = bf16[512,2048]{1,0:T(8,128)(2,1)} custom-call(s32[1]{0:T(128)} %bitcast._.me.refs_0_, s32[160]{0:T(256)} %constant.43.clone._, s32[160]{0:T(256)} %constant.44.clone.valid, s32[160]{0:T(256)} %constant.45.clone.__, bf16[512,2048]{1,0:T(8,128)(2,1)} %shard_map.184.mine.refs_0_, bf16[512,2048]{1,0:T(8,128)(2,1)} %copy-done.1, ...), custom_call_target="tpu_custom_call" | custom-call | bytes 10485760 | tf_op jit(solution)/shard_map/pallas_call | solution.py:216
  229.2 3.7 %shard_map.193 = bf16[384,2048]{1,0:T(8,128)(2,1)} custom-call(s32[1]{0:T(128)} %bitcast._.me.refs_0_, s32[96]{0:T(128)} %constant.41.clone.__, bf16[512,2048]{1,0:T(8,128)(2,1)} %shard_map.188.mine.refs_4_, bf16[512,2048]{1,0:T(8,128)(2,1)} %copy-done), custom_call_target="tpu_custom_call" | custom-call | bytes 4718592 | tf_op jit(solution)/shard_map/pallas_call | solution.py:150
  232.9 1.5 collective-permute-start.19
  234.4 11.0 %shard_map.191 = (bf16[128,2048]{1,0:T(8,128)(2,1)}, bf16[128,2048]{1,0:T(8,128)(2,1)}, bf16[128,2048]{1,0:T(8,128)(2,1)}, bf16[128,2048]{1,0:T(8,128)(2,1)}) custom-call(s32[1]{0:T(128)} %bitcast._.me.refs_0_, s32[128]{0:T(128)} %constant.42.clone.take, bf16[128,4096]{1,0:T(8,128)(2,1)} %collective-permute-done.16.refs_0_.refs_18_, ...), custom_call_target="tpu_custom_call" | custom-call | flops 4294967296 | bytes 19922944 | tf_op jit(solution)/shard_map/pallas_call | solution.py:80
  245.4 4.8 %collective-permute-start.23 = (bf16[128,2048]{1,0:T(8,128)(2,1)}, bf16[128,2048]{1,0:T(8,128)(2,1)S(1)}, u32[]{:S(2)}, u32[]{:S(2)}) collective-permute-start(bf16[128,2048]{1,0:T(8,128)(2,1)} %get-tuple-element.89), channel_id=1, source_target_pairs={{0,1},{3,0},{4,5},{7,4},{9,10},{11,8},{13,14},{15,12},{16,17},{18,... | collective-permute-start | bytes 1572872 | tf_op jit(solution)/shard_map/ppermute | solution.py:283
  250.2 2.1 collective-permute-start.24
  252.3 1.5 collective-permute-start.25
  253.8 37.4 %shard_map.192 = (bf16[2048,4096]{1,0:T(8,128)(2,1)}, bf16[2048,4096]{1,0:T(8,128)(2,1)}) custom-call(s32[1]{0:T(128)} %bitcast._.me.refs_0_, s32[320]{0:T(512)} %constant.46.clone.__, bf16[2048,2048]{1,0:T(8,128)(2,1)} %all-gather.2.cloned.1.call-done.refs_0_.refs_1_.refs_2_.refs_3_.refs_4_.refs_5_.refs_6_.refs_7_.refs_8_.refs_9_, ...), custom_call_target="tpu_custom_call" | custom-call | flops 21474836480 | bytes 67108864 | tf_op jit(solution)/shard_map/pallas_call | solution.py:129
  292.8 6.6 %shard_map.195 = bf16[512,2048]{1,0:T(8,128)(2,1)} custom-call(s32[1]{0:T(128)} %bitcast._.me.refs_0_, s32[160]{0:T(256)} %constant.47.clone.refs_1_, s32[160]{0:T(256)} %constant.48.clone.refs_2_, s32[160]{0:T(256)} %constant.49.clone.refs_3_, bf16[512,2048]{1,0:T(8,128)(2,1)} %shard_map.188.mine.refs_4_, ...), custom_call_target="tpu_custom_call", output_to_operand_aliasing={{}: (15, {})} | custom-call | bytes 10485760 | tf_op jit(solution)/shard_map/pallas_call | solution.py:216
  (68 shorter events, 22.3 us)
Async XLA Ops:
  7.2 123.3 %all-gather.2.cloned.1.call-start = ((), (), s32[]{:S(2)}) async-start(), calls=%async_computation | async-start | bytes 10485760 | tf_op jit(solution)/shard_map/all_gather | solution.py:291
  9.7 26.6 %copy-start.4 = (bf16[128,4096]{1,0:T(8,128)(2,1)}, bf16[128,4096]{1,0:T(8,128)(2,1)S(1)}, u32[]{:S(2)}) copy-start(bf16[128,4096]{1,0:T(8,128)(2,1)S(1)} %get-tuple-element.105.refs_1_.refs_7_) | copy-start | bytes 3145732
  9.7 26.6 %copy-start.5 = (bf16[128,4096]{1,0:T(8,128)(2,1)}, bf16[128,4096]{1,0:T(8,128)(2,1)S(1)}, u32[]{:S(2)}) copy-start(bf16[128,4096]{1,0:T(8,128)(2,1)S(1)} %get-tuple-element.106.refs_0_.refs_6_) | copy-start | bytes 3145732
  9.7 24.2 %collective-permute-start.1 = (bf16[128,4096]{1,0:T(8,128)(2,1)S(1)}, bf16[128,4096]{1,0:T(8,128)(2,1)S(1)}, u32[]{:S(2)}, u32[]{:S(2)}) collective-permute-start(bf16[128,4096]{1,0:T(8,128)(2,1)S(1)} %get-tuple-element.105.refs_1_.refs_7_), channel_id=1, source_target_pairs={{8,0},{16,8},{24,16},{28,24},{20,28},{12,20},{4,12},{0,4},{9,1},{1... | collective-permute-start | bytes 3145736 | tf_op jit(solution)/shard_map/ppermute | solution.py:330
  10.9 23.8 %collective-permute-start = (bf16[128,4096]{1,0:T(8,128)(2,1)S(1)}, bf16[128,4096]{1,0:T(8,128)(2,1)}, u32[]{:S(2)}, u32[]{:S(2)}) collective-permute-start(bf16[128,4096]{1,0:T(8,128)(2,1)S(1)} %get-tuple-element.106.refs_0_.refs_6_), channel_id=1, source_target_pairs={{0,8},{8,16},{16,24},{24,28},{28,20},{20,12},{12,4},{4,0},{1,9},{9... | collective-permute-start | bytes 3145736 | tf_op jit(solution)/shard_map/ppermute | solution.py:330
  34.8 23.1 %collective-permute-start.2 = (bf16[128,4096]{1,0:T(8,128)(2,1)}, bf16[128,4096]{1,0:T(8,128)(2,1)}, u32[]{:S(2)}, u32[]{:S(2)}) collective-permute-start(bf16[128,4096]{1,0:T(8,128)(2,1)} %collective-permute-done.refs_2_.refs_8_), channel_id=1, source_target_pairs={{0,8},{8,16},{16,24},{24,28},{28,20},{20,12},{12,4},{4,0},{1,9},{9... | collective-permute-start | bytes 3145736 | tf_op jit(solution)/shard_map/ppermute | solution.py:330
  35.2 22.8 %collective-permute-start.3 = (bf16[128,4096]{1,0:T(8,128)(2,1)S(1)}, bf16[128,4096]{1,0:T(8,128)(2,1)}, u32[]{:S(2)}, u32[]{:S(2)}) collective-permute-start(bf16[128,4096]{1,0:T(8,128)(2,1)S(1)} %collective-permute-done.1.refs_3_.refs_9_), channel_id=1, source_target_pairs={{8,0},{16,8},{24,16},{28,24},{20,28},{12,20},{4,12},{0,4},{9,1},{1... | collective-permute-start | bytes 3145736 | tf_op jit(solution)/shard_map/ppermute | solution.py:330
  57.9 29.0 %collective-permute-start.6 = (bf16[512,2048]{1,0:T(8,128)(2,1)}, bf16[512,2048]{1,0:T(8,128)(2,1)S(1)}, u32[]{:S(2)}, u32[]{:S(2)}) collective-permute-start(bf16[512,2048]{1,0:T(8,128)(2,1)} %shard_map.184.mine.refs_0_), channel_id=1, source_target_pairs={{0,1},{1,0},{2,3},{3,2},{4,5},{5,4},{6,7},{7,6},{8,9},{9,8},{10,11... | collective-permute-start | bytes 6291464 | tf_op jit(solution)/shard_map/ppermute | solution.py:273
  60.8 25.1 %collective-permute-start.4 = (bf16[128,4096]{1,0:T(8,128)(2,1)}, bf16[128,4096]{1,0:T(8,128)(2,1)S(1)}, u32[]{:S(2)}, u32[]{:S(2)}) collective-permute-start(bf16[128,4096]{1,0:T(8,128)(2,1)} %collective-permute-done.2.refs_0_.refs_10_), channel_id=1, source_target_pairs={{0,8},{8,16},{16,24},{24,28},{28,20},{20,12},{12,4},{4,0},{1,9},{9... | collective-permute-start | bytes 3145736 | tf_op jit(solution)/shard_map/ppermute | solution.py:330
  62.1 24.8 %collective-permute-start.5 = (bf16[128,4096]{1,0:T(8,128)(2,1)}, bf16[128,4096]{1,0:T(8,128)(2,1)}, u32[]{:S(2)}, u32[]{:S(2)}) collective-permute-start(bf16[128,4096]{1,0:T(8,128)(2,1)} %collective-permute-done.3.refs_1_.refs_11_), channel_id=1, source_target_pairs={{8,0},{16,8},{24,16},{28,24},{20,28},{12,20},{4,12},{0,4},{9,1},{1... | collective-permute-start | bytes 3145736 | tf_op jit(solution)/shard_map/ppermute | solution.py:330
  92.0 35.0 %collective-permute-start.9 = (bf16[384,2048]{1,0:T(8,128)(2,1)}, bf16[384,2048]{1,0:T(8,128)(2,1)}, u32[]{:S(2)}, u32[]{:S(2)}) collective-permute-start(bf16[384,2048]{1,0:T(8,128)(2,1)} %shard_map.186), channel_id=1, source_target_pairs={{2,0},{3,1},{6,4},{7,5},{8,10},{10,8},{11,9},{12,14},{14,12},{15,1... | collective-permute-start | bytes 4718600 | tf_op jit(solution)/shard_map/ppermute | solution.py:277
  95.2 23.6 %collective-permute-start.7 = (bf16[128,4096]{1,0:T(8,128)(2,1)S(1)}, bf16[128,4096]{1,0:T(8,128)(2,1)S(1)}, u32[]{:S(2)}, u32[]{:S(2)}) collective-permute-start(bf16[128,4096]{1,0:T(8,128)(2,1)S(1)} %collective-permute-done.4.refs_2_.refs_10_), channel_id=1, source_target_pairs={{0,8},{8,16},{16,24},{24,28},{28,20},{20,12},{12,4},{4,0},{1,9},{9... | collective-permute-start | bytes 3145736 | tf_op jit(solution)/shard_map/ppermute | solution.py:330
  96.5 24.4 %collective-permute-start.8 = (bf16[128,4096]{1,0:T(8,128)(2,1)}, bf16[128,4096]{1,0:T(8,128)(2,1)S(1)}, u32[]{:S(2)}, u32[]{:S(2)}) collective-permute-start(bf16[128,4096]{1,0:T(8,128)(2,1)} %collective-permute-done.5.refs_3_.refs_11_), channel_id=1, source_target_pairs={{8,0},{16,8},{24,16},{28,24},{20,28},{12,20},{4,12},{0,4},{9,1},{1... | collective-permute-start | bytes 3145736 | tf_op jit(solution)/shard_map/ppermute | solution.py:330
  118.8 34.6 %copy-start.8 = (bf16[128,4096]{1,0:T(8,128)(2,1)}, bf16[128,4096]{1,0:T(8,128)(2,1)S(1)}, u32[]{:S(2)}) copy-start(bf16[128,4096]{1,0:T(8,128)(2,1)S(1)} %collective-permute-done.7.refs_0_.refs_12_) | copy-start | bytes 3145732
  127.0 30.2 %collective-permute-start.12 = (bf16[512,2048]{1,0:T(8,128)(2,1)}, bf16[512,2048]{1,0:T(8,128)(2,1)S(1)}, u32[]{:S(2)}, u32[]{:S(2)}) collective-permute-start(bf16[512,2048]{1,0:T(8,128)(2,1)} %shard_map.185.mine.refs_3_), channel_id=1, source_target_pairs={{0,1},{1,0},{2,3},{3,2},{4,5},{5,4},{6,7},{7,6},{8,9},{9,8},{10,11... | collective-permute-start | bytes 6291464 | tf_op jit(solution)/shard_map/ppermute | solution.py:273
  129.0 24.9 %collective-permute-start.10 = (bf16[128,4096]{1,0:T(8,128)(2,1)S(1)}, bf16[128,4096]{1,0:T(8,128)(2,1)}, u32[]{:S(2)}, u32[]{:S(2)}) collective-permute-start(bf16[128,4096]{1,0:T(8,128)(2,1)S(1)} %collective-permute-done.7.refs_0_.refs_12_), channel_id=1, source_target_pairs={{0,8},{8,16},{16,24},{24,28},{28,20},{20,12},{12,4},{4,0},{1,9},{9... | collective-permute-start | bytes 3145736 | tf_op jit(solution)/shard_map/ppermute | solution.py:330
  130.3 26.8 %collective-permute-start.11 = (bf16[128,4096]{1,0:T(8,128)(2,1)}, bf16[128,4096]{1,0:T(8,128)(2,1)}, u32[]{:S(2)}, u32[]{:S(2)}) collective-permute-start(bf16[128,4096]{1,0:T(8,128)(2,1)} %copy-done.9), channel_id=1, source_target_pairs={{8,0},{16,8},{24,16},{28,24},{20,28},{12,20},{4,12},{0,4},{9,1},{1... | collective-permute-start | bytes 3145736 | tf_op jit(solution)/shard_map/ppermute | solution.py:330
  161.4 26.1 %collective-permute-start.15 = (bf16[256,2048]{1,0:T(8,128)(2,1)}, bf16[256,2048]{1,0:T(8,128)(2,1)S(1)}, u32[]{:S(2)}, u32[]{:S(2)}) collective-permute-start(bf16[256,2048]{1,0:T(8,128)(2,1)} %shard_map.189), channel_id=1, source_target_pairs={{0,2},{1,3},{3,1},{4,6},{5,7},{7,5},{9,11},{10,8},{11,9},{13,15},{... | collective-permute-start | bytes 3145736 | tf_op jit(solution)/shard_map/ppermute | solution.py:277
  163.7 25.2 %collective-permute-start.13 = (bf16[128,4096]{1,0:T(8,128)(2,1)}, bf16[128,4096]{1,0:T(8,128)(2,1)S(1)}, u32[]{:S(2)}, u32[]{:S(2)}) collective-permute-start(bf16[128,4096]{1,0:T(8,128)(2,1)} %collective-permute-done.10.refs_2_.refs_14_), channel_id=1, source_target_pairs={{0,8},{8,16},{16,24},{24,28},{28,20},{20,12},{12,4},{4,0},{1,9},{9... | collective-permute-start | bytes 3145736 | tf_op jit(solution)/shard_map/ppermute | solution.py:330
  164.7 24.2 %collective-permute-start.14 = (bf16[128,4096]{1,0:T(8,128)(2,1)}, bf16[128,4096]{1,0:T(8,128)(2,1)}, u32[]{:S(2)}, u32[]{:S(2)}) collective-permute-start(bf16[128,4096]{1,0:T(8,128)(2,1)} %collective-permute-done.11.refs_3_.refs_15_), channel_id=1, source_target_pairs={{8,0},{16,8},{24,16},{28,24},{20,28},{12,20},{4,12},{0,4},{9,1},{1... | collective-permute-start | bytes 3145736 | tf_op jit(solution)/shard_map/ppermute | solution.py:330
  188.9 26.8 %collective-permute-start.18 = (bf16[512,2048]{1,0:T(8,128)(2,1)}, bf16[512,2048]{1,0:T(8,128)(2,1)S(1)}, u32[]{:S(2)}, u32[]{:S(2)}) collective-permute-start(bf16[512,2048]{1,0:T(8,128)(2,1)} %shard_map.188.mine.refs_4_), channel_id=1, source_target_pairs={{0,1},{1,0},{2,3},{3,2},{4,5},{5,4},{6,7},{7,6},{8,9},{9,8},{10,11... | collective-permute-start | bytes 6291464 | tf_op jit(solution)/shard_map/ppermute | solution.py:273
  190.6 24.9 %collective-permute-start.16 = (bf16[128,4096]{1,0:T(8,128)(2,1)S(1)}, bf16[128,4096]{1,0:T(8,128)(2,1)}, u32[]{:S(2)}, u32[]{:S(2)}) collective-permute-start(bf16[128,4096]{1,0:T(8,128)(2,1)S(1)} %collective-permute-done.13.refs_0_.refs_16_), channel_id=1, source_target_pairs={{0,8},{8,16},{16,24},{24,28},{28,20},{20,12},{12,4},{4,0},{1,9},{9... | collective-permute-start | bytes 3145736 | tf_op jit(solution)/shard_map/ppermute | solution.py:330
  191.0 24.8 %collective-permute-start.17 = (bf16[128,4096]{1,0:T(8,128)(2,1)}, bf16[128,4096]{1,0:T(8,128)(2,1)}, u32[]{:S(2)}, u32[]{:S(2)}) collective-permute-start(bf16[128,4096]{1,0:T(8,128)(2,1)} %collective-permute-done.14.refs_1_.refs_17_), channel_id=1, source_target_pairs={{8,0},{16,8},{24,16},{28,24},{20,28},{12,20},{4,12},{0,4},{9,1},{1... | collective-permute-start | bytes 3145736 | tf_op jit(solution)/shard_map/ppermute | solution.py:330
  215.7 34.5 %collective-permute-start.20 = (bf16[128,2048]{1,0:T(8,128)(2,1)}, bf16[128,2048]{1,0:T(8,128)(2,1)S(1)}, u32[]{:S(2)}, u32[]{:S(2)}) collective-permute-start(bf16[128,2048]{1,0:T(8,128)(2,1)} %get-tuple-element.86), channel_id=1, source_target_pairs={{0,1},{1,2},{4,5},{5,6},{10,11},{11,8},{14,15},{15,12},{18,19},{19... | collective-permute-start | bytes 1572872 | tf_op jit(solution)/shard_map/ppermute | solution.py:283
  216.4 35.9 %collective-permute-start.21 = (bf16[128,2048]{1,0:T(8,128)(2,1)}, bf16[128,2048]{1,0:T(8,128)(2,1)S(1)}, u32[]{:S(2)}, u32[]{:S(2)}) collective-permute-start(bf16[128,2048]{1,0:T(8,128)(2,1)} %get-tuple-element.87), channel_id=1, source_target_pairs={{0,2},{3,1},{4,6},{7,5},{9,11},{10,8},{13,15},{14,12},{17,19},{18,... | collective-permute-start | bytes 1572872 | tf_op jit(solution)/shard_map/ppermute | solution.py:283
  227.9 63.4 %collective-permute-start.22 = (bf16[128,2048]{1,0:T(8,128)(2,1)}, bf16[128,2048]{1,0:T(8,128)(2,1)S(1)}, u32[]{:S(2)}, u32[]{:S(2)}) collective-permute-start(bf16[128,2048]{1,0:T(8,128)(2,1)} %get-tuple-element.88), channel_id=1, source_target_pairs={{2,1},{3,2},{6,5},{7,6},{8,11},{9,8},{12,15},{13,12},{16,19},{17,1... | collective-permute-start | bytes 1572872 | tf_op jit(solution)/shard_map/ppermute | solution.py:283
  232.9 58.4 %collective-permute-start.19 = (bf16[384,2048]{1,0:T(8,128)(2,1)}, bf16[384,2048]{1,0:T(8,128)(2,1)S(1)}, u32[]{:S(2)}, u32[]{:S(2)}) collective-permute-start(bf16[384,2048]{1,0:T(8,128)(2,1)} %shard_map.193), channel_id=1, source_target_pairs={{0,2},{1,3},{4,6},{5,7},{8,10},{9,11},{11,9},{12,14},{13,15},{15,1... | collective-permute-start | bytes 4718600 | tf_op jit(solution)/shard_map/ppermute | solution.py:277
  245.4 45.8 %collective-permute-start.23 = (bf16[128,2048]{1,0:T(8,128)(2,1)}, bf16[128,2048]{1,0:T(8,128)(2,1)S(1)}, u32[]{:S(2)}, u32[]{:S(2)}) collective-permute-start(bf16[128,2048]{1,0:T(8,128)(2,1)} %get-tuple-element.89), channel_id=1, source_target_pairs={{0,1},{3,0},{4,5},{7,4},{9,10},{11,8},{13,14},{15,12},{16,17},{18,... | collective-permute-start | bytes 1572872 | tf_op jit(solution)/shard_map/ppermute | solution.py:283
  250.2 41.0 %copy-start.12 = (bf16[128,2048]{1,0:T(8,128)(2,1)}, bf16[128,2048]{1,0:T(8,128)(2,1)S(1)}, u32[]{:S(2)}) copy-start(bf16[128,2048]{1,0:T(8,128)(2,1)S(1)} %collective-permute-done.20.refs_8_) | copy-start | bytes 1572868
  250.2 41.1 %collective-permute-start.24 = (bf16[128,2048]{1,0:T(8,128)(2,1)}, bf16[128,2048]{1,0:T(8,128)(2,1)}, u32[]{:S(2)}, u32[]{:S(2)}) collective-permute-start(bf16[128,2048]{1,0:T(8,128)(2,1)} %get-tuple-element.90), channel_id=1, source_target_pairs={{2,0},{3,1},{6,4},{7,5},{8,10},{10,8},{12,14},{14,12},{17,19},{19,... | collective-permute-start | bytes 1572872 | tf_op jit(solution)/shard_map/ppermute | solution.py:283
  252.3 38.9 %copy-start.13 = (bf16[128,2048]{1,0:T(8,128)(2,1)}, bf16[128,2048]{1,0:T(8,128)(2,1)S(1)}, u32[]{:S(2)}) copy-start(bf16[128,2048]{1,0:T(8,128)(2,1)S(1)} %collective-permute-done.21.refs_9_) | copy-start | bytes 1572868
  252.3 39.0 %collective-permute-start.25 = (bf16[128,2048]{1,0:T(8,128)(2,1)}, bf16[128,2048]{1,0:T(8,128)(2,1)}, u32[]{:S(2)}, u32[]{:S(2)}) collective-permute-start(bf16[128,2048]{1,0:T(8,128)(2,1)} %get-tuple-element.91), channel_id=1, source_target_pairs={{1,0},{2,1},{5,4},{6,5},{9,8},{11,10},{13,12},{15,14},{16,19},{18,... | collective-permute-start | bytes 1572872 | tf_op jit(solution)/shard_map/ppermute | solution.py:283
  (11 other events, 36.7 us)
Sparse Core Ops, SparseCore 0:
  9.6 58.7 all-gather.1

commit v2 on v1

--- a/solution.py
+++ b/solution.py
@@ -140,38 +140,44 @@
     )(me, jnp.asarray(order.reshape(-1), jnp.int32), *([attn_all] * n), *[x for x, _ in pieces], *wides, *old)
 
 
-def pair_sum_kernel(_, __, mine, other, out):
-    out[...] = (mine[...].astype(F32) + other[...].astype(F32)).astype(BF16)
-
-
-def pair_sum(me, which, mine, other, half):
+def pair_sum_kernel(_, __, *refs, n):
+    ins, outs = refs[: 2 * n], refs[2 * n :]
+    for s in range(n):
+        outs[s][...] = (ins[2 * s][...].astype(F32) + ins[2 * s + 1][...].astype(F32)).astype(BF16)
+
+
+def pair_sum(me, which, mine, other, half, tile=512):
     n, width = which.shape[1], mine.shape[1]
-    picked = pl.BlockSpec((half, width), lambda i, me, w: (w[me[0] * n + i], 0))
+    tile = fit(width, tile)
+    picked = [pl.BlockSpec((half, tile), lambda i, me, w, s=s: (w[me[0] * n + s], i)) for s in range(n) for _ in range(2)]
     return call(
-        pair_sum_kernel,
-        (n,),
-        [picked, picked],
-        pl.BlockSpec((half, width), lambda i, *_: (i, 0)),
-        jax.ShapeDtypeStruct((n * half, width), BF16),
+        functools.partial(pair_sum_kernel, n=n),
+        (width // tile,),
+        picked,
+        [pl.BlockSpec((half, tile), lambda i, *_: (0, i))] * n,
+        [jax.ShapeDtypeStruct((half, width), BF16)] * n,
         scalars=(me, which),
         bytes_accessed=6 * n * half * width,
-    )(me, jnp.asarray(which.reshape(-1), jnp.int32), mine, other)
+    )(me, jnp.asarray(which.reshape(-1), jnp.int32), *([mine, other] * n))
 
 
 def place_kernel(me, _, valid, __, *refs, spans, total_slots):
     out, i = refs[-1], pl.program_id(0)
     flag = valid[me[0] * total_slots + i]
     at = 0
-    for first, slots, n in spans:
-        mine = refs[at : at + n]
-        at += n
-
-        @pl.when((flag == 1) & (i >= first) & (i < first + slots))
-        def _():
-            total = mine[0][...].astype(F32)
-            for r in mine[1:]:
-                total = total + r[...].astype(F32)
-            out[...] = total.astype(BF16)
+    for counts, n_picked in spans:
+        picked = refs[at : at + n_picked]
+        at += n_picked
+        for slot, n_received in counts:
+            mine = [*picked, *refs[at : at + n_received]]
+            at += n_received
+
+            @pl.when((flag == 1) & (i == slot))
+            def _():
+                total = mine[0][...].astype(F32)
+                for r in mine[1:]:
+                    total = total + r[...].astype(F32)
+                out[...] = total.astype(BF16)
 
     if len(refs) > at + 1:
 
@@ -199,20 +205,23 @@
         slots = tables[0].shape[1]
         at = lambda i, f=first, s=slots: jnp.clip(i, f, f + s - 1)
         specs += [pl.BlockSpec((half, width), lambda i, me, w, v, p, at=at: (w[me[0] * n + at(i)], 0)) for _ in picked]
-        specs += [pl.BlockSpec((half, width), lambda i, me, w, v, p, at=at, f=first: (at(i) - f, 0)) for _ in received]
-        args += [*picked, *received]
-        spans.append((first, slots, len(picked) + len(received)))
+        args += picked
+        for r in received:
+            specs += [pl.BlockSpec((half, width), lambda i, *_: (0, 0)) for _ in r]
+            args += r
+        spans.append(([(first + s, len(r)) for s, r in enumerate(received)], len(picked)))
         first += slots
     spec = pl.BlockSpec((half, width), lambda i, me, w, v, p: (p[me[0] * n + i], 0))
     aliases = {}
+    kernel = functools.partial(place_kernel, spans=spans, total_slots=n)
     if out is not None:
-        specs.append(spec if (valid == 2).any() else pl.BlockSpec(memory_space=pl.ANY))
+        keep = (valid == 2).any()
+        specs.append(spec if keep else pl.BlockSpec(memory_space=pl.ANY))
         args.append(out)
         aliases = {4 + len(args) - 1: 0}
-    kernel = functools.partial(place_kernel, spans=spans, total_slots=n)
-    if out is not None and not (valid == 2).any():
-        inner = kernel
-        kernel = lambda *refs: inner(*refs[:-2], refs[-1])
+        if not keep:
+            inner = kernel
+            kernel = lambda *refs: inner(*refs[:-2], refs[-1])
     return call(
         kernel,
         (n,),
@@ -261,27 +270,32 @@
             where[d] = spots[:slots]
         return which, valid, where
 
-    def route(valid, shift):
+    def route(valid, shift, slot):
         to = [(r, (c + shift) % n_col) for r, c in devices]
-        return [(d, r * n_col + c) for d, (r, c) in enumerate(to) if valid[r * n_col + c].any()]
+        return [(d, r * n_col + c) for d, (r, c) in enumerate(to) if valid[r * n_col + c, slot]]
+
+    def send(arrays, valid, shift):
+        return [lax.ppermute(x, ("row", "col"), route(valid, shift, s)) for s, x in enumerate(arrays)]
 
     def shifted(table, shift):
         return np.stack([table[r * n_col + (c + shift) % n_col] for r, c in devices])
 
-    def reduce_in_pairs(steps, part):
+    def reduce_in_pairs(steps, part, late=False):
         tables = tables_of(steps)
-        (other,) = yield [lax.ppermute(part, "col", [(c, c ^ 1) for c in range(n_col)])]
-        received = []
-        for s in range(2, n_col, 2):
-            sent = pair_sum(me, shifted(tables[0], s), part, other, half)
-            received.append(lax.ppermute(sent, ("row", "col"), route(tables[1], s)))
+        other = lax.ppermute(part, "col", [(c, c ^ 1) for c in range(n_col)])
+        shifts = range(2, n_col, 2)
+        sums = [pair_sum(me, shifted(tables[0], s), part, other, half) for s in shifts]
+        other, sums = yield other, sums
+        received = [send(sums[i], tables[1], s) for i, s in enumerate(shifts)]
+        if late:
+            yield ()
         received = yield received
-        done.append((tables, [part, other], received))
+        done.append((tables, [part, other], [list(r) for r in zip(*received)]))
 
     def reduce_direct(step, parts):
         tables = tables_of([step])
-        received = yield [lax.ppermute(parts[s], ("row", "col"), route(tables[1], s)) for s in range(1, n_col)]
-        done.append((tables, [], [parts[0], *received]))
+        received = yield [send([parts[s]], tables[1], s)[0] for s in range(1, n_col)]
+        done.append((tables, [], [[parts[0], *received]]))
 
     def sorted_part(step):
         which = tables_of([step])[0]
@@ -298,11 +312,11 @@
     early = list(range(0, mid - 1))
     late = list(range(mid - 1, n_row))
     at_work = {
-        2: [("pairs", [0, 1])],
-        mid: [("pairs", list(range(2, mid)))],
-        mid + 1: [("first",)],
-        top - 1: [("pairs", list(range(mid, top - 1)))],
-        top: [("direct", top - 1)],
+        2: ["pairs", [0, 1]],
+        mid: ["first"],
+        mid + 1: ["pairs", list(range(2, mid))],
+        top - 1: ["pairs", list(range(mid, top - 1))],
+        top: ["pairs", [top - 1]],
     }
     done, moving = [], []
     grad_in = None
@@ -310,8 +324,7 @@
 
     def turn(on_link, work):
         nonlocal moving
-        flights = [f for _, f in moving]
-        on_link, work, flights = tie(on_link, work, flights)
+        on_link, work, flights = tie(on_link, work, [f for _, f in moving])
         moving = [[g, f] for (g, _), f in zip(moving, flights)]
         return on_link, work
 
@@ -325,33 +338,40 @@
                 pass
         moving = still
 
+    def begin(g):
+        moving.append([g, next(g)])
+
     for k in range(1, n_row):
         a, b = arrived[k - 1]
         nxt = (lax.ppermute(a, "row", right), lax.ppermute(b, "row", left))
-        jobs = at_work.get(k, [])
-        results = []
-        for job in jobs:
-            if job[0] == "pairs":
-                results.append([grad_in_part(pieces_of(job[1]), weight)])
-            elif job[0] == "direct":
-                results.append(sorted_part(job[1]))
-            else:
-                results.append([token_pass(me, order_of(early), attn_all, whole_pieces(early), (momentum,), out_dtype=BF16)])
-        arrived[k], results = turn(nxt, results)
+        job = at_work.get(k, ["none"])
+        work = ()
+        if job[0] == "pairs":
+            work = grad_in_part(pieces_of(job[1]), weight)
+        elif job[0] == "first":
+            work = token_pass(me, order_of(early), attn_all, whole_pieces(early), (momentum,), out_dtype=BF16)
+        if k == top:
+            grad_in = place(me, done, None, out_shape, half) if done else jnp.zeros(out_shape, BF16)
+            done.clear()
+            work = (work, grad_in)
+        arrived[k], work = turn(nxt, work)
+        if k == top:
+            work, grad_in = work
         advance()
-        for job, result in zip(jobs, results):
-            if job[0] == "first":
-                acc = result[0]
-                continue
-            g = reduce_in_pairs(job[1], result[0]) if job[0] == "pairs" else reduce_direct(job[1], result)
-            moving.append([g, next(g)])
+        if job[0] == "pairs":
+            begin(reduce_in_pairs(job[1], work, late=k == 2))
+        elif job[0] == "first":
+            acc = work
     parts = sorted_part(top)
-    if done:
-        grad_in = place(me, done, None, out_shape, half)
-        done.clear()
-    parts, acc = tie(parts, acc)
-    g = reduce_direct(top, parts)
-    moving.append([g, next(g)])
+    sums = [f for g, f in moving if len(f) == 2 and not isinstance(f, list)]
+    parts, acc, sums = tie(parts, acc, sums)
+    sums = iter(sums)
+    moving = [[g, next(sums) if len(f) == 2 and not isinstance(f, list) else f] for g, f in moving]
+    still = []
+    for g, f in moving:
+        still.append([g, g.send(f)] if not isinstance(f, list) else [g, f])
+    moving = still
+    begin(reduce_direct(top, parts))
     new_w, new_m = token_pass(me, order_of(late), attn_all, whole_pieces(late), (acc, weight))
     _, (new_w, new_m) = turn((), (new_w, new_m))
     while moving:

time: 308 us -> 281 us (0.912)
  waiting for transfers between devices: 98.7 us -> 63.5 us
  Pallas kernels: 147 us -> 153 us
    ppermute x14, waiting for transfers between devices: 84.3 us -> 60 us  [body(): nxt = (lax.ppermute(a, 'row', right), lax.ppermute(b, 'row', left))]
    pallas_call x2 -> x1, Pallas kernels: 22 us -> 11.1 us  [grad_in_part(): call(kernel, (feats // tile,), specs, outs, shapes, scalars=(me, take), *...]
    ppermute x12 -> x16, waiting for transfers between devices: 13.7 us -> 2.81 us  [the longest x4 2.78 us: reduce_in_pairs(): other = lax.ppermute(part, 'col', [(c, c ^ 1) for c in range(n_col)])]
    pallas_call x3 -> x4, Pallas kernels: 41.3 us -> 51.3 us  [grad_in_part(): call(kernel, (feats // tile,), specs, out, jax.ShapeDtypeStruct((rows, fe...]
    pallas_call x3 -> x4, Pallas kernels: 10.4 us -> 18.5 us  [pair_sum(): call(functools.partial(pair_sum_kernel, n=n), (width // tile,), picked, [...]
    ppermute x12 -> x16, starting transfers between devices: 29.5 us -> 28.3 us  [the longest x12 19.4 us: send(): lax.ppermute(x, ('row', 'col'), route(valid, shift, s))]
  transfers between devices with their start and end apart: 27 -> 31, of which waited for: 15 -> 13; matrix products, arithmetic and copies ran while one was open for 1% -> 1% of each run, Pallas kernels for 45% -> 52%
where the time goes in v2:
time: 281 us; the launch traced here: 276 us
  Pallas kernels  153 us (54%)
  waiting for transfers between devices  63.5 us (23%)
  starting transfers between devices  39.6 us (14%)
  between operations  14.4 us (5%)
  local copies, waits for them, and re-layouts  6.34 us (2%)
    pallas_call x2, Pallas kernels, token_pass(): call(functools.partial(pass_kernel, n=n, n_grads=n, last=last, n_old=len(...  60.3 us
    ppermute x14, waiting for transfers between devices, body(): nxt = (lax.ppermute(a, 'row', right), lax.ppermute(b, 'row', left))  60 us
    pallas_call x4, Pallas kernels, grad_in_part(): call(kernel, (feats // tile,), specs, out, jax.ShapeDtypeStruct((rows, fe...  51.3 us
    ppermute x12, starting transfers between devices, send(): lax.ppermute(x, ('row', 'col'), route(valid, shift, s))  19.4 us
    pallas_call x4, Pallas kernels, pair_sum(): call(functools.partial(pair_sum_kernel, n=n), (width // tile,), picked, [...  18.5 us
    pallas_call x2, Pallas kernels, place(): call(kernel, (n,), specs, spec, jax.ShapeDtypeStruct(shape, BF16), scalar...  11.4 us
    ppermute x14, starting transfers between devices, body(): nxt = (lax.ppermute(a, 'row', right), lax.ppermute(b, 'row', left))  11.3 us
    pallas_call x1, Pallas kernels, grad_in_part(): call(kernel, (feats // tile,), specs, outs, shapes, scalars=(me, take), *...  11.1 us
  transfers between devices with their start and end apart: 31, of which 13 were waited for; matrix products, arithmetic and copies ran while one was open for 1% of the time, Pallas kernels for 52%

profile of v2, /device:TPU:5, one launch (start us, length us, event | category | flops | bytes accessed | tf_op | source)
XLA Modules:
  0.0 276.4 jit_solution(7686459115135916993)
XLA Ops:
  7.9 1.8 fusion
  11.2 22.7 %collective-permute-done.1.refs_3_.refs_9_ = bf16[128,4096]{1,0:T(8,128)(2,1)} collective-permute-done((bf16[128,4096]{1,0:T(8,128)(2,1)S(1)}, bf16[128,4096]{1,0:T(8,128)(2,1)}, u32[]{:S(2)}, u32[]{:S(2)}) %collective-permute-start.1) | collective-permute-done | bytes 1048608 | tf_op jit(solution)/shard_map/ppermute | solution.py:346
  36.2 13.8 %shard_map.184.refs_0_.refs_2_.refs_4_ = bf16[512,2048]{1,0:T(8,128)(2,1)} custom-call(bf16[128,4096]{1,0:T(8,128)(2,1)} %copy-done.4, bf16[128,4096]{1,0:T(8,128)(2,1)} %copy-done.3, bf16[128,4096]{1,0:T(8,128)(2,1)} %collective-permute-done.refs_2_.refs_8_, bf16[128,4096]{1,0:T(8,128)(2,1)} %collective-permute-done.1.refs_3_.refs_9_, ...), custom_call_target="tpu_custom_call" | custom-call | flops 8589934592 | bytes 23068672 | tf_op jit(solution)/shard_map/pallas_call | solution.py:75
  50.0 7.9 %collective-permute-done.2.refs_10_.refs_0_ = bf16[128,4096]{1,0:T(8,128)(2,1)S(1)} collective-permute-done((bf16[128,4096]{1,0:T(8,128)(2,1)}, bf16[128,4096]{1,0:T(8,128)(2,1)S(1)}, u32[]{:S(2)}, u32[]{:S(2)}) %collective-permute-start.2) | collective-permute-done | bytes 1048608 | tf_op jit(solution)/shard_map/ppermute | solution.py:346
  58.8 2.7 collective-permute-start.6
  63.0 2.8 %collective-permute-done.6.refs_1_.refs_3_.refs_5_ = bf16[512,2048]{1,0:T(8,128)(2,1)S(1)} collective-permute-done((bf16[512,2048]{1,0:T(8,128)(2,1)}, bf16[512,2048]{1,0:T(8,128)(2,1)S(1)}, u32[]{:S(2)}, u32[]{:S(2)}) %collective-permute-start.6) | collective-permute-done | bytes 2097184 | tf_op jit(solution)/shard_map/ppermute | solution.py:285
  65.8 1.3 copy-done.1
  67.1 4.9 %shard_map.185 = (bf16[128,2048]{1,0:T(8,128)(2,1)}, bf16[128,2048]{1,0:T(8,128)(2,1)}, bf16[128,2048]{1,0:T(8,128)(2,1)}) custom-call(s32[1]{0:T(128)} %bitcast._.me.refs_0_, s32[96]{0:T(128)} %constant.37.clone.__, bf16[512,2048]{1,0:T(8,128)(2,1)} %shard_map.184.refs_0_.refs_2_.refs_4_, bf16[512,2048]{1,0:T(8,128)(2,1)} %copy-done.1, ...), custom_call_target="tpu_custom_call" | custom-call | bytes 4718592 | tf_op jit(solution)/shard_map/pallas_call | solution.py:153
  71.9 14.7 %collective-permute-done.4.refs_2_.refs_10_ = bf16[128,4096]{1,0:T(8,128)(2,1)S(1)} collective-permute-done((bf16[128,4096]{1,0:T(8,128)(2,1)}, bf16[128,4096]{1,0:T(8,128)(2,1)S(1)}, u32[]{:S(2)}, u32[]{:S(2)}) %collective-permute-start.4) | collective-permute-done | bytes 1048608 | tf_op jit(solution)/shard_map/ppermute | solution.py:346
  87.1 1.3 collective-permute-start.7
  88.6 22.9 %shard_map.186.refs_20_ = bf16[2048,4096]{1,0:T(8,128)(2,1)} custom-call(s32[1]{0:T(128)} %bitcast._.me.refs_0_, s32[192]{0:T(256)} %constant.38.clone.__, bf16[2048,2048]{1,0:T(8,128)(2,1)} %all-gather.2.cloned.1.call-done.refs_0_.refs_1_.refs_2_.refs_3_.refs_4_.refs_5_.refs_6_.refs_7_.refs_8_.refs_9_, ...), custom_call_target="tpu_custom_call" | custom-call | flops 12884901888 | bytes 67108864 | tf_op jit(solution)/shard_map/pallas_call | solution.py:129
  113.4 2.2 collective-permute-start.11
  116.9 13.8 %shard_map.187.refs_0_.refs_2_.refs_4_ = bf16[512,2048]{1,0:T(8,128)(2,1)} custom-call(bf16[128,4096]{1,0:T(8,128)(2,1)} %copy-done.9, bf16[128,4096]{1,0:T(8,128)(2,1)} %collective-permute-done.3.refs_11_.refs_1_, bf16[128,4096]{1,0:T(8,128)(2,1)} %copy-done.6, bf16[128,4096]{1,0:T(8,128)(2,1)} %collective-permute-done.5.refs_3_.refs_11_, ...), custom_call_target="tpu_custom_call" | custom-call | flops 8589934592 | bytes 23068672 | tf_op jit(solution)/shard_map/pallas_call | solution.py:75
  130.8 3.6 %collective-permute-done.9.refs_2_.refs_14_ = bf16[128,4096]{1,0:T(8,128)(2,1)} collective-permute-done((bf16[128,4096]{1,0:T(8,128)(2,1)S(1)}, bf16[128,4096]{1,0:T(8,128)(2,1)}, u32[]{:S(2)}, u32[]{:S(2)}) %collective-permute-start.9) | collective-permute-done | bytes 1048608 | tf_op jit(solution)/shard_map/ppermute | solution.py:346
  135.3 3.9 %collective-permute-start.16 = (bf16[512,2048]{1,0:T(8,128)(2,1)}, bf16[512,2048]{1,0:T(8,128)(2,1)}, u32[]{:S(2)}, u32[]{:S(2)}) collective-permute-start(bf16[512,2048]{1,0:T(8,128)(2,1)} %shard_map.187.refs_0_.refs_2_.refs_4_), channel_id=1, source_target_pairs={{0,1},{1,0},{2,3},{3,2},{4,5},{5,4},{6,7},{7,6},{8,9},{9,8},{10,11... | collective-permute-start | bytes 6291464 | tf_op jit(solution)/shard_map/ppermute | solution.py:285
  140.7 13.8 %shard_map.188.refs_0_.refs_2_.refs_4_.refs_8_ = bf16[512,2048]{1,0:T(8,128)(2,1)} custom-call(bf16[128,4096]{1,0:T(8,128)(2,1)} %copy-done.7, bf16[128,4096]{1,0:T(8,128)(2,1)} %copy-done.8, bf16[128,4096]{1,0:T(8,128)(2,1)} %collective-permute-done.9.refs_2_.refs_14_, bf16[128,4096]{1,0:T(8,128)(2,1)} %collective-permute-done.10.refs_3_.refs_15_, ...), custom_call_target="tpu_custom_call" | custom-call | flops 8589934592 | bytes 23068672 | tf_op jit(solution)/shard_map/pallas_call | solution.py:75
  154.5 4.5 %shard_map.189 = (bf16[128,2048]{1,0:T(8,128)(2,1)}, bf16[128,2048]{1,0:T(8,128)(2,1)}) custom-call(s32[1]{0:T(128)} %bitcast._.me.refs_0_, s32[64]{0:T(128)} %constant.39.clone.__, bf16[512,2048]{1,0:T(8,128)(2,1)} %shard_map.187.refs_0_.refs_2_.refs_4_, bf16[512,2048]{1,0:T(8,128)(2,1)} %collective-permute-done.16.refs_1_.refs_3_.refs_5_, ...), custom_call_target="tpu_custom_call" | custom-call | bytes 3145728 | tf_op jit(solution)/shard_map/pallas_call | solution.py:153
  159.0 5.2 %collective-permute-done.14.refs_0_.refs_16_ = bf16[128,4096]{1,0:T(8,128)(2,1)} collective-permute-done((bf16[128,4096]{1,0:T(8,128)(2,1)}, bf16[128,4096]{1,0:T(8,128)(2,1)}, u32[]{:S(2)}, u32[]{:S(2)}) %collective-permute-start.14) | collective-permute-done | bytes 1048608 | tf_op jit(solution)/shard_map/ppermute | solution.py:346
  165.8 2.4 collective-permute-start.17
  168.3 2.3 collective-permute-start.19
  170.6 1.5 collective-permute-start.20
  172.1 3.2 %shard_map.191.refs_20_ = bf16[512,2048]{1,0:T(8,128)(2,1)} custom-call(s32[1]{0:T(128)} %bitcast._.me.refs_0_, s32[96]{0:T(128)} %constant.41.clone._, s32[96]{0:T(128)} %constant.42.clone.valid, s32[96]{0:T(128)} %constant.43.clone.__, bf16[512,2048]{1,0:T(8,128)(2,1)} %shard_map.184.refs_0_.refs_2_.refs_4_, bf16[512,2048]{1,0:T(8,128)(2,1)} %copy-done.1, ...), custom_call_target="tpu_custom_call" | custom-call | bytes 6291456 | tf_op jit(solution)/shard_map/pallas_call | solution.py:225
  175.3 10.0 %shard_map.190.refs_0_.refs_13_ = bf16[256,2048]{1,0:T(8,128)(2,1)} custom-call(bf16[128,4096]{1,0:T(8,128)(2,1)} %collective-permute-done.14.refs_0_.refs_16_, bf16[128,4096]{1,0:T(8,128)(2,1)} %collective-permute-done.15.refs_1_.refs_17_, bf16[2048,4096]{1,0:T(8,128)(2,1)} %refs_21_.1), custom_call_target="tpu_custom_call" | custom-call | flops 4294967296 | bytes 19922944 | tf_op jit(solution)/shard_map/pallas_call | solution.py:75
  185.3 4.9 %shard_map.192 = (bf16[128,2048]{1,0:T(8,128)(2,1)}, bf16[128,2048]{1,0:T(8,128)(2,1)}, bf16[128,2048]{1,0:T(8,128)(2,1)}) custom-call(s32[1]{0:T(128)} %bitcast._.me.refs_0_, s32[96]{0:T(128)} %constant.40.clone.__, bf16[512,2048]{1,0:T(8,128)(2,1)} %shard_map.188.refs_0_.refs_2_.refs_4_.refs_8_, ...), custom_call_target="tpu_custom_call" | custom-call | bytes 4718592 | tf_op jit(solution)/shard_map/pallas_call | solution.py:153
  191.2 1.9 collective-permute-done.18.refs_1_.refs_19_
  198.1 11.1 %shard_map.193 = (bf16[128,2048]{1,0:T(8,128)(2,1)}, bf16[128,2048]{1,0:T(8,128)(2,1)}, bf16[128,2048]{1,0:T(8,128)(2,1)}, bf16[128,2048]{1,0:T(8,128)(2,1)}) custom-call(s32[1]{0:T(128)} %bitcast._.me.refs_0_, s32[128]{0:T(128)} %constant.45.clone.take, bf16[128,4096]{1,0:T(8,128)(2,1)} %collective-permute-done.17.refs_0_.refs_18_, ...), custom_call_target="tpu_custom_call" | custom-call | flops 4294967296 | bytes 19922944 | tf_op jit(solution)/shard_map/pallas_call | solution.py:80
  210.1 4.2 %shard_map.194 = bf16[128,2048]{1,0:T(8,128)(2,1)} custom-call(s32[1]{0:T(128)} %bitcast._.me.refs_0_, s32[32]{0:T(128)} %constant.44.clone.__, bf16[256,2048]{1,0:T(8,128)(2,1)} %shard_map.190.refs_0_.refs_13_, bf16[256,2048]{1,0:T(8,128)(2,1)} %copy-done.5), custom_call_target="tpu_custom_call" | custom-call | bytes 1572864 | tf_op jit(solution)/shard_map/pallas_call | solution.py:153
  214.3 4.9 %collective-permute-start.26 = (bf16[128,2048]{1,0:T(8,128)(2,1)}, bf16[128,2048]{1,0:T(8,128)(2,1)S(1)}, u32[]{:S(2)}, u32[]{:S(2)}) collective-permute-start(bf16[128,2048]{1,0:T(8,128)(2,1)} %shard_map.194), channel_id=1, source_target_pairs={{0,2},{3,1},{4,6},{7,5},{9,11},{10,8},{13,15},{14,12},{17,19},{18,... | collective-permute-start | bytes 1572872 | tf_op jit(solution)/shard_map/ppermute | solution.py:278
  219.2 1.3 collective-permute-start.27
  220.5 1.3 collective-permute-start.28
  222.6 37.4 %shard_map.195 = (bf16[2048,4096]{1,0:T(8,128)(2,1)}, bf16[2048,4096]{1,0:T(8,128)(2,1)}) custom-call(s32[1]{0:T(128)} %bitcast._.me.refs_0_, s32[320]{0:T(512)} %constant.46.clone.__, bf16[2048,2048]{1,0:T(8,128)(2,1)} %all-gather.2.cloned.1.call-done.refs_0_.refs_1_.refs_2_.refs_3_.refs_4_.refs_5_.refs_6_.refs_7_.refs_8_.refs_9_, ...), custom_call_target="tpu_custom_call" | custom-call | flops 21474836480 | bytes 67108864 | tf_op jit(solution)/shard_map/pallas_call | solution.py:129
  261.4 8.2 %shard_map.196 = bf16[512,2048]{1,0:T(8,128)(2,1)} custom-call(s32[1]{0:T(128)} %bitcast._.me.refs_0_, s32[224]{0:T(256)} %constant.47.clone.refs_1_, s32[224]{0:T(256)} %constant.48.clone.refs_2_, s32[224]{0:T(256)} %constant.49.clone.refs_3_, bf16[512,2048]{1,0:T(8,128)(2,1)} %shard_map.187.refs_0_.refs_2_.refs_4_, ...), custom_call_target="tpu_custom_call", output_to_operand_aliasing={{}: (20, {})} | custom-call | bytes 14680064 | tf_op jit(solution)/shard_map/pallas_call | solution.py:225
  (87 shorter events, 23.9 us)
Async XLA Ops:
  7.2 81.4 %all-gather.2.cloned.1.call-start = ((), (), s32[]{:S(2)}) async-start(), calls=%async_computation | async-start | bytes 10485760 | tf_op jit(solution)/shard_map/all_gather | solution.py:305
  9.7 24.2 %collective-permute-start.1 = (bf16[128,4096]{1,0:T(8,128)(2,1)S(1)}, bf16[128,4096]{1,0:T(8,128)(2,1)}, u32[]{:S(2)}, u32[]{:S(2)}) collective-permute-start(bf16[128,4096]{1,0:T(8,128)(2,1)S(1)} %get-tuple-element.135.refs_1_.refs_7_), channel_id=1, source_target_pairs={{8,0},{16,8},{24,16},{28,24},{20,28},{12,20},{4,12},{0,4},{9,1},{1... | collective-permute-start | bytes 3145736 | tf_op jit(solution)/shard_map/ppermute | solution.py:346
  10.9 23.8 %collective-permute-start = (bf16[128,4096]{1,0:T(8,128)(2,1)S(1)}, bf16[128,4096]{1,0:T(8,128)(2,1)}, u32[]{:S(2)}, u32[]{:S(2)}) collective-permute-start(bf16[128,4096]{1,0:T(8,128)(2,1)S(1)} %get-tuple-element.136.refs_0_.refs_6_), channel_id=1, source_target_pairs={{0,8},{8,16},{16,24},{24,28},{28,20},{20,12},{12,4},{4,0},{1,9},{9... | collective-permute-start | bytes 3145736 | tf_op jit(solution)/shard_map/ppermute | solution.py:346
  34.8 23.1 %collective-permute-start.2 = (bf16[128,4096]{1,0:T(8,128)(2,1)}, bf16[128,4096]{1,0:T(8,128)(2,1)S(1)}, u32[]{:S(2)}, u32[]{:S(2)}) collective-permute-start(bf16[128,4096]{1,0:T(8,128)(2,1)} %collective-permute-done.refs_2_.refs_8_), channel_id=1, source_target_pairs={{0,8},{8,16},{16,24},{24,28},{28,20},{20,12},{12,4},{4,0},{1,9},{9... | collective-permute-start | bytes 3145736 | tf_op jit(solution)/shard_map/ppermute | solution.py:346
  35.2 23.7 %collective-permute-start.3 = (bf16[128,4096]{1,0:T(8,128)(2,1)}, bf16[128,4096]{1,0:T(8,128)(2,1)}, u32[]{:S(2)}, u32[]{:S(2)}) collective-permute-start(bf16[128,4096]{1,0:T(8,128)(2,1)} %collective-permute-done.1.refs_3_.refs_9_), channel_id=1, source_target_pairs={{8,0},{16,8},{24,16},{28,24},{20,28},{12,20},{4,12},{0,4},{9,1},{1... | collective-permute-start | bytes 3145736 | tf_op jit(solution)/shard_map/ppermute | solution.py:346
  58.8 6.9 %collective-permute-start.6 = (bf16[512,2048]{1,0:T(8,128)(2,1)}, bf16[512,2048]{1,0:T(8,128)(2,1)S(1)}, u32[]{:S(2)}, u32[]{:S(2)}) collective-permute-start(bf16[512,2048]{1,0:T(8,128)(2,1)} %shard_map.184.refs_0_.refs_2_.refs_4_), channel_id=1, source_target_pairs={{0,1},{1,0},{2,3},{3,2},{4,5},{5,4},{6,7},{7,6},{8,9},{9,8},{10,11... | collective-permute-start | bytes 6291464 | tf_op jit(solution)/shard_map/ppermute | solution.py:285
  61.5 25.1 %collective-permute-start.4 = (bf16[128,4096]{1,0:T(8,128)(2,1)}, bf16[128,4096]{1,0:T(8,128)(2,1)S(1)}, u32[]{:S(2)}, u32[]{:S(2)}) collective-permute-start(bf16[128,4096]{1,0:T(8,128)(2,1)} %copy-done.9), channel_id=1, source_target_pairs={{0,8},{8,16},{16,24},{24,28},{28,20},{20,12},{12,4},{4,0},{1,9},{9... | collective-permute-start | bytes 3145736 | tf_op jit(solution)/shard_map/ppermute | solution.py:346
  62.3 24.8 %collective-permute-start.5 = (bf16[128,4096]{1,0:T(8,128)(2,1)}, bf16[128,4096]{1,0:T(8,128)(2,1)}, u32[]{:S(2)}, u32[]{:S(2)}) collective-permute-start(bf16[128,4096]{1,0:T(8,128)(2,1)} %collective-permute-done.3.refs_11_.refs_1_), channel_id=1, source_target_pairs={{8,0},{16,8},{24,16},{28,24},{20,28},{12,20},{4,12},{0,4},{9,1},{1... | collective-permute-start | bytes 3145736 | tf_op jit(solution)/shard_map/ppermute | solution.py:346
  87.1 24.4 %collective-permute-start.7 = (bf16[128,4096]{1,0:T(8,128)(2,1)S(1)}, bf16[128,4096]{1,0:T(8,128)(2,1)S(1)}, u32[]{:S(2)}, u32[]{:S(2)}) collective-permute-start(bf16[128,4096]{1,0:T(8,128)(2,1)S(1)} %collective-permute-done.4.refs_2_.refs_10_), channel_id=1, source_target_pairs={{0,8},{8,16},{16,24},{24,28},{28,20},{20,12},{12,4},{4,0},{1,9},{9... | collective-permute-start | bytes 3145736 | tf_op jit(solution)/shard_map/ppermute | solution.py:346
  88.4 23.5 %collective-permute-start.8 = (bf16[128,4096]{1,0:T(8,128)(2,1)}, bf16[128,4096]{1,0:T(8,128)(2,1)S(1)}, u32[]{:S(2)}, u32[]{:S(2)}) collective-permute-start(bf16[128,4096]{1,0:T(8,128)(2,1)} %collective-permute-done.5.refs_3_.refs_11_), channel_id=1, source_target_pairs={{8,0},{16,8},{24,16},{28,24},{20,28},{12,20},{4,12},{0,4},{9,1},{1... | collective-permute-start | bytes 3145736 | tf_op jit(solution)/shard_map/ppermute | solution.py:346
  111.9 22.5 %collective-permute-start.9 = (bf16[128,4096]{1,0:T(8,128)(2,1)S(1)}, bf16[128,4096]{1,0:T(8,128)(2,1)}, u32[]{:S(2)}, u32[]{:S(2)}) collective-permute-start(bf16[128,4096]{1,0:T(8,128)(2,1)S(1)} %collective-permute-done.7.refs_0_.refs_12_), channel_id=1, source_target_pairs={{0,8},{8,16},{16,24},{24,28},{28,20},{20,12},{12,4},{4,0},{1,9},{9... | collective-permute-start | bytes 3145736 | tf_op jit(solution)/shard_map/ppermute | solution.py:346
  113.1 22.2 %collective-permute-start.10 = (bf16[128,4096]{1,0:T(8,128)(2,1)S(1)}, bf16[128,4096]{1,0:T(8,128)(2,1)}, u32[]{:S(2)}, u32[]{:S(2)}) collective-permute-start(bf16[128,4096]{1,0:T(8,128)(2,1)S(1)} %collective-permute-done.8.refs_1_.refs_13_), channel_id=1, source_target_pairs={{8,0},{16,8},{24,16},{28,24},{20,28},{12,20},{4,12},{0,4},{9,1},{1... | collective-permute-start | bytes 3145736 | tf_op jit(solution)/shard_map/ppermute | solution.py:346
  113.4 17.4 %collective-permute-start.11 = (bf16[128,2048]{1,0:T(8,128)(2,1)}, bf16[128,2048]{1,0:T(8,128)(2,1)S(1)}, u32[]{:S(2)}, u32[]{:S(2)}) collective-permute-start(bf16[128,2048]{1,0:T(8,128)(2,1)} %get-tuple-element.81), channel_id=1, source_target_pairs={{2,0},{3,1},{6,4},{7,5},{8,10},{10,8},{11,9},{12,14},{14,12},{15,1... | collective-permute-start | bytes 1572872 | tf_op jit(solution)/shard_map/ppermute | solution.py:278
  115.5 15.2 %collective-permute-start.12 = (bf16[128,2048]{1,0:T(8,128)(2,1)}, bf16[128,2048]{1,0:T(8,128)(2,1)S(1)}, u32[]{:S(2)}, u32[]{:S(2)}) collective-permute-start(bf16[128,2048]{1,0:T(8,128)(2,1)} %get-tuple-element.82), channel_id=1, source_target_pairs={{2,0},{6,4},{11,9},{15,13},{16,18},{20,22},{25,27},{29,31}} | collective-permute-start | bytes 1572872 | tf_op jit(solution)/shard_map/ppermute | solution.py:278
  116.2 14.5 %collective-permute-start.13 = (bf16[128,2048]{1,0:T(8,128)(2,1)}, bf16[128,2048]{1,0:T(8,128)(2,1)S(1)}, u32[]{:S(2)}, u32[]{:S(2)}) collective-permute-start(bf16[128,2048]{1,0:T(8,128)(2,1)} %get-tuple-element.83), channel_id=1, source_target_pairs={{2,0},{6,4},{25,27},{29,31}} | collective-permute-start | bytes 1572872 | tf_op jit(solution)/shard_map/ppermute | solution.py:278
  135.3 19.2 %collective-permute-start.16 = (bf16[512,2048]{1,0:T(8,128)(2,1)}, bf16[512,2048]{1,0:T(8,128)(2,1)}, u32[]{:S(2)}, u32[]{:S(2)}) collective-permute-start(bf16[512,2048]{1,0:T(8,128)(2,1)} %shard_map.187.refs_0_.refs_2_.refs_4_), channel_id=1, source_target_pairs={{0,1},{1,0},{2,3},{3,2},{4,5},{5,4},{6,7},{7,6},{8,9},{9,8},{10,11... | collective-permute-start | bytes 6291464 | tf_op jit(solution)/shard_map/ppermute | solution.py:285
  139.3 25.0 %collective-permute-start.14 = (bf16[128,4096]{1,0:T(8,128)(2,1)}, bf16[128,4096]{1,0:T(8,128)(2,1)}, u32[]{:S(2)}, u32[]{:S(2)}) collective-permute-start(bf16[128,4096]{1,0:T(8,128)(2,1)} %collective-permute-done.9.refs_2_.refs_14_), channel_id=1, source_target_pairs={{0,8},{8,16},{16,24},{24,28},{28,20},{20,12},{12,4},{4,0},{1,9},{9... | collective-permute-start | bytes 3145736 | tf_op jit(solution)/shard_map/ppermute | solution.py:346
  140.0 24.8 %collective-permute-start.15 = (bf16[128,4096]{1,0:T(8,128)(2,1)}, bf16[128,4096]{1,0:T(8,128)(2,1)}, u32[]{:S(2)}, u32[]{:S(2)}) collective-permute-start(bf16[128,4096]{1,0:T(8,128)(2,1)} %collective-permute-done.10.refs_3_.refs_15_), channel_id=1, source_target_pairs={{8,0},{16,8},{24,16},{28,24},{20,28},{12,20},{4,12},{0,4},{9,1},{1... | collective-permute-start | bytes 3145736 | tf_op jit(solution)/shard_map/ppermute | solution.py:346
  164.7 20.5 %collective-permute-start.21 = (bf16[512,2048]{1,0:T(8,128)(2,1)S(1)}, bf16[512,2048]{1,0:T(8,128)(2,1)}, u32[]{:S(2)}, u32[]{:S(2)}) collective-permute-start(bf16[512,2048]{1,0:T(8,128)(2,1)S(1)} %copy-done), channel_id=1, source_target_pairs={{0,1},{1,0},{2,3},{3,2},{4,5},{5,4},{6,7},{7,6},{8,9},{9,8},{10,11... | collective-permute-start | bytes 6291464 | tf_op jit(solution)/shard_map/ppermute | solution.py:285
  165.8 25.3 %collective-permute-start.17 = (bf16[128,4096]{1,0:T(8,128)(2,1)}, bf16[128,4096]{1,0:T(8,128)(2,1)}, u32[]{:S(2)}, u32[]{:S(2)}) collective-permute-start(bf16[128,4096]{1,0:T(8,128)(2,1)} %collective-permute-done.14.refs_0_.refs_16_), channel_id=1, source_target_pairs={{0,8},{8,16},{16,24},{24,28},{28,20},{20,12},{12,4},{4,0},{1,9},{9... | collective-permute-start | bytes 3145736 | tf_op jit(solution)/shard_map/ppermute | solution.py:346
  168.3 24.8 %collective-permute-start.18 = (bf16[128,4096]{1,0:T(8,128)(2,1)}, bf16[128,4096]{1,0:T(8,128)(2,1)}, u32[]{:S(2)}, u32[]{:S(2)}) collective-permute-start(bf16[128,4096]{1,0:T(8,128)(2,1)} %collective-permute-done.15.refs_1_.refs_17_), channel_id=1, source_target_pairs={{8,0},{16,8},{24,16},{28,24},{20,28},{12,20},{4,12},{0,4},{9,1},{1... | collective-permute-start | bytes 3145736 | tf_op jit(solution)/shard_map/ppermute | solution.py:346
  168.3 21.9 %collective-permute-start.19 = (bf16[128,2048]{1,0:T(8,128)(2,1)}, bf16[128,2048]{1,0:T(8,128)(2,1)S(1)}, u32[]{:S(2)}, u32[]{:S(2)}) collective-permute-start(bf16[128,2048]{1,0:T(8,128)(2,1)} %get-tuple-element.96), channel_id=1, source_target_pairs={{0,2},{1,3},{3,1},{4,6},{5,7},{7,5},{9,11},{10,8},{11,9},{13,15},{... | collective-permute-start | bytes 1572872 | tf_op jit(solution)/shard_map/ppermute | solution.py:278
  170.6 19.6 %collective-permute-start.20 = (bf16[128,2048]{1,0:T(8,128)(2,1)}, bf16[128,2048]{1,0:T(8,128)(2,1)}, u32[]{:S(2)}, u32[]{:S(2)}) collective-permute-start(bf16[128,2048]{1,0:T(8,128)(2,1)} %get-tuple-element.97), channel_id=1, source_target_pairs={{0,2},{4,6},{9,11},{13,15},{18,16},{22,20},{27,25},{31,29}} | collective-permute-start | bytes 1572872 | tf_op jit(solution)/shard_map/ppermute | solution.py:278
  193.1 16.0 %collective-permute-start.22 = (bf16[256,2048]{1,0:T(8,128)(2,1)S(1)}, bf16[256,2048]{1,0:T(8,128)(2,1)S(1)}, u32[]{:S(2)}, u32[]{:S(2)}) collective-permute-start(bf16[256,2048]{1,0:T(8,128)(2,1)S(1)} %copy-done.2), channel_id=1, source_target_pairs={{0,1},{1,0},{2,3},{3,2},{4,5},{5,4},{6,7},{7,6},{8,9},{9,8},{10,11... | collective-permute-start | bytes 3145736 | tf_op jit(solution)/shard_map/ppermute | solution.py:285
  194.2 26.3 %collective-permute-start.23 = (bf16[128,2048]{1,0:T(8,128)(2,1)}, bf16[128,2048]{1,0:T(8,128)(2,1)S(1)}, u32[]{:S(2)}, u32[]{:S(2)}) collective-permute-start(bf16[128,2048]{1,0:T(8,128)(2,1)} %get-tuple-element.116), channel_id=1, source_target_pairs={{0,2},{1,3},{4,6},{5,7},{8,10},{9,11},{11,9},{12,14},{13,15},{15,1... | collective-permute-start | bytes 1572872 | tf_op jit(solution)/shard_map/ppermute | solution.py:278
  195.5 26.4 %collective-permute-start.24 = (bf16[128,2048]{1,0:T(8,128)(2,1)}, bf16[128,2048]{1,0:T(8,128)(2,1)S(1)}, u32[]{:S(2)}, u32[]{:S(2)}) collective-permute-start(bf16[128,2048]{1,0:T(8,128)(2,1)} %get-tuple-element.117), channel_id=1, source_target_pairs={{1,3},{5,7},{8,10},{12,14},{19,17},{23,21},{26,24},{30,28}} | collective-permute-start | bytes 1572872 | tf_op jit(solution)/shard_map/ppermute | solution.py:278
  196.8 63.3 %collective-permute-start.25 = (bf16[128,2048]{1,0:T(8,128)(2,1)}, bf16[128,2048]{1,0:T(8,128)(2,1)}, u32[]{:S(2)}, u32[]{:S(2)}) collective-permute-start(bf16[128,2048]{1,0:T(8,128)(2,1)} %get-tuple-element.118), channel_id=1, source_target_pairs={{1,3},{5,7},{26,24},{30,28}} | collective-permute-start | bytes 1572872 | tf_op jit(solution)/shard_map/ppermute | solution.py:278
  214.3 45.8 %collective-permute-start.26 = (bf16[128,2048]{1,0:T(8,128)(2,1)}, bf16[128,2048]{1,0:T(8,128)(2,1)S(1)}, u32[]{:S(2)}, u32[]{:S(2)}) collective-permute-start(bf16[128,2048]{1,0:T(8,128)(2,1)} %shard_map.194), channel_id=1, source_target_pairs={{0,2},{3,1},{4,6},{7,5},{9,11},{10,8},{13,15},{14,12},{17,19},{18,... | collective-permute-start | bytes 1572872 | tf_op jit(solution)/shard_map/ppermute | solution.py:278
  219.2 40.9 %collective-permute-start.27 = (bf16[128,2048]{1,0:T(8,128)(2,1)}, bf16[128,2048]{1,0:T(8,128)(2,1)S(1)}, u32[]{:S(2)}, u32[]{:S(2)}) collective-permute-start(bf16[128,2048]{1,0:T(8,128)(2,1)} %get-tuple-element.120), channel_id=1, source_target_pairs={{0,1},{3,0},{4,5},{7,4},{9,10},{11,8},{13,14},{15,12},{16,17},{18,... | collective-permute-start | bytes 1572872 | tf_op jit(solution)/shard_map/ppermute | solution.py:278
  220.5 39.5 %copy-start.11 = (bf16[128,2048]{1,0:T(8,128)(2,1)}, bf16[128,2048]{1,0:T(8,128)(2,1)S(1)}, u32[]{:S(2)}) copy-start(bf16[128,2048]{1,0:T(8,128)(2,1)S(1)} %collective-permute-done.23.refs_10_) | copy-start | bytes 1572868
  220.5 39.6 %collective-permute-start.28 = (bf16[128,2048]{1,0:T(8,128)(2,1)}, bf16[128,2048]{1,0:T(8,128)(2,1)S(1)}, u32[]{:S(2)}, u32[]{:S(2)}) collective-permute-start(bf16[128,2048]{1,0:T(8,128)(2,1)} %get-tuple-element.121), channel_id=1, source_target_pairs={{2,0},{3,1},{6,4},{7,5},{8,10},{10,8},{12,14},{14,12},{17,19},{19,... | collective-permute-start | bytes 1572872 | tf_op jit(solution)/shard_map/ppermute | solution.py:278
  221.9 38.2 %collective-permute-start.29 = (bf16[128,2048]{1,0:T(8,128)(2,1)S(1)}, bf16[128,2048]{1,0:T(8,128)(2,1)S(1)}, u32[]{:S(2)}, u32[]{:S(2)}) collective-permute-start(bf16[128,2048]{1,0:T(8,128)(2,1)S(1)} %copy-done.20), channel_id=1, source_target_pairs={{1,0},{2,1},{5,4},{6,5},{9,8},{11,10},{13,12},{15,14},{16,19},{18,... | collective-permute-start | bytes 1572872 | tf_op jit(solution)/shard_map/ppermute | solution.py:278
  (20 other events, 267.7 us)
Sparse Core Ops, SparseCore 0:
  9.6 58.7 all-gather.1

commit v3 on v2

--- a/solution.py
+++ b/solution.py
@@ -13,6 +13,7 @@
 NT = (((1,), (1,)), ((), ()))
 TN = (((0,), (0,)), ((), ()))
 VMEM_BYTES = 60 << 20
+GRAD_IN_VMEM, SUM_VMEM = 50 << 20, 24 << 20
 
 
 def snake(n):
@@ -29,7 +30,7 @@
     return want
 
 
-def call(kernel, grid, in_specs, out_specs, out_shape, scalars=(), scratch=(), aliases=None, flops=0, bytes_accessed=0):
+def call(kernel, grid, in_specs, out_specs, out_shape, scalars=(), scratch=(), aliases=None, flops=0, bytes_accessed=0, vmem=VMEM_BYTES):
     return pl.pallas_call(
         kernel,
         grid_spec=pltpu.PrefetchScalarGridSpec(
@@ -37,7 +38,7 @@
         ),
         out_shape=out_shape,
         input_output_aliases=aliases or {},
-        compiler_params=pltpu.CompilerParams(vmem_limit_bytes=VMEM_BYTES),
+        compiler_params=pltpu.CompilerParams(vmem_limit_bytes=vmem),
         cost_estimate=pl.CostEstimate(flops=flops, bytes_accessed=bytes_accessed, transcendentals=0),
     )
 
@@ -68,7 +69,7 @@
     flat = [x for p in pieces for x in p]
     specs = [pl.BlockSpec(x.shape, lambda i, *_: (0, 0)) for x in flat]
     specs.append(pl.BlockSpec((tile, cols), lambda i, *_: (i, 0)))
-    cost = dict(flops=2 * rows * feats * cols, bytes_accessed=2 * (rows * cols + feats * cols + rows * feats))
+    cost = dict(vmem=GRAD_IN_VMEM, flops=2 * rows * feats * cols, bytes_accessed=2 * (rows * cols + feats * cols + rows * feats))
     if take is None:
         kernel = functools.partial(grad_in_kernel, n=len(flat), parts=parts)
         out = pl.BlockSpec((rows, tile), lambda i: (0, i))
@@ -157,6 +158,7 @@
         [pl.BlockSpec((half, tile), lambda i, *_: (0, i))] * n,
         [jax.ShapeDtypeStruct((half, width), BF16)] * n,
         scalars=(me, which),
+        vmem=SUM_VMEM,
         bytes_accessed=6 * n * half * width,
     )(me, jnp.asarray(which.reshape(-1), jnp.int32), *([mine, other] * n))
 
@@ -198,7 +200,8 @@
             continue
         for s in range(n):
             before = real[real <= s]
-            where[d, s] = where[d, before[-1] if len(before) else real[0]]
+            near = before[-1] if len(before) else real[0]
+            where[d, s] = where[d, near]
     width = shape[1]
     specs, args, spans, first = [], [], [], 0
     for tables, picked, received in groups:
@@ -253,8 +256,14 @@
             arrives[r, k, 0] = 2 * ring[(pos[r] - k) % n_row]
             arrives[r, k, 1] = 2 * ring[(pos[r] + k) % n_row] + 1
 
+    held = np.zeros((n_row * n_col, 2 * n_row), np.int32)
+    for d, (r, c) in enumerate(devices):
+        near = [(c + s) % n_col for s in range(0, n_col, 2)]
+        for at, owner in enumerate(near + [o ^ 1 for o in near]):
+            held[d, owner * 2 * per_owner : (owner + 1) * 2 * per_owner] = np.arange(2 * per_owner) + at * 2 * per_owner
+
     def order_of(steps):
-        return np.stack([arrives[r, np.array(steps)].reshape(-1) for r, _ in devices])
+        return np.stack([held[d, arrives[r, np.array(steps)].reshape(-1)] for d, (r, _) in enumerate(devices)])
 
     def tables_of(steps):
         halves = arrives[:, np.array(steps), :].reshape(n_row, -1)
@@ -274,20 +283,26 @@
         to = [(r, (c + shift) % n_col) for r, c in devices]
         return [(d, r * n_col + c) for d, (r, c) in enumerate(to) if valid[r * n_col + c, slot]]
 
+    cores = [(c, c ^ 1) for c in range(n_col)]
+
     def send(arrays, valid, shift):
         return [lax.ppermute(x, ("row", "col"), route(valid, shift, s)) for s, x in enumerate(arrays)]
 
     def shifted(table, shift):
         return np.stack([table[r * n_col + (c + shift) % n_col] for r, c in devices])
 
-    def reduce_in_pairs(steps, part, late=False):
+    def reduce_in_pairs(steps, part, wait=0, hold=0, late=0):
         tables = tables_of(steps)
-        other = lax.ppermute(part, "col", [(c, c ^ 1) for c in range(n_col)])
+        for _ in range(wait):
+            yield ()
+        other = lax.ppermute(part, "col", cores)
         shifts = range(2, n_col, 2)
         sums = [pair_sum(me, shifted(tables[0], s), part, other, half) for s in shifts]
         other, sums = yield other, sums
+        for _ in range(hold):
+            yield ()
         received = [send(sums[i], tables[1], s) for i, s in enumerate(shifts)]
-        if late:
+        for _ in range(late):
             yield ()
         received = yield received
         done.append((tables, [part, other], [list(r) for r in zip(*received)]))
@@ -302,7 +317,6 @@
         take = np.concatenate([shifted(which, s) for s in range(n_col)], axis=1)
         return grad_in_part(pieces_of([step]), weight, take, me)
 
-    attn_all = lax.all_gather(attn, "col", axis=0, tiled=True)
     arrived = {0: (grad_out[:half], grad_out[half:])}
     pieces_of = lambda steps: [(x,) for k in steps for x in arrived[k]]
     whole_pieces = lambda steps: [(x, 0) for k in steps for x in arrived[k]]
@@ -312,15 +326,15 @@
     early = list(range(0, mid - 1))
     late = list(range(mid - 1, n_row))
     at_work = {
-        2: ["pairs", [0, 1]],
-        mid: ["first"],
-        mid + 1: ["pairs", list(range(2, mid))],
-        top - 1: ["pairs", list(range(mid, top - 1))],
-        top: ["pairs", [top - 1]],
+        1: ([0], 0, 0, 0),
+        2: ([1], 2, 0, 0),
+        mid - 1: (list(range(2, mid - 1)), 1, 0, 0),
+        mid + 1: ([mid - 1, mid], 0, 0, 0),
+        top - 1: (list(range(mid + 1, top - 1)), 0, 0, 0),
+        top: ([top - 1], 0, 0, 0),
     }
     done, moving = [], []
-    grad_in = None
-    acc = None
+    acc = grad_in = None
 
     def turn(on_link, work):
         nonlocal moving
@@ -344,23 +358,35 @@
     for k in range(1, n_row):
         a, b = arrived[k - 1]
         nxt = (lax.ppermute(a, "row", right), lax.ppermute(b, "row", left))
-        job = at_work.get(k, ["none"])
         work = ()
-        if job[0] == "pairs":
-            work = grad_in_part(pieces_of(job[1]), weight)
-        elif job[0] == "first":
+        if k in at_work:
+            work = grad_in_part(pieces_of(at_work[k][0]), weight)
+        elif k == mid:
             work = token_pass(me, order_of(early), attn_all, whole_pieces(early), (momentum,), out_dtype=BF16)
-        if k == top:
-            grad_in = place(me, done, None, out_shape, half) if done else jnp.zeros(out_shape, BF16)
+        extra = ()
+        if k == 1:
+            far = [lax.ppermute(attn, "col", [(c, (c - s) % n_col) for c in range(n_col)]) for s in range(2, n_col, 2)]
+            extra = lax.ppermute(attn, "col", cores)
+        elif k == 2:
+            extra = far
+        elif k == 3:
+            extra = jnp.concatenate([attn, *far, beside, *[lax.ppermute(x, "col", cores) for x in far]])
+        elif k == top and done:
+            extra = place(me, done, None, out_shape, half)
             done.clear()
-            work = (work, grad_in)
-        arrived[k], work = turn(nxt, work)
-        if k == top:
-            work, grad_in = work
+        arrived[k], (work, extra) = turn(nxt, (work, extra))
+        if k == 1:
+            beside = extra
+        elif k == 2:
+            far = extra
+        elif k == 3:
+            attn_all = extra
+        elif k == top and not isinstance(extra, tuple):
+            grad_in = extra
         advance()
-        if job[0] == "pairs":
-            begin(reduce_in_pairs(job[1], work, late=k == 2))
-        elif job[0] == "first":
+        if k in at_work:
+            begin(reduce_in_pairs(at_work[k][0], work, *at_work[k][1:]))
+        elif k == mid:
             acc = work
     parts = sorted_part(top)
     sums = [f for g, f in moving if len(f) == 2 and not isinstance(f, list)]

time: 281 us -> 264 us (0.940)
  between operations: 14.4 us -> 1.28 us
  waiting for transfers between devices: 63.5 us -> 56.7 us
  other arithmetic: 0 us -> 6.13 us
  starting transfers between devices: 39.6 us -> 42.7 us
    ppermute x14, waiting for transfers between devices: 60 us -> 35.8 us  [body(): nxt = (lax.ppermute(a, 'row', right), lax.ppermute(b, 'row', left))]
    ppermute x12, waiting for transfers between devices: 0.03 us -> 12.3 us  [send(): lax.ppermute(x, ('row', 'col'), route(valid, shift, s))]
    pallas_call x4 -> x6, Pallas kernels: 18.5 us -> 9.68 us  [pair_sum(): call(functools.partial(pair_sum_kernel, n=n), (width // tile,), picked, [...]
    pallas_call x4 -> x6, Pallas kernels: 51.3 us -> 59.1 us  [grad_in_part(): call(kernel, (feats // tile,), specs, out, jax.ShapeDtypeStruct((rows, fe...]
    concatenate x0 -> x1, other arithmetic: none -> 6.13 us  [body(): jnp.concatenate([attn, *far, beside, *[lax.ppermute(x, 'col', cores) for...]
    ppermute x4 -> x9, waiting for transfers between devices: 2.78 us -> 8.68 us  [the longest x1 8.66 us: body(): lax.ppermute(attn, 'col', [(c, (c - s) % n_col) for c in range(n_col)])]
    ppermute x4 -> x9, starting transfers between devices: 8.83 us -> 8.66 us  [the longest x6 6.76 us: reduce_in_pairs(): other = lax.ppermute(part, 'col', cores)]
  transfers between devices with their start and end apart: 31 -> 35, of which waited for: 13 -> 13; matrix products, arithmetic and copies ran while one was open for 1% -> 3% of each run, Pallas kernels for 52% -> 55%
where the time goes in v3:
time: 264 us; the launch traced here: 262 us
  Pallas kernels  151 us (57%)
  waiting for transfers between devices  56.7 us (21%)
  starting transfers between devices  42.7 us (16%)
  other arithmetic  6.13 us (2%)
  local copies, waits for them, and re-layouts  3.89 us (1%)
    pallas_call x2, Pallas kernels, token_pass(): call(functools.partial(pass_kernel, n=n, n_grads=n, last=last, n_old=len(...  60.4 us
    pallas_call x6, Pallas kernels, grad_in_part(): call(kernel, (feats // tile,), specs, out, jax.ShapeDtypeStruct((rows, fe...  59.1 us
    ppermute x14, waiting for transfers between devices, body(): nxt = (lax.ppermute(a, 'row', right), lax.ppermute(b, 'row', left))  35.8 us
    ppermute x12, starting transfers between devices, send(): lax.ppermute(x, ('row', 'col'), route(valid, shift, s))  21.7 us
    ppermute x14, starting transfers between devices, body(): nxt = (lax.ppermute(a, 'row', right), lax.ppermute(b, 'row', left))  12.3 us
    ppermute x12, waiting for transfers between devices, send(): lax.ppermute(x, ('row', 'col'), route(valid, shift, s))  12.3 us
    pallas_call x2, Pallas kernels, place(): call(kernel, (n,), specs, spec, jax.ShapeDtypeStruct(shape, BF16), scalar...  11.8 us
    pallas_call x1, Pallas kernels, grad_in_part(): call(kernel, (feats // tile,), specs, outs, shapes, scalars=(me, take), *...  10.4 us
  transfers between devices with their start and end apart: 35, of which 13 were waited for; matrix products, arithmetic and copies ran while one was open for 3% of the time, Pallas kernels for 55%

profile of v3, /device:TPU:5, one launch (start us, length us, event | category | flops | bytes accessed | tf_op | source)
XLA Modules:
  0.0 262.0 jit_solution(2839575805858040607)
XLA Ops:
  1.4 1.7 fusion
  4.8 8.5 %shard_map.202.refs_0_.refs_2_ = bf16[256,2048]{1,0:T(8,128)(2,1)S(1)} custom-call(bf16[128,4096]{1,0:T(8,128)(2,1)S(1)} %get-tuple-element.144.refs_0_.refs_6_, bf16[128,4096]{1,0:T(8,128)(2,1)S(1)} %get-tuple-element.143.refs_1_.refs_7_, bf16[2048,4096]{1,0:T(8,128)(2,1)} %refs_21_.1), custom_call_target="tpu_custom_call" | custom-call | flops 4294967296 | bytes 19922944 | tf_op jit(solution)/shard_map/pallas_call | solution.py:76
  13.3 14.8 %collective-permute-done.1.refs_1_.refs_9_ = bf16[128,4096]{1,0:T(8,128)(2,1)} collective-permute-done((bf16[128,4096]{1,0:T(8,128)(2,1)S(1)}, bf16[128,4096]{1,0:T(8,128)(2,1)}, u32[]{:S(2)}, u32[]{:S(2)}) %collective-permute-start.1) | collective-permute-done | bytes 1048608 | tf_op jit(solution)/shard_map/ppermute | solution.py:360
  31.5 10.0 %shard_map.203.refs_0_.refs_4_ = bf16[256,2048]{1,0:T(8,128)(2,1)} custom-call(bf16[128,4096]{1,0:T(8,128)(2,1)} %collective-permute-done.refs_0_.refs_8_, bf16[128,4096]{1,0:T(8,128)(2,1)} %collective-permute-done.1.refs_1_.refs_9_, bf16[2048,4096]{1,0:T(8,128)(2,1)} %refs_21_.1), custom_call_target="tpu_custom_call" | custom-call | flops 4294967296 | bytes 19922944 | tf_op jit(solution)/shard_map/pallas_call | solution.py:76
  42.9 8.7 %collective-permute-done.5 = bf16[512,2048]{1,0:T(8,128)(2,1)} collective-permute-done((bf16[512,2048]{1,0:T(8,128)(2,1)}, bf16[512,2048]{1,0:T(8,128)(2,1)}, u32[]{:S(2)}, u32[]{:S(2)}) %collective-permute-start.5) | collective-permute-done | bytes 2097184 | tf_op jit(solution)/shard_map/ppermute | solution.py:368
  51.6 3.6 %collective-permute-done.3.refs_0_.refs_10_ = bf16[128,4096]{1,0:T(8,128)(2,1)} collective-permute-done((bf16[128,4096]{1,0:T(8,128)(2,1)}, bf16[128,4096]{1,0:T(8,128)(2,1)}, u32[]{:S(2)}, u32[]{:S(2)}) %collective-permute-start.3) | collective-permute-done | bytes 1048608 | tf_op jit(solution)/shard_map/ppermute | solution.py:360
  57.6 3.4 %collective-permute-start.7 = (bf16[128,4096]{1,0:T(8,128)(2,1)}, bf16[128,4096]{1,0:T(8,128)(2,1)}, u32[]{:S(2)}, u32[]{:S(2)}) collective-permute-start(bf16[128,4096]{1,0:T(8,128)(2,1)} %collective-permute-done.3.refs_0_.refs_10_), channel_id=1, source_target_pairs={{0,8},{8,16},{16,24},{24,28},{28,20},{20,12},{12,4},{4,0},{1,9},{9... | collective-permute-start | bytes 3145736 | tf_op jit(solution)/shard_map/ppermute | solution.py:360
  61.1 9.1 %shard_map.205.refs_0_.refs_7_ = bf16[256,2048]{1,0:T(8,128)(2,1)S(1)} custom-call(bf16[128,4096]{1,0:T(8,128)(2,1)} %collective-permute-done.3.refs_0_.refs_10_, bf16[128,4096]{1,0:T(8,128)(2,1)} %collective-permute-done.4.refs_1_.refs_11_, bf16[2048,4096]{1,0:T(8,128)(2,1)} %refs_21_.1), custom_call_target="tpu_custom_call" | custom-call | flops 4294967296 | bytes 19922944 | tf_op jit(solution)/shard_map/pallas_call | solution.py:76
  71.3 6.1 %pad_maximum_fusion.refs_0_.refs_1_.refs_2_.refs_3_.refs_4_.refs_5_.refs_6_.refs_7_.refs_8_.refs_9_ = bf16[2048,2048]{1,0:T(8,128)(2,1)} fusion(bf16[512,2048]{1,0:T(8,128)(2,1)S(1)} %collective-permute-done.9, bf16[512,2048]{1,0:T(8,128)(2,1)} %collective-permute-done.2, bf16[512,2048]{1,0:T(8,128)(2,1)} %collective-permute-done.5, ...), kind=kLoop, calls=%fused_computation | loop fusion | flops 33554432 | bytes 16777216 | tf_op jit(solution)/shard_map/concatenate | solution.py:373
  77.5 6.1 %collective-permute-done.7.refs_0_.refs_10_ = bf16[128,4096]{1,0:T(8,128)(2,1)} collective-permute-done((bf16[128,4096]{1,0:T(8,128)(2,1)}, bf16[128,4096]{1,0:T(8,128)(2,1)}, u32[]{:S(2)}, u32[]{:S(2)}) %collective-permute-start.7) | collective-permute-done | bytes 1048608 | tf_op jit(solution)/shard_map/ppermute | solution.py:360
  83.5 2.2 collective-permute-done.8.refs_1_.refs_11_
  85.8 1.5 collective-permute-start.13
  88.1 23.0 %shard_map.206.refs_20_ = bf16[2048,4096]{1,0:T(8,128)(2,1)} custom-call(s32[1]{0:T(128)} %bitcast._.me.refs_0_, s32[192]{0:T(256)} %constant.42.clone.__, bf16[2048,2048]{1,0:T(8,128)(2,1)} %pad_maximum_fusion.refs_0_.refs_1_.refs_2_.refs_3_.refs_4_.refs_5_.refs_6_.refs_7_.refs_8_.refs_9_, ...), custom_call_target="tpu_custom_call" | custom-call | flops 12884901888 | bytes 67108864 | tf_op jit(solution)/shard_map/pallas_call | solution.py:130
  112.6 2.6 shard_map.208
  116.3 13.8 %shard_map.207.refs_0_.refs_2_.refs_4_ = bf16[512,2048]{1,0:T(8,128)(2,1)} custom-call(bf16[128,4096]{1,0:T(8,128)(2,1)} %collective-permute-done.7.refs_0_.refs_10_, bf16[128,4096]{1,0:T(8,128)(2,1)} %collective-permute-done.8.refs_1_.refs_11_, bf16[128,4096]{1,0:T(8,128)(2,1)} %collective-permute-done.12.refs_2_.refs_12_, ...), custom_call_target="tpu_custom_call" | custom-call | flops 8589934592 | bytes 23068672 | tf_op jit(solution)/shard_map/pallas_call | solution.py:76
  130.1 5.1 %collective-permute-done.14.refs_0_.refs_14_ = bf16[128,4096]{1,0:T(8,128)(2,1)S(1)} collective-permute-done((bf16[128,4096]{1,0:T(8,128)(2,1)}, bf16[128,4096]{1,0:T(8,128)(2,1)S(1)}, u32[]{:S(2)}, u32[]{:S(2)}) %collective-permute-start.14) | collective-permute-done | bytes 1048608 | tf_op jit(solution)/shard_map/ppermute | solution.py:360
  135.5 2.5 collective-permute-start.22
  139.5 4.1 %collective-permute-start.20 = (bf16[128,2048]{1,0:T(8,128)(2,1)S(1)}, bf16[128,2048]{1,0:T(8,128)(2,1)S(1)}, u32[]{:S(2)}, u32[]{:S(2)}) collective-permute-start(bf16[128,2048]{1,0:T(8,128)(2,1)S(1)} %shard_map.208), channel_id=1, source_target_pairs={{2,0},{3,1},{6,4},{7,5},{8,10},{10,8},{12,14},{14,12},{17,19},{19,... | collective-permute-start | bytes 1572872 | tf_op jit(solution)/shard_map/ppermute | solution.py:289
  144.9 8.5 %shard_map.210.refs_0_.refs_9_ = bf16[256,2048]{1,0:T(8,128)(2,1)S(1)} custom-call(bf16[128,4096]{1,0:T(8,128)(2,1)S(1)} %collective-permute-done.14.refs_0_.refs_14_, bf16[128,4096]{1,0:T(8,128)(2,1)S(1)} %collective-permute-done.15.refs_1_.refs_15_, bf16[2048,4096]{1,0:T(8,128)(2,1)} %refs_21_.1), custom_call_target="tpu_custom_call" | custom-call | flops 4294967296 | bytes 19922944 | tf_op jit(solution)/shard_map/pallas_call | solution.py:76
  153.5 2.9 %shard_map.211 = (bf16[128,2048]{1,0:T(8,128)(2,1)}, bf16[128,2048]{1,0:T(8,128)(2,1)}, bf16[128,2048]{1,0:T(8,128)(2,1)}) custom-call(s32[1]{0:T(128)} %bitcast._.me.refs_0_, s32[96]{0:T(128)S(1)} %copy-done.21, bf16[512,2048]{1,0:T(8,128)(2,1)S(1)} %copy-done, bf16[512,2048]{1,0:T(8,128)(2,1)S(1)} %collective-permute-done.22.refs_1_.refs_3_.refs_5_, ...), custom_call_target="tpu_custom_call" | custom-call | bytes 4718592 | tf_op jit(solution)/shard_map/pallas_call | solution.py:154
  156.3 4.5 %collective-permute-done.21.refs_9_ = bf16[128,2048]{1,0:T(8,128)(2,1)S(1)} collective-permute-done((bf16[128,2048]{1,0:T(8,128)(2,1)S(1)}, bf16[128,2048]{1,0:T(8,128)(2,1)S(1)}, u32[]{:S(2)}, u32[]{:S(2)}) %collective-permute-start.21) | collective-permute-done | bytes 524320 | tf_op jit(solution)/shard_map/ppermute | solution.py:289
  160.9 2.0 collective-permute-done.18.refs_0_.refs_16_
  171.2 4.0 %shard_map.213.refs_19_ = bf16[512,2048]{1,0:T(8,128)(2,1)} custom-call(s32[1]{0:T(128)} %bitcast._.me.refs_0_, s32[128]{0:T(128)} %constant.47.clone._, s32[128]{0:T(128)} %constant.48.clone.valid, s32[128]{0:T(128)} %constant.49.clone.__, bf16[256,2048]{1,0:T(8,128)(2,1)} %copy-done.2, bf16[256,2048]{1,0:T(8,128)(2,1)} %copy-done.7, ...), custom_call_target="tpu_custom_call" | custom-call | bytes 8388608 | tf_op jit(solution)/shard_map/pallas_call | solution.py:228
  175.2 9.2 %shard_map.212.refs_0_.refs_12_ = bf16[256,2048]{1,0:T(8,128)(2,1)S(1)} custom-call(bf16[128,4096]{1,0:T(8,128)(2,1)} %collective-permute-done.18.refs_0_.refs_16_, bf16[128,4096]{1,0:T(8,128)(2,1)} %collective-permute-done.19.refs_1_.refs_17_, bf16[2048,4096]{1,0:T(8,128)(2,1)} %refs_21_.1), custom_call_target="tpu_custom_call" | custom-call | flops 4294967296 | bytes 19922944 | tf_op jit(solution)/shard_map/pallas_call | solution.py:76
  185.5 2.4 collective-permute-done.26.refs_7_
  187.9 5.3 %collective-permute-done.27.refs_8_ = bf16[128,2048]{1,0:T(8,128)(2,1)} collective-permute-done((bf16[128,2048]{1,0:T(8,128)(2,1)}, bf16[128,2048]{1,0:T(8,128)(2,1)}, u32[]{:S(2)}, u32[]{:S(2)}) %collective-permute-start.27) | collective-permute-done | bytes 524320 | tf_op jit(solution)/shard_map/ppermute | solution.py:289
  194.6 10.4 %shard_map.215 = (bf16[128,2048]{1,0:T(8,128)(2,1)S(1)}, bf16[128,2048]{1,0:T(8,128)(2,1)}, bf16[128,2048]{1,0:T(8,128)(2,1)}, bf16[128,2048]{1,0:T(8,128)(2,1)}) custom-call(s32[1]{0:T(128)} %bitcast._.me.refs_0_, s32[128]{0:T(128)S(1)} %copy-done.18, bf16[128,4096]{1,0:T(8,128)(2,1)S(1)} %collective-permute-done.23.refs_0_.refs_18_, ...), custom_call_target="tpu_custom_call" | custom-call | flops 4294967296 | bytes 19922944 | tf_op jit(solution)/shard_map/pallas_call | solution.py:81
  206.1 4.8 %collective-permute-start.31 = (bf16[128,2048]{1,0:T(8,128)(2,1)S(1)}, bf16[128,2048]{1,0:T(8,128)(2,1)S(1)}, u32[]{:S(2)}, u32[]{:S(2)}) collective-permute-start(bf16[128,2048]{1,0:T(8,128)(2,1)S(1)} %shard_map.216), channel_id=1, source_target_pairs={{0,2},{3,1},{4,6},{7,5},{9,11},{10,8},{13,15},{14,12},{17,19},{18,... | collective-permute-start | bytes 1572872 | tf_op jit(solution)/shard_map/ppermute | solution.py:289
  210.9 2.0 collective-permute-start.32
  214.2 1.5 collective-permute-start.34
  215.7 37.4 %shard_map.217 = (bf16[2048,4096]{1,0:T(8,128)(2,1)}, bf16[2048,4096]{1,0:T(8,128)(2,1)}) custom-call(s32[1]{0:T(128)} %bitcast._.me.refs_0_, s32[320]{0:T(512)} %constant.52.clone.__, bf16[2048,2048]{1,0:T(8,128)(2,1)} %pad_maximum_fusion.refs_0_.refs_1_.refs_2_.refs_3_.refs_4_.refs_5_.refs_6_.refs_7_.refs_8_.refs_9_, ...), custom_call_target="tpu_custom_call" | custom-call | flops 21474836480 | bytes 67108864 | tf_op jit(solution)/shard_map/pallas_call | solution.py:130
  254.3 7.8 %shard_map.218 = bf16[512,2048]{1,0:T(8,128)(2,1)} custom-call(s32[1]{0:T(128)} %bitcast._.me.refs_0_, s32[192]{0:T(256)} %constant.53.clone.refs_1_, s32[192]{0:T(256)} %constant.54.clone.refs_2_, s32[192]{0:T(256)} %constant.55.clone.refs_3_, bf16[512,2048]{1,0:T(8,128)(2,1)} %shard_map.207.refs_0_.refs_2_.refs_4_, ...), custom_call_target="tpu_custom_call", output_to_operand_aliasing={{}: (19, {})} | custom-call | bytes 12582912 | tf_op jit(solution)/shard_map/pallas_call | solution.py:228
  (123 shorter events, 31.3 us)
Async XLA Ops:
  0.6 28.3 %collective-permute-start.2 = (bf16[512,2048]{1,0:T(8,128)(2,1)}, bf16[512,2048]{1,0:T(8,128)(2,1)}, u32[]{:S(2)}, u32[]{:S(2)}) collective-permute-start(bf16[512,2048]{1,0:T(8,128)(2,1)} %param.19), channel_id=1, source_target_pairs={{0,1},{1,0},{2,3},{3,2},{4,5},{5,4},{6,7},{7,6},{8,9},{9,8},{10,11... | collective-permute-start | bytes 6291464 | tf_op jit(solution)/shard_map/ppermute | solution.py:369
  3.1 24.9 %collective-permute-start.1 = (bf16[128,4096]{1,0:T(8,128)(2,1)S(1)}, bf16[128,4096]{1,0:T(8,128)(2,1)}, u32[]{:S(2)}, u32[]{:S(2)}) collective-permute-start(bf16[128,4096]{1,0:T(8,128)(2,1)S(1)} %get-tuple-element.143.refs_1_.refs_7_), channel_id=1, source_target_pairs={{8,0},{16,8},{24,16},{28,24},{20,28},{12,20},{4,12},{0,4},{9,1},{1... | collective-permute-start | bytes 3145736 | tf_op jit(solution)/shard_map/ppermute | solution.py:360
  4.4 24.6 %collective-permute-start = (bf16[128,4096]{1,0:T(8,128)(2,1)S(1)}, bf16[128,4096]{1,0:T(8,128)(2,1)}, u32[]{:S(2)}, u32[]{:S(2)}) collective-permute-start(bf16[128,4096]{1,0:T(8,128)(2,1)S(1)} %get-tuple-element.144.refs_0_.refs_6_), channel_id=1, source_target_pairs={{0,8},{8,16},{16,24},{24,28},{28,20},{20,12},{12,4},{4,0},{1,9},{9... | collective-permute-start | bytes 3145736 | tf_op jit(solution)/shard_map/ppermute | solution.py:360
  4.6 46.9 %collective-permute-start.5 = (bf16[512,2048]{1,0:T(8,128)(2,1)}, bf16[512,2048]{1,0:T(8,128)(2,1)}, u32[]{:S(2)}, u32[]{:S(2)}) collective-permute-start(bf16[512,2048]{1,0:T(8,128)(2,1)} %param.19), channel_id=1, source_target_pairs={{0,2},{1,3},{2,0},{3,1},{4,6},{5,7},{6,4},{7,5},{8,10},{9,11},{10,... | collective-permute-start | bytes 6291464 | tf_op jit(solution)/shard_map/ppermute | solution.py:368
  30.1 25.1 %collective-permute-start.3 = (bf16[128,4096]{1,0:T(8,128)(2,1)}, bf16[128,4096]{1,0:T(8,128)(2,1)}, u32[]{:S(2)}, u32[]{:S(2)}) collective-permute-start(bf16[128,4096]{1,0:T(8,128)(2,1)} %collective-permute-done.refs_0_.refs_8_), channel_id=1, source_target_pairs={{0,8},{8,16},{16,24},{24,28},{28,20},{20,12},{12,4},{4,0},{1,9},{9... | collective-permute-start | bytes 3145736 | tf_op jit(solution)/shard_map/ppermute | solution.py:360
  30.3 24.9 %collective-permute-start.4 = (bf16[128,4096]{1,0:T(8,128)(2,1)}, bf16[128,4096]{1,0:T(8,128)(2,1)}, u32[]{:S(2)}, u32[]{:S(2)}) collective-permute-start(bf16[128,4096]{1,0:T(8,128)(2,1)} %collective-permute-done.1.refs_1_.refs_9_), channel_id=1, source_target_pairs={{8,0},{16,8},{24,16},{28,24},{20,28},{12,20},{4,12},{0,4},{9,1},{1... | collective-permute-start | bytes 3145736 | tf_op jit(solution)/shard_map/ppermute | solution.py:360
  55.2 15.0 %collective-permute-start.9 = (bf16[512,2048]{1,0:T(8,128)(2,1)}, bf16[512,2048]{1,0:T(8,128)(2,1)S(1)}, u32[]{:S(2)}, u32[]{:S(2)}) collective-permute-start(bf16[512,2048]{1,0:T(8,128)(2,1)} %collective-permute-done.5), channel_id=1, source_target_pairs={{0,1},{1,0},{2,3},{3,2},{4,5},{5,4},{6,7},{7,6},{8,9},{9,8},{10,11... | collective-permute-start | bytes 6291464 | tf_op jit(solution)/shard_map/ppermute | solution.py:373
  56.2 21.2 %collective-permute-start.10 = (bf16[128,2048]{1,0:T(8,128)(2,1)S(1)}, bf16[128,2048]{1,0:T(8,128)(2,1)S(1)}, u32[]{:S(2)}, u32[]{:S(2)}) collective-permute-start(bf16[128,2048]{1,0:T(8,128)(2,1)S(1)} %get-tuple-element.82), channel_id=1, source_target_pairs={{2,0},{6,4},{11,9},{15,13},{16,18},{20,22},{25,27},{29,31}} | collective-permute-start | bytes 1572872 | tf_op jit(solution)/shard_map/ppermute | solution.py:289
  56.9 20.6 %collective-permute-start.11 = (bf16[128,2048]{1,0:T(8,128)(2,1)S(1)}, bf16[128,2048]{1,0:T(8,128)(2,1)S(1)}, u32[]{:S(2)}, u32[]{:S(2)}) collective-permute-start(bf16[128,2048]{1,0:T(8,128)(2,1)S(1)} %get-tuple-element.83), channel_id=1, source_target_pairs={{2,0},{6,4},{11,9},{15,13},{16,18},{20,22},{25,27},{29,31}} | collective-permute-start | bytes 1572872 | tf_op jit(solution)/shard_map/ppermute | solution.py:289
  57.6 25.9 %collective-permute-start.7 = (bf16[128,4096]{1,0:T(8,128)(2,1)}, bf16[128,4096]{1,0:T(8,128)(2,1)}, u32[]{:S(2)}, u32[]{:S(2)}) collective-permute-start(bf16[128,4096]{1,0:T(8,128)(2,1)} %collective-permute-done.3.refs_0_.refs_10_), channel_id=1, source_target_pairs={{0,8},{8,16},{16,24},{24,28},{28,20},{20,12},{12,4},{4,0},{1,9},{9... | collective-permute-start | bytes 3145736 | tf_op jit(solution)/shard_map/ppermute | solution.py:360
  61.0 24.7 %collective-permute-start.8 = (bf16[128,4096]{1,0:T(8,128)(2,1)}, bf16[128,4096]{1,0:T(8,128)(2,1)}, u32[]{:S(2)}, u32[]{:S(2)}) collective-permute-start(bf16[128,4096]{1,0:T(8,128)(2,1)} %collective-permute-done.4.refs_1_.refs_11_), channel_id=1, source_target_pairs={{8,0},{16,8},{24,16},{28,24},{20,28},{12,20},{4,12},{0,4},{9,1},{1... | collective-permute-start | bytes 3145736 | tf_op jit(solution)/shard_map/ppermute | solution.py:360
  70.2 42.4 %collective-permute-start.16 = (bf16[256,2048]{1,0:T(8,128)(2,1)}, bf16[256,2048]{1,0:T(8,128)(2,1)S(1)}, u32[]{:S(2)}, u32[]{:S(2)}) collective-permute-start(bf16[256,2048]{1,0:T(8,128)(2,1)} %shard_map.203.refs_0_.refs_4_), channel_id=1, source_target_pairs={{0,1},{1,0},{2,3},{3,2},{4,5},{5,4},{6,7},{7,6},{8,9},{9,8},{10,11... | collective-permute-start | bytes 3145736 | tf_op jit(solution)/shard_map/ppermute | solution.py:298
  85.8 25.3 %collective-permute-start.12 = (bf16[128,4096]{1,0:T(8,128)(2,1)}, bf16[128,4096]{1,0:T(8,128)(2,1)}, u32[]{:S(2)}, u32[]{:S(2)}) collective-permute-start(bf16[128,4096]{1,0:T(8,128)(2,1)} %collective-permute-done.7.refs_0_.refs_10_), channel_id=1, source_target_pairs={{0,8},{8,16},{16,24},{24,28},{28,20},{20,12},{12,4},{4,0},{1,9},{9... | collective-permute-start | bytes 3145736 | tf_op jit(solution)/shard_map/ppermute | solution.py:360
  85.8 25.3 %collective-permute-start.13 = (bf16[128,4096]{1,0:T(8,128)(2,1)}, bf16[128,4096]{1,0:T(8,128)(2,1)}, u32[]{:S(2)}, u32[]{:S(2)}) collective-permute-start(bf16[128,4096]{1,0:T(8,128)(2,1)} %collective-permute-done.8.refs_1_.refs_11_), channel_id=1, source_target_pairs={{8,0},{16,8},{24,16},{28,24},{20,28},{12,20},{4,12},{0,4},{9,1},{1... | collective-permute-start | bytes 3145736 | tf_op jit(solution)/shard_map/ppermute | solution.py:360
  87.3 28.0 %collective-permute-start.17 = (bf16[256,2048]{1,0:T(8,128)(2,1)S(1)}, bf16[256,2048]{1,0:T(8,128)(2,1)S(1)}, u32[]{:S(2)}, u32[]{:S(2)}) collective-permute-start(bf16[256,2048]{1,0:T(8,128)(2,1)S(1)} %shard_map.205.refs_0_.refs_7_), channel_id=1, source_target_pairs={{0,1},{1,0},{2,3},{3,2},{4,5},{5,4},{6,7},{7,6},{8,9},{9,8},{10,11... | collective-permute-start | bytes 3145736 | tf_op jit(solution)/shard_map/ppermute | solution.py:298
  111.1 24.0 %collective-permute-start.14 = (bf16[128,4096]{1,0:T(8,128)(2,1)}, bf16[128,4096]{1,0:T(8,128)(2,1)S(1)}, u32[]{:S(2)}, u32[]{:S(2)}) collective-permute-start(bf16[128,4096]{1,0:T(8,128)(2,1)} %collective-permute-done.12.refs_2_.refs_12_), channel_id=1, source_target_pairs={{0,8},{8,16},{16,24},{24,28},{28,20},{20,12},{12,4},{4,0},{1,9},{9... | collective-permute-start | bytes 3145736 | tf_op jit(solution)/shard_map/ppermute | solution.py:360
  112.2 23.3 %collective-permute-start.15 = (bf16[128,4096]{1,0:T(8,128)(2,1)}, bf16[128,4096]{1,0:T(8,128)(2,1)S(1)}, u32[]{:S(2)}, u32[]{:S(2)}) collective-permute-start(bf16[128,4096]{1,0:T(8,128)(2,1)} %collective-permute-done.13.refs_3_.refs_13_), channel_id=1, source_target_pairs={{8,0},{16,8},{24,16},{28,24},{20,28},{12,20},{4,12},{0,4},{9,1},{1... | collective-permute-start | bytes 3145736 | tf_op jit(solution)/shard_map/ppermute | solution.py:360
  135.5 17.9 %collective-permute-start.22 = (bf16[512,2048]{1,0:T(8,128)(2,1)}, bf16[512,2048]{1,0:T(8,128)(2,1)S(1)}, u32[]{:S(2)}, u32[]{:S(2)}) collective-permute-start(bf16[512,2048]{1,0:T(8,128)(2,1)} %shard_map.207.refs_0_.refs_2_.refs_4_), channel_id=1, source_target_pairs={{0,1},{1,0},{2,3},{3,2},{4,5},{5,4},{6,7},{7,6},{8,9},{9,8},{10,11... | collective-permute-start | bytes 6291464 | tf_op jit(solution)/shard_map/ppermute | solution.py:298
  138.0 24.9 %collective-permute-start.18 = (bf16[128,4096]{1,0:T(8,128)(2,1)S(1)}, bf16[128,4096]{1,0:T(8,128)(2,1)}, u32[]{:S(2)}, u32[]{:S(2)}) collective-permute-start(bf16[128,4096]{1,0:T(8,128)(2,1)S(1)} %collective-permute-done.14.refs_0_.refs_14_), channel_id=1, source_target_pairs={{0,8},{8,16},{16,24},{24,28},{28,20},{20,12},{12,4},{4,0},{1,9},{9... | collective-permute-start | bytes 3145736 | tf_op jit(solution)/shard_map/ppermute | solution.py:360
  139.0 24.6 %collective-permute-start.19 = (bf16[128,4096]{1,0:T(8,128)(2,1)S(1)}, bf16[128,4096]{1,0:T(8,128)(2,1)}, u32[]{:S(2)}, u32[]{:S(2)}) collective-permute-start(bf16[128,4096]{1,0:T(8,128)(2,1)S(1)} %collective-permute-done.15.refs_1_.refs_15_), channel_id=1, source_target_pairs={{8,0},{16,8},{24,16},{28,24},{20,28},{12,20},{4,12},{0,4},{9,1},{1... | collective-permute-start | bytes 3145736 | tf_op jit(solution)/shard_map/ppermute | solution.py:360
  139.5 16.9 %collective-permute-start.20 = (bf16[128,2048]{1,0:T(8,128)(2,1)S(1)}, bf16[128,2048]{1,0:T(8,128)(2,1)S(1)}, u32[]{:S(2)}, u32[]{:S(2)}) collective-permute-start(bf16[128,2048]{1,0:T(8,128)(2,1)S(1)} %shard_map.208), channel_id=1, source_target_pairs={{2,0},{3,1},{6,4},{7,5},{8,10},{10,8},{12,14},{14,12},{17,19},{19,... | collective-permute-start | bytes 1572872 | tf_op jit(solution)/shard_map/ppermute | solution.py:289
  143.6 17.3 %collective-permute-start.21 = (bf16[128,2048]{1,0:T(8,128)(2,1)S(1)}, bf16[128,2048]{1,0:T(8,128)(2,1)S(1)}, u32[]{:S(2)}, u32[]{:S(2)}) collective-permute-start(bf16[128,2048]{1,0:T(8,128)(2,1)S(1)} %shard_map.209), channel_id=1, source_target_pairs={{0,2},{3,1},{4,6},{7,5},{9,11},{10,8},{13,15},{14,12},{17,19},{18,... | collective-permute-start | bytes 1572872 | tf_op jit(solution)/shard_map/ppermute | solution.py:289
  164.7 28.6 %collective-permute-start.23 = (bf16[128,4096]{1,0:T(8,128)(2,1)}, bf16[128,4096]{1,0:T(8,128)(2,1)S(1)}, u32[]{:S(2)}, u32[]{:S(2)}) collective-permute-start(bf16[128,4096]{1,0:T(8,128)(2,1)} %collective-permute-done.18.refs_0_.refs_16_), channel_id=1, source_target_pairs={{0,8},{8,16},{16,24},{24,28},{28,20},{20,12},{12,4},{4,0},{1,9},{9... | collective-permute-start | bytes 3145736 | tf_op jit(solution)/shard_map/ppermute | solution.py:360
  165.7 27.5 %collective-permute-start.24 = (bf16[128,4096]{1,0:T(8,128)(2,1)}, bf16[128,4096]{1,0:T(8,128)(2,1)}, u32[]{:S(2)}, u32[]{:S(2)}) collective-permute-start(bf16[128,4096]{1,0:T(8,128)(2,1)} %collective-permute-done.19.refs_1_.refs_17_), channel_id=1, source_target_pairs={{8,0},{16,8},{24,16},{28,24},{20,28},{12,20},{4,12},{0,4},{9,1},{1... | collective-permute-start | bytes 3145736 | tf_op jit(solution)/shard_map/ppermute | solution.py:360
  166.1 19.3 %collective-permute-start.25 = (bf16[128,2048]{1,0:T(8,128)(2,1)}, bf16[128,2048]{1,0:T(8,128)(2,1)}, u32[]{:S(2)}, u32[]{:S(2)}) collective-permute-start(bf16[128,2048]{1,0:T(8,128)(2,1)} %get-tuple-element.109), channel_id=1, source_target_pairs={{0,2},{1,3},{4,6},{5,7},{8,10},{9,11},{11,9},{12,14},{13,15},{15,1... | collective-permute-start | bytes 1572872 | tf_op jit(solution)/shard_map/ppermute | solution.py:289
  167.4 20.5 %collective-permute-start.26 = (bf16[128,2048]{1,0:T(8,128)(2,1)}, bf16[128,2048]{1,0:T(8,128)(2,1)}, u32[]{:S(2)}, u32[]{:S(2)}) collective-permute-start(bf16[128,2048]{1,0:T(8,128)(2,1)} %get-tuple-element.110), channel_id=1, source_target_pairs={{1,3},{5,7},{8,10},{12,14},{19,17},{23,21},{26,24},{30,28}} | collective-permute-start | bytes 1572872 | tf_op jit(solution)/shard_map/ppermute | solution.py:289
  169.7 23.5 %collective-permute-start.27 = (bf16[128,2048]{1,0:T(8,128)(2,1)}, bf16[128,2048]{1,0:T(8,128)(2,1)}, u32[]{:S(2)}, u32[]{:S(2)}) collective-permute-start(bf16[128,2048]{1,0:T(8,128)(2,1)} %get-tuple-element.111), channel_id=1, source_target_pairs={{1,3},{5,7},{26,24},{30,28}} | collective-permute-start | bytes 1572872 | tf_op jit(solution)/shard_map/ppermute | solution.py:289
  193.3 59.8 %collective-permute-start.30 = (bf16[128,2048]{1,0:T(8,128)(2,1)S(1)}, bf16[128,2048]{1,0:T(8,128)(2,1)}, u32[]{:S(2)}, u32[]{:S(2)}) collective-permute-start(bf16[128,2048]{1,0:T(8,128)(2,1)S(1)} %shard_map.214), channel_id=1, source_target_pairs={{0,2},{1,3},{4,6},{5,7},{9,11},{11,9},{13,15},{15,13},{16,18},{18,... | collective-permute-start | bytes 1572872 | tf_op jit(solution)/shard_map/ppermute | solution.py:289
  206.1 47.0 %collective-permute-start.31 = (bf16[128,2048]{1,0:T(8,128)(2,1)S(1)}, bf16[128,2048]{1,0:T(8,128)(2,1)S(1)}, u32[]{:S(2)}, u32[]{:S(2)}) collective-permute-start(bf16[128,2048]{1,0:T(8,128)(2,1)S(1)} %shard_map.216), channel_id=1, source_target_pairs={{0,2},{3,1},{4,6},{7,5},{9,11},{10,8},{13,15},{14,12},{17,19},{18,... | collective-permute-start | bytes 1572872 | tf_op jit(solution)/shard_map/ppermute | solution.py:289
  210.9 42.2 %collective-permute-start.32 = (bf16[128,2048]{1,0:T(8,128)(2,1)}, bf16[128,2048]{1,0:T(8,128)(2,1)S(1)}, u32[]{:S(2)}, u32[]{:S(2)}) collective-permute-start(bf16[128,2048]{1,0:T(8,128)(2,1)} %get-tuple-element.130), channel_id=1, source_target_pairs={{0,1},{3,0},{4,5},{7,4},{9,10},{11,8},{13,14},{15,12},{16,17},{18,... | collective-permute-start | bytes 1572872 | tf_op jit(solution)/shard_map/ppermute | solution.py:289
  212.8 40.3 %collective-permute-start.33 = (bf16[128,2048]{1,0:T(8,128)(2,1)}, bf16[128,2048]{1,0:T(8,128)(2,1)S(1)}, u32[]{:S(2)}, u32[]{:S(2)}) collective-permute-start(bf16[128,2048]{1,0:T(8,128)(2,1)} %get-tuple-element.131), channel_id=1, source_target_pairs={{2,0},{3,1},{6,4},{7,5},{8,10},{10,8},{12,14},{14,12},{17,19},{19,... | collective-permute-start | bytes 1572872 | tf_op jit(solution)/shard_map/ppermute | solution.py:289
  214.2 39.0 %collective-permute-start.34 = (bf16[128,2048]{1,0:T(8,128)(2,1)}, bf16[128,2048]{1,0:T(8,128)(2,1)}, u32[]{:S(2)}, u32[]{:S(2)}) collective-permute-start(bf16[128,2048]{1,0:T(8,128)(2,1)} %get-tuple-element.132), channel_id=1, source_target_pairs={{1,0},{2,1},{5,4},{6,5},{9,8},{11,10},{13,12},{15,14},{16,19},{18,... | collective-permute-start | bytes 1572872 | tf_op jit(solution)/shard_map/ppermute | solution.py:289
  (36 other events, 569.9 us)

commit v4 on v3

--- a/solution.py
+++ b/solution.py
@@ -65,7 +65,7 @@
     parts, half = len(pieces[0]), pieces[0][0].shape[0]
     feats, cols = weight.shape
     rows = half * len(pieces)
-    tile = fit(feats, tile)
+    tile = fit(feats, tile if rows > 2 * half else 2 * tile)
     flat = [x for p in pieces for x in p]
     specs = [pl.BlockSpec(x.shape, lambda i, *_: (0, 0)) for x in flat]
     specs.append(pl.BlockSpec((tile, cols), lambda i, *_: (i, 0)))
@@ -326,7 +326,7 @@
     early = list(range(0, mid - 1))
     late = list(range(mid - 1, n_row))
     at_work = {
-        1: ([0], 0, 0, 0),
+        1: ([0], 0, 2, 0),
         2: ([1], 2, 0, 0),
         mid - 1: (list(range(2, mid - 1)), 1, 0, 0),
         mid + 1: ([mid - 1, mid], 0, 0, 0),
@@ -362,7 +362,7 @@
         if k in at_work:
             work = grad_in_part(pieces_of(at_work[k][0]), weight)
         elif k == mid:
-            work = token_pass(me, order_of(early), attn_all, whole_pieces(early), (momentum,), out_dtype=BF16)
+            work = token_pass(me, order_of(early), attn_all, whole_pieces(early), (momentum,), out_dtype=BF16, tile=1024)
         extra = ()
         if k == 1:
             far = [lax.ppermute(attn, "col", [(c, (c - s) % n_col) for c in range(n_col)]) for s in range(2, n_col, 2)]

time: 264 us -> 259 us (0.981)
  starting transfers between devices: 42.7 us -> 39.9 us
where the time goes in v4:
time: 259 us; the launch traced here: 258 us
  Pallas kernels  149 us (58%)
  waiting for transfers between devices  57.7 us (22%)
  starting transfers between devices  39.9 us (15%)
  other arithmetic  6.5 us (3%)
  local copies, waits for them, and re-layouts  3.93 us (2%)
    pallas_call x2, Pallas kernels, token_pass(): call(functools.partial(pass_kernel, n=n, n_grads=n, last=last, n_old=len(...  59.2 us
    pallas_call x6, Pallas kernels, grad_in_part(): call(kernel, (feats // tile,), specs, out, jax.ShapeDtypeStruct((rows, fe...  57.3 us
    ppermute x14, waiting for transfers between devices, body(): nxt = (lax.ppermute(a, 'row', right), lax.ppermute(b, 'row', left))  36.5 us
    ppermute x12, starting transfers between devices, send(): lax.ppermute(x, ('row', 'col'), route(valid, shift, s))  19.7 us
    ppermute x12, waiting for transfers between devices, send(): lax.ppermute(x, ('row', 'col'), route(valid, shift, s))  13.2 us
    pallas_call x2, Pallas kernels, place(): call(kernel, (n,), specs, spec, jax.ShapeDtypeStruct(shape, BF16), scalar...  11.8 us
    pallas_call x6, Pallas kernels, pair_sum(): call(functools.partial(pair_sum_kernel, n=n), (width // tile,), picked, [...  10.7 us
    ppermute x14, starting transfers between devices, body(): nxt = (lax.ppermute(a, 'row', right), lax.ppermute(b, 'row', left))  10.4 us
  transfers between devices with their start and end apart: 35, of which 13 were waited for; matrix products, arithmetic and copies ran while one was open for 3% of the time, Pallas kernels for 55%

profile of v4, /device:TPU:5, one launch (start us, length us, event | category | flops | bytes accessed | tf_op | source)
XLA Modules:
  0.0 258.4 jit_solution(5066496406799677625)
XLA Ops:
  1.4 1.7 fusion
  4.8 8.2 %shard_map.202.refs_0_.refs_2_ = bf16[256,2048]{1,0:T(8,128)(2,1)S(1)} custom-call(bf16[128,4096]{1,0:T(8,128)(2,1)S(1)} %get-tuple-element.144.refs_0_.refs_6_, bf16[128,4096]{1,0:T(8,128)(2,1)S(1)} %get-tuple-element.143.refs_1_.refs_7_, bf16[2048,4096]{1,0:T(8,128)(2,1)} %refs_21_.1), custom_call_target="tpu_custom_call" | custom-call | flops 4294967296 | bytes 19922944 | tf_op jit(solution)/shard_map/pallas_call | solution.py:76
  13.0 15.1 %collective-permute-done.1.refs_1_.refs_9_ = bf16[128,4096]{1,0:T(8,128)(2,1)} collective-permute-done((bf16[128,4096]{1,0:T(8,128)(2,1)S(1)}, bf16[128,4096]{1,0:T(8,128)(2,1)}, u32[]{:S(2)}, u32[]{:S(2)}) %collective-permute-start.1) | collective-permute-done | bytes 1048608 | tf_op jit(solution)/shard_map/ppermute | solution.py:360
  31.5 9.6 %shard_map.203.refs_0_.refs_4_ = bf16[256,2048]{1,0:T(8,128)(2,1)} custom-call(bf16[128,4096]{1,0:T(8,128)(2,1)} %collective-permute-done.refs_0_.refs_8_, bf16[128,4096]{1,0:T(8,128)(2,1)} %collective-permute-done.1.refs_1_.refs_9_, bf16[2048,4096]{1,0:T(8,128)(2,1)} %refs_21_.1), custom_call_target="tpu_custom_call" | custom-call | flops 4294967296 | bytes 19922944 | tf_op jit(solution)/shard_map/pallas_call | solution.py:76
  41.1 2.4 shard_map.204
  43.5 8.0 %collective-permute-done.5 = bf16[512,2048]{1,0:T(8,128)(2,1)} collective-permute-done((bf16[512,2048]{1,0:T(8,128)(2,1)}, bf16[512,2048]{1,0:T(8,128)(2,1)}, u32[]{:S(2)}, u32[]{:S(2)}) %collective-permute-start.5) | collective-permute-done | bytes 2097184 | tf_op jit(solution)/shard_map/ppermute | solution.py:368
  51.6 3.6 %collective-permute-done.3.refs_0_.refs_10_ = bf16[128,4096]{1,0:T(8,128)(2,1)} collective-permute-done((bf16[128,4096]{1,0:T(8,128)(2,1)}, bf16[128,4096]{1,0:T(8,128)(2,1)}, u32[]{:S(2)}, u32[]{:S(2)}) %collective-permute-start.3) | collective-permute-done | bytes 1048608 | tf_op jit(solution)/shard_map/ppermute | solution.py:360
  58.2 8.8 %shard_map.205.refs_0_.refs_7_ = bf16[256,2048]{1,0:T(8,128)(2,1)S(1)} custom-call(bf16[128,4096]{1,0:T(8,128)(2,1)} %collective-permute-done.3.refs_0_.refs_10_, bf16[128,4096]{1,0:T(8,128)(2,1)} %collective-permute-done.4.refs_1_.refs_11_, bf16[2048,4096]{1,0:T(8,128)(2,1)} %refs_21_.1), custom_call_target="tpu_custom_call" | custom-call | flops 4294967296 | bytes 19922944 | tf_op jit(solution)/shard_map/pallas_call | solution.py:76
  67.1 6.5 %pad_maximum_fusion.refs_0_.refs_1_.refs_2_.refs_3_.refs_4_.refs_5_.refs_6_.refs_7_.refs_8_.refs_9_ = bf16[2048,2048]{1,0:T(8,128)(2,1)} fusion(bf16[512,2048]{1,0:T(8,128)(2,1)S(1)} %collective-permute-done.9, bf16[512,2048]{1,0:T(8,128)(2,1)} %collective-permute-done.2, bf16[512,2048]{1,0:T(8,128)(2,1)} %collective-permute-done.5, ...), kind=kLoop, calls=%fused_computation | loop fusion | flops 33554432 | bytes 16777216 | tf_op jit(solution)/shard_map/concatenate | solution.py:373
  73.6 7.8 %collective-permute-done.7.refs_0_.refs_10_ = bf16[128,4096]{1,0:T(8,128)(2,1)} collective-permute-done((bf16[128,4096]{1,0:T(8,128)(2,1)}, bf16[128,4096]{1,0:T(8,128)(2,1)}, u32[]{:S(2)}, u32[]{:S(2)}) %collective-permute-start.7) | collective-permute-done | bytes 1048608 | tf_op jit(solution)/shard_map/ppermute | solution.py:360
  83.8 1.7 collective-permute-start.17
  85.4 21.8 %shard_map.206.refs_20_ = bf16[2048,4096]{1,0:T(8,128)(2,1)} custom-call(s32[1]{0:T(128)} %bitcast._.me.refs_0_, s32[192]{0:T(256)} %constant.42.clone.__, bf16[2048,2048]{1,0:T(8,128)(2,1)} %pad_maximum_fusion.refs_0_.refs_1_.refs_2_.refs_3_.refs_4_.refs_5_.refs_6_.refs_7_.refs_8_.refs_9_, ...), custom_call_target="tpu_custom_call" | custom-call | flops 12884901888 | bytes 67108864 | tf_op jit(solution)/shard_map/pallas_call | solution.py:130
  107.3 1.3 collective-permute-start.12
  110.4 2.6 %shard_map.208 = bf16[128,2048]{1,0:T(8,128)(2,1)S(1)} custom-call(s32[1]{0:T(128)} %bitcast._.me.refs_0_, s32[32]{0:T(128)S(1)} %copy-done.23, bf16[256,2048]{1,0:T(8,128)(2,1)} %shard_map.203.refs_0_.refs_4_, bf16[256,2048]{1,0:T(8,128)(2,1)S(1)} %collective-permute-done.16.refs_1_.refs_5_), custom_call_target="tpu_custom_call" | custom-call | bytes 1572864 | tf_op jit(solution)/shard_map/pallas_call | solution.py:154
  114.0 13.8 %shard_map.207.refs_0_.refs_2_.refs_4_ = bf16[512,2048]{1,0:T(8,128)(2,1)} custom-call(bf16[128,4096]{1,0:T(8,128)(2,1)} %collective-permute-done.7.refs_0_.refs_10_, bf16[128,4096]{1,0:T(8,128)(2,1)} %collective-permute-done.8.refs_1_.refs_11_, bf16[128,4096]{1,0:T(8,128)(2,1)} %collective-permute-done.10.refs_2_.refs_12_, ...), custom_call_target="tpu_custom_call" | custom-call | flops 8589934592 | bytes 23068672 | tf_op jit(solution)/shard_map/pallas_call | solution.py:76
  127.9 2.2 collective-permute-done.12.refs_0_.refs_14_
  131.1 3.4 %collective-permute-start.22 = (bf16[512,2048]{1,0:T(8,128)(2,1)}, bf16[512,2048]{1,0:T(8,128)(2,1)S(1)}, u32[]{:S(2)}, u32[]{:S(2)}) collective-permute-start(bf16[512,2048]{1,0:T(8,128)(2,1)} %shard_map.207.refs_0_.refs_2_.refs_4_), channel_id=1, source_target_pairs={{0,1},{1,0},{2,3},{3,2},{4,5},{5,4},{6,7},{7,6},{8,9},{9,8},{10,11... | collective-permute-start | bytes 6291464 | tf_op jit(solution)/shard_map/ppermute | solution.py:298
  135.9 2.2 collective-permute-start.20
  139.4 8.2 %shard_map.210.refs_0_.refs_9_ = bf16[256,2048]{1,0:T(8,128)(2,1)S(1)} custom-call(bf16[128,4096]{1,0:T(8,128)(2,1)S(1)} %collective-permute-done.12.refs_0_.refs_14_, bf16[128,4096]{1,0:T(8,128)(2,1)S(1)} %collective-permute-done.13.refs_1_.refs_15_, bf16[2048,4096]{1,0:T(8,128)(2,1)} %refs_21_.1), custom_call_target="tpu_custom_call" | custom-call | flops 4294967296 | bytes 19922944 | tf_op jit(solution)/shard_map/pallas_call | solution.py:76
  147.7 2.8 %shard_map.211 = (bf16[128,2048]{1,0:T(8,128)(2,1)}, bf16[128,2048]{1,0:T(8,128)(2,1)}, bf16[128,2048]{1,0:T(8,128)(2,1)}) custom-call(s32[1]{0:T(128)} %bitcast._.me.refs_0_, s32[96]{0:T(128)S(1)} %copy-done.21, bf16[512,2048]{1,0:T(8,128)(2,1)S(1)} %copy-done, bf16[512,2048]{1,0:T(8,128)(2,1)S(1)} %collective-permute-done.22.refs_1_.refs_3_.refs_5_, ...), custom_call_target="tpu_custom_call" | custom-call | bytes 4718592 | tf_op jit(solution)/shard_map/pallas_call | solution.py:154
  150.5 4.9 %collective-permute-done.21.refs_9_ = bf16[128,2048]{1,0:T(8,128)(2,1)S(1)} collective-permute-done((bf16[128,2048]{1,0:T(8,128)(2,1)S(1)}, bf16[128,2048]{1,0:T(8,128)(2,1)S(1)}, u32[]{:S(2)}, u32[]{:S(2)}) %collective-permute-start.21) | collective-permute-done | bytes 524320 | tf_op jit(solution)/shard_map/ppermute | solution.py:289
  155.4 4.0 %collective-permute-done.18.refs_0_.refs_16_ = bf16[128,4096]{1,0:T(8,128)(2,1)} collective-permute-done((bf16[128,4096]{1,0:T(8,128)(2,1)S(1)}, bf16[128,4096]{1,0:T(8,128)(2,1)}, u32[]{:S(2)}, u32[]{:S(2)}) %collective-permute-start.18) | collective-permute-done | bytes 1048608 | tf_op jit(solution)/shard_map/ppermute | solution.py:360
  167.7 4.0 %shard_map.213.refs_19_ = bf16[512,2048]{1,0:T(8,128)(2,1)} custom-call(s32[1]{0:T(128)} %bitcast._.me.refs_0_, s32[128]{0:T(128)} %constant.47.clone._, s32[128]{0:T(128)} %constant.48.clone.valid, s32[128]{0:T(128)} %constant.49.clone.__, bf16[256,2048]{1,0:T(8,128)(2,1)} %copy-done.2, bf16[256,2048]{1,0:T(8,128)(2,1)} %copy-done.7, ...), custom_call_target="tpu_custom_call" | custom-call | bytes 8388608 | tf_op jit(solution)/shard_map/pallas_call | solution.py:228
  171.8 8.9 %shard_map.212.refs_0_.refs_12_ = bf16[256,2048]{1,0:T(8,128)(2,1)S(1)} custom-call(bf16[128,4096]{1,0:T(8,128)(2,1)} %collective-permute-done.18.refs_0_.refs_16_, bf16[128,4096]{1,0:T(8,128)(2,1)} %collective-permute-done.19.refs_1_.refs_17_, bf16[2048,4096]{1,0:T(8,128)(2,1)} %refs_21_.1), custom_call_target="tpu_custom_call" | custom-call | flops 4294967296 | bytes 19922944 | tf_op jit(solution)/shard_map/pallas_call | solution.py:76
  181.7 3.0 %collective-permute-done.26.refs_7_ = bf16[128,2048]{1,0:T(8,128)(2,1)} collective-permute-done((bf16[128,2048]{1,0:T(8,128)(2,1)}, bf16[128,2048]{1,0:T(8,128)(2,1)}, u32[]{:S(2)}, u32[]{:S(2)}) %collective-permute-start.26) | collective-permute-done | bytes 524320 | tf_op jit(solution)/shard_map/ppermute | solution.py:289
  184.6 5.3 %collective-permute-done.27.refs_8_ = bf16[128,2048]{1,0:T(8,128)(2,1)} collective-permute-done((bf16[128,2048]{1,0:T(8,128)(2,1)}, bf16[128,2048]{1,0:T(8,128)(2,1)}, u32[]{:S(2)}, u32[]{:S(2)}) %collective-permute-start.27) | collective-permute-done | bytes 524320 | tf_op jit(solution)/shard_map/ppermute | solution.py:289
  191.4 10.0 %shard_map.215 = (bf16[128,2048]{1,0:T(8,128)(2,1)S(1)}, bf16[128,2048]{1,0:T(8,128)(2,1)}, bf16[128,2048]{1,0:T(8,128)(2,1)}, bf16[128,2048]{1,0:T(8,128)(2,1)}) custom-call(s32[1]{0:T(128)} %bitcast._.me.refs_0_, s32[128]{0:T(128)S(1)} %copy-done.18, bf16[128,4096]{1,0:T(8,128)(2,1)S(1)} %collective-permute-done.23.refs_0_.refs_18_, ...), custom_call_target="tpu_custom_call" | custom-call | flops 4294967296 | bytes 19922944 | tf_op jit(solution)/shard_map/pallas_call | solution.py:81
  202.4 4.8 %collective-permute-start.31 = (bf16[128,2048]{1,0:T(8,128)(2,1)S(1)}, bf16[128,2048]{1,0:T(8,128)(2,1)S(1)}, u32[]{:S(2)}, u32[]{:S(2)}) collective-permute-start(bf16[128,2048]{1,0:T(8,128)(2,1)S(1)} %shard_map.216), channel_id=1, source_target_pairs={{0,2},{3,1},{4,6},{7,5},{9,11},{10,8},{13,15},{14,12},{17,19},{18,... | collective-permute-start | bytes 1572872 | tf_op jit(solution)/shard_map/ppermute | solution.py:289
  207.1 2.0 collective-permute-start.32
  210.5 1.5 collective-permute-start.34
  212.0 37.4 %shard_map.217 = (bf16[2048,4096]{1,0:T(8,128)(2,1)}, bf16[2048,4096]{1,0:T(8,128)(2,1)}) custom-call(s32[1]{0:T(128)} %bitcast._.me.refs_0_, s32[320]{0:T(512)} %constant.52.clone.__, bf16[2048,2048]{1,0:T(8,128)(2,1)} %pad_maximum_fusion.refs_0_.refs_1_.refs_2_.refs_3_.refs_4_.refs_5_.refs_6_.refs_7_.refs_8_.refs_9_, ...), custom_call_target="tpu_custom_call" | custom-call | flops 21474836480 | bytes 67108864 | tf_op jit(solution)/shard_map/pallas_call | solution.py:130
  250.6 7.8 %shard_map.218 = bf16[512,2048]{1,0:T(8,128)(2,1)} custom-call(s32[1]{0:T(128)} %bitcast._.me.refs_0_, s32[192]{0:T(256)} %constant.53.clone.refs_1_, s32[192]{0:T(256)} %constant.54.clone.refs_2_, s32[192]{0:T(256)} %constant.55.clone.refs_3_, bf16[512,2048]{1,0:T(8,128)(2,1)} %shard_map.207.refs_0_.refs_2_.refs_4_, ...), custom_call_target="tpu_custom_call", output_to_operand_aliasing={{}: (19, {})} | custom-call | bytes 12582912 | tf_op jit(solution)/shard_map/pallas_call | solution.py:228
  (123 shorter events, 32.1 us)
Async XLA Ops:
  0.6 28.3 %collective-permute-start.2 = (bf16[512,2048]{1,0:T(8,128)(2,1)}, bf16[512,2048]{1,0:T(8,128)(2,1)}, u32[]{:S(2)}, u32[]{:S(2)}) collective-permute-start(bf16[512,2048]{1,0:T(8,128)(2,1)} %param.19), channel_id=1, source_target_pairs={{0,1},{1,0},{2,3},{3,2},{4,5},{5,4},{6,7},{7,6},{8,9},{9,8},{10,11... | collective-permute-start | bytes 6291464 | tf_op jit(solution)/shard_map/ppermute | solution.py:369
  3.1 24.9 %collective-permute-start.1 = (bf16[128,4096]{1,0:T(8,128)(2,1)S(1)}, bf16[128,4096]{1,0:T(8,128)(2,1)}, u32[]{:S(2)}, u32[]{:S(2)}) collective-permute-start(bf16[128,4096]{1,0:T(8,128)(2,1)S(1)} %get-tuple-element.143.refs_1_.refs_7_), channel_id=1, source_target_pairs={{8,0},{16,8},{24,16},{28,24},{20,28},{12,20},{4,12},{0,4},{9,1},{1... | collective-permute-start | bytes 3145736 | tf_op jit(solution)/shard_map/ppermute | solution.py:360
  4.4 24.6 %collective-permute-start = (bf16[128,4096]{1,0:T(8,128)(2,1)S(1)}, bf16[128,4096]{1,0:T(8,128)(2,1)}, u32[]{:S(2)}, u32[]{:S(2)}) collective-permute-start(bf16[128,4096]{1,0:T(8,128)(2,1)S(1)} %get-tuple-element.144.refs_0_.refs_6_), channel_id=1, source_target_pairs={{0,8},{8,16},{16,24},{24,28},{28,20},{20,12},{12,4},{4,0},{1,9},{9... | collective-permute-start | bytes 3145736 | tf_op jit(solution)/shard_map/ppermute | solution.py:360
  4.6 46.9 %collective-permute-start.5 = (bf16[512,2048]{1,0:T(8,128)(2,1)}, bf16[512,2048]{1,0:T(8,128)(2,1)}, u32[]{:S(2)}, u32[]{:S(2)}) collective-permute-start(bf16[512,2048]{1,0:T(8,128)(2,1)} %param.19), channel_id=1, source_target_pairs={{0,2},{1,3},{2,0},{3,1},{4,6},{5,7},{6,4},{7,5},{8,10},{9,11},{10,... | collective-permute-start | bytes 6291464 | tf_op jit(solution)/shard_map/ppermute | solution.py:368
  28.9 12.1 %collective-permute-start.6 = (bf16[256,2048]{1,0:T(8,128)(2,1)S(1)}, bf16[256,2048]{1,0:T(8,128)(2,1)S(1)}, u32[]{:S(2)}, u32[]{:S(2)}) collective-permute-start(bf16[256,2048]{1,0:T(8,128)(2,1)S(1)} %shard_map.202.refs_0_.refs_2_), channel_id=1, source_target_pairs={{0,1},{1,0},{2,3},{3,2},{4,5},{5,4},{6,7},{7,6},{8,9},{9,8},{10,11... | collective-permute-start | bytes 3145736 | tf_op jit(solution)/shard_map/ppermute | solution.py:298
  30.1 25.1 %collective-permute-start.3 = (bf16[128,4096]{1,0:T(8,128)(2,1)}, bf16[128,4096]{1,0:T(8,128)(2,1)}, u32[]{:S(2)}, u32[]{:S(2)}) collective-permute-start(bf16[128,4096]{1,0:T(8,128)(2,1)} %collective-permute-done.refs_0_.refs_8_), channel_id=1, source_target_pairs={{0,8},{8,16},{16,24},{24,28},{28,20},{20,12},{12,4},{4,0},{1,9},{9... | collective-permute-start | bytes 3145736 | tf_op jit(solution)/shard_map/ppermute | solution.py:360
  30.3 24.9 %collective-permute-start.4 = (bf16[128,4096]{1,0:T(8,128)(2,1)}, bf16[128,4096]{1,0:T(8,128)(2,1)}, u32[]{:S(2)}, u32[]{:S(2)}) collective-permute-start(bf16[128,4096]{1,0:T(8,128)(2,1)} %collective-permute-done.1.refs_1_.refs_9_), channel_id=1, source_target_pairs={{8,0},{16,8},{24,16},{28,24},{20,28},{12,20},{4,12},{0,4},{9,1},{1... | collective-permute-start | bytes 3145736 | tf_op jit(solution)/shard_map/ppermute | solution.py:360
  56.2 25.1 %collective-permute-start.7 = (bf16[128,4096]{1,0:T(8,128)(2,1)}, bf16[128,4096]{1,0:T(8,128)(2,1)}, u32[]{:S(2)}, u32[]{:S(2)}) collective-permute-start(bf16[128,4096]{1,0:T(8,128)(2,1)} %collective-permute-done.3.refs_0_.refs_10_), channel_id=1, source_target_pairs={{0,8},{8,16},{16,24},{24,28},{28,20},{20,12},{12,4},{4,0},{1,9},{9... | collective-permute-start | bytes 3145736 | tf_op jit(solution)/shard_map/ppermute | solution.py:360
  57.5 24.8 %collective-permute-start.8 = (bf16[128,4096]{1,0:T(8,128)(2,1)}, bf16[128,4096]{1,0:T(8,128)(2,1)}, u32[]{:S(2)}, u32[]{:S(2)}) collective-permute-start(bf16[128,4096]{1,0:T(8,128)(2,1)} %collective-permute-done.4.refs_1_.refs_11_), channel_id=1, source_target_pairs={{8,0},{16,8},{24,16},{28,24},{20,28},{12,20},{4,12},{0,4},{9,1},{1... | collective-permute-start | bytes 3145736 | tf_op jit(solution)/shard_map/ppermute | solution.py:360
  57.7 51.8 %collective-permute-start.16 = (bf16[256,2048]{1,0:T(8,128)(2,1)}, bf16[256,2048]{1,0:T(8,128)(2,1)S(1)}, u32[]{:S(2)}, u32[]{:S(2)}) collective-permute-start(bf16[256,2048]{1,0:T(8,128)(2,1)} %shard_map.203.refs_0_.refs_4_), channel_id=1, source_target_pairs={{0,1},{1,0},{2,3},{3,2},{4,5},{5,4},{6,7},{7,6},{8,9},{9,8},{10,11... | collective-permute-start | bytes 3145736 | tf_op jit(solution)/shard_map/ppermute | solution.py:298
  82.3 25.0 %collective-permute-start.10 = (bf16[128,4096]{1,0:T(8,128)(2,1)}, bf16[128,4096]{1,0:T(8,128)(2,1)}, u32[]{:S(2)}, u32[]{:S(2)}) collective-permute-start(bf16[128,4096]{1,0:T(8,128)(2,1)} %collective-permute-done.7.refs_0_.refs_10_), channel_id=1, source_target_pairs={{0,8},{8,16},{16,24},{24,28},{28,20},{20,12},{12,4},{4,0},{1,9},{9... | collective-permute-start | bytes 3145736 | tf_op jit(solution)/shard_map/ppermute | solution.py:360
  83.6 23.7 %collective-permute-start.11 = (bf16[128,4096]{1,0:T(8,128)(2,1)}, bf16[128,4096]{1,0:T(8,128)(2,1)}, u32[]{:S(2)}, u32[]{:S(2)}) collective-permute-start(bf16[128,4096]{1,0:T(8,128)(2,1)} %collective-permute-done.8.refs_1_.refs_11_), channel_id=1, source_target_pairs={{8,0},{16,8},{24,16},{28,24},{20,28},{12,20},{4,12},{0,4},{9,1},{1... | collective-permute-start | bytes 3145736 | tf_op jit(solution)/shard_map/ppermute | solution.py:360
  83.8 29.3 %collective-permute-start.17 = (bf16[256,2048]{1,0:T(8,128)(2,1)S(1)}, bf16[256,2048]{1,0:T(8,128)(2,1)S(1)}, u32[]{:S(2)}, u32[]{:S(2)}) collective-permute-start(bf16[256,2048]{1,0:T(8,128)(2,1)S(1)} %shard_map.205.refs_0_.refs_7_), channel_id=1, source_target_pairs={{0,1},{1,0},{2,3},{3,2},{4,5},{5,4},{6,7},{7,6},{8,9},{9,8},{10,11... | collective-permute-start | bytes 3145736 | tf_op jit(solution)/shard_map/ppermute | solution.py:298
  107.3 22.8 %collective-permute-start.12 = (bf16[128,4096]{1,0:T(8,128)(2,1)}, bf16[128,4096]{1,0:T(8,128)(2,1)S(1)}, u32[]{:S(2)}, u32[]{:S(2)}) collective-permute-start(bf16[128,4096]{1,0:T(8,128)(2,1)} %collective-permute-done.10.refs_2_.refs_12_), channel_id=1, source_target_pairs={{0,8},{8,16},{16,24},{24,28},{28,20},{20,12},{12,4},{4,0},{1,9},{9... | collective-permute-start | bytes 3145736 | tf_op jit(solution)/shard_map/ppermute | solution.py:360
  108.6 22.4 %collective-permute-start.13 = (bf16[128,4096]{1,0:T(8,128)(2,1)}, bf16[128,4096]{1,0:T(8,128)(2,1)S(1)}, u32[]{:S(2)}, u32[]{:S(2)}) collective-permute-start(bf16[128,4096]{1,0:T(8,128)(2,1)} %collective-permute-done.11.refs_3_.refs_13_), channel_id=1, source_target_pairs={{8,0},{16,8},{24,16},{28,24},{20,28},{12,20},{4,12},{0,4},{9,1},{1... | collective-permute-start | bytes 3145736 | tf_op jit(solution)/shard_map/ppermute | solution.py:360
  108.8 19.0 %collective-permute-start.14 = (bf16[128,2048]{1,0:T(8,128)(2,1)}, bf16[128,2048]{1,0:T(8,128)(2,1)S(1)}, u32[]{:S(2)}, u32[]{:S(2)}) collective-permute-start(bf16[128,2048]{1,0:T(8,128)(2,1)} %get-tuple-element.87), channel_id=1, source_target_pairs={{2,0},{6,4},{11,9},{15,13},{16,18},{20,22},{25,27},{29,31}} | collective-permute-start | bytes 1572872 | tf_op jit(solution)/shard_map/ppermute | solution.py:289
  109.5 18.4 %collective-permute-start.15 = (bf16[128,2048]{1,0:T(8,128)(2,1)}, bf16[128,2048]{1,0:T(8,128)(2,1)S(1)}, u32[]{:S(2)}, u32[]{:S(2)}) collective-permute-start(bf16[128,2048]{1,0:T(8,128)(2,1)} %get-tuple-element.88), channel_id=1, source_target_pairs={{2,0},{6,4},{11,9},{15,13},{16,18},{20,22},{25,27},{29,31}} | collective-permute-start | bytes 1572872 | tf_op jit(solution)/shard_map/ppermute | solution.py:289
  131.1 16.5 %collective-permute-start.22 = (bf16[512,2048]{1,0:T(8,128)(2,1)}, bf16[512,2048]{1,0:T(8,128)(2,1)S(1)}, u32[]{:S(2)}, u32[]{:S(2)}) collective-permute-start(bf16[512,2048]{1,0:T(8,128)(2,1)} %shard_map.207.refs_0_.refs_2_.refs_4_), channel_id=1, source_target_pairs={{0,1},{1,0},{2,3},{3,2},{4,5},{5,4},{6,7},{7,6},{8,9},{9,8},{10,11... | collective-permute-start | bytes 6291464 | tf_op jit(solution)/shard_map/ppermute | solution.py:298
  134.4 24.9 %collective-permute-start.18 = (bf16[128,4096]{1,0:T(8,128)(2,1)S(1)}, bf16[128,4096]{1,0:T(8,128)(2,1)}, u32[]{:S(2)}, u32[]{:S(2)}) collective-permute-start(bf16[128,4096]{1,0:T(8,128)(2,1)S(1)} %collective-permute-done.12.refs_0_.refs_14_), channel_id=1, source_target_pairs={{0,8},{8,16},{16,24},{24,28},{28,20},{20,12},{12,4},{4,0},{1,9},{9... | collective-permute-start | bytes 3145736 | tf_op jit(solution)/shard_map/ppermute | solution.py:360
  135.7 24.6 %collective-permute-start.19 = (bf16[128,4096]{1,0:T(8,128)(2,1)S(1)}, bf16[128,4096]{1,0:T(8,128)(2,1)}, u32[]{:S(2)}, u32[]{:S(2)}) collective-permute-start(bf16[128,4096]{1,0:T(8,128)(2,1)S(1)} %collective-permute-done.13.refs_1_.refs_15_), channel_id=1, source_target_pairs={{8,0},{16,8},{24,16},{28,24},{20,28},{12,20},{4,12},{0,4},{9,1},{1... | collective-permute-start | bytes 3145736 | tf_op jit(solution)/shard_map/ppermute | solution.py:360
  135.9 14.6 %collective-permute-start.20 = (bf16[128,2048]{1,0:T(8,128)(2,1)S(1)}, bf16[128,2048]{1,0:T(8,128)(2,1)S(1)}, u32[]{:S(2)}, u32[]{:S(2)}) collective-permute-start(bf16[128,2048]{1,0:T(8,128)(2,1)S(1)} %shard_map.208), channel_id=1, source_target_pairs={{2,0},{3,1},{6,4},{7,5},{8,10},{10,8},{12,14},{14,12},{17,19},{19,... | collective-permute-start | bytes 1572872 | tf_op jit(solution)/shard_map/ppermute | solution.py:289
  138.0 17.3 %collective-permute-start.21 = (bf16[128,2048]{1,0:T(8,128)(2,1)S(1)}, bf16[128,2048]{1,0:T(8,128)(2,1)S(1)}, u32[]{:S(2)}, u32[]{:S(2)}) collective-permute-start(bf16[128,2048]{1,0:T(8,128)(2,1)S(1)} %shard_map.209), channel_id=1, source_target_pairs={{0,2},{3,1},{4,6},{7,5},{9,11},{10,8},{13,15},{14,12},{17,19},{18,... | collective-permute-start | bytes 1572872 | tf_op jit(solution)/shard_map/ppermute | solution.py:289
  161.4 28.6 %collective-permute-start.23 = (bf16[128,4096]{1,0:T(8,128)(2,1)}, bf16[128,4096]{1,0:T(8,128)(2,1)S(1)}, u32[]{:S(2)}, u32[]{:S(2)}) collective-permute-start(bf16[128,4096]{1,0:T(8,128)(2,1)} %collective-permute-done.18.refs_0_.refs_16_), channel_id=1, source_target_pairs={{0,8},{8,16},{16,24},{24,28},{28,20},{20,12},{12,4},{4,0},{1,9},{9... | collective-permute-start | bytes 3145736 | tf_op jit(solution)/shard_map/ppermute | solution.py:360
  162.6 27.3 %collective-permute-start.24 = (bf16[128,4096]{1,0:T(8,128)(2,1)}, bf16[128,4096]{1,0:T(8,128)(2,1)}, u32[]{:S(2)}, u32[]{:S(2)}) collective-permute-start(bf16[128,4096]{1,0:T(8,128)(2,1)} %collective-permute-done.19.refs_1_.refs_17_), channel_id=1, source_target_pairs={{8,0},{16,8},{24,16},{28,24},{20,28},{12,20},{4,12},{0,4},{9,1},{1... | collective-permute-start | bytes 3145736 | tf_op jit(solution)/shard_map/ppermute | solution.py:360
  162.9 18.8 %collective-permute-start.25 = (bf16[128,2048]{1,0:T(8,128)(2,1)}, bf16[128,2048]{1,0:T(8,128)(2,1)}, u32[]{:S(2)}, u32[]{:S(2)}) collective-permute-start(bf16[128,2048]{1,0:T(8,128)(2,1)} %get-tuple-element.109), channel_id=1, source_target_pairs={{0,2},{1,3},{4,6},{5,7},{8,10},{9,11},{11,9},{12,14},{13,15},{15,1... | collective-permute-start | bytes 1572872 | tf_op jit(solution)/shard_map/ppermute | solution.py:289
  164.2 20.5 %collective-permute-start.26 = (bf16[128,2048]{1,0:T(8,128)(2,1)}, bf16[128,2048]{1,0:T(8,128)(2,1)}, u32[]{:S(2)}, u32[]{:S(2)}) collective-permute-start(bf16[128,2048]{1,0:T(8,128)(2,1)} %get-tuple-element.110), channel_id=1, source_target_pairs={{1,3},{5,7},{8,10},{12,14},{19,17},{23,21},{26,24},{30,28}} | collective-permute-start | bytes 1572872 | tf_op jit(solution)/shard_map/ppermute | solution.py:289
  166.4 23.5 %collective-permute-start.27 = (bf16[128,2048]{1,0:T(8,128)(2,1)}, bf16[128,2048]{1,0:T(8,128)(2,1)}, u32[]{:S(2)}, u32[]{:S(2)}) collective-permute-start(bf16[128,2048]{1,0:T(8,128)(2,1)} %get-tuple-element.111), channel_id=1, source_target_pairs={{1,3},{5,7},{26,24},{30,28}} | collective-permute-start | bytes 1572872 | tf_op jit(solution)/shard_map/ppermute | solution.py:289
  190.0 59.3 %collective-permute-start.30 = (bf16[128,2048]{1,0:T(8,128)(2,1)S(1)}, bf16[128,2048]{1,0:T(8,128)(2,1)}, u32[]{:S(2)}, u32[]{:S(2)}) collective-permute-start(bf16[128,2048]{1,0:T(8,128)(2,1)S(1)} %shard_map.214), channel_id=1, source_target_pairs={{0,2},{1,3},{4,6},{5,7},{9,11},{11,9},{13,15},{15,13},{16,18},{18,... | collective-permute-start | bytes 1572872 | tf_op jit(solution)/shard_map/ppermute | solution.py:289
  202.4 47.0 %collective-permute-start.31 = (bf16[128,2048]{1,0:T(8,128)(2,1)S(1)}, bf16[128,2048]{1,0:T(8,128)(2,1)S(1)}, u32[]{:S(2)}, u32[]{:S(2)}) collective-permute-start(bf16[128,2048]{1,0:T(8,128)(2,1)S(1)} %shard_map.216), channel_id=1, source_target_pairs={{0,2},{3,1},{4,6},{7,5},{9,11},{10,8},{13,15},{14,12},{17,19},{18,... | collective-permute-start | bytes 1572872 | tf_op jit(solution)/shard_map/ppermute | solution.py:289
  207.1 42.3 %collective-permute-start.32 = (bf16[128,2048]{1,0:T(8,128)(2,1)}, bf16[128,2048]{1,0:T(8,128)(2,1)S(1)}, u32[]{:S(2)}, u32[]{:S(2)}) collective-permute-start(bf16[128,2048]{1,0:T(8,128)(2,1)} %get-tuple-element.130), channel_id=1, source_target_pairs={{0,1},{3,0},{4,5},{7,4},{9,10},{11,8},{13,14},{15,12},{16,17},{18,... | collective-permute-start | bytes 1572872 | tf_op jit(solution)/shard_map/ppermute | solution.py:289
  209.1 40.3 %collective-permute-start.33 = (bf16[128,2048]{1,0:T(8,128)(2,1)}, bf16[128,2048]{1,0:T(8,128)(2,1)S(1)}, u32[]{:S(2)}, u32[]{:S(2)}) collective-permute-start(bf16[128,2048]{1,0:T(8,128)(2,1)} %get-tuple-element.131), channel_id=1, source_target_pairs={{2,0},{3,1},{6,4},{7,5},{8,10},{10,8},{12,14},{14,12},{17,19},{19,... | collective-permute-start | bytes 1572872 | tf_op jit(solution)/shard_map/ppermute | solution.py:289
  210.5 39.0 %collective-permute-start.34 = (bf16[128,2048]{1,0:T(8,128)(2,1)}, bf16[128,2048]{1,0:T(8,128)(2,1)}, u32[]{:S(2)}, u32[]{:S(2)}) collective-permute-start(bf16[128,2048]{1,0:T(8,128)(2,1)} %get-tuple-element.132), channel_id=1, source_target_pairs={{1,0},{2,1},{5,4},{6,5},{9,8},{11,10},{13,12},{15,14},{16,19},{18,... | collective-permute-start | bytes 1572872 | tf_op jit(solution)/shard_map/ppermute | solution.py:289
  (36 other events, 583.7 us)

commit v5 on v4

--- a/solution.py
+++ b/solution.py
@@ -13,7 +13,7 @@
 NT = (((1,), (1,)), ((), ()))
 TN = (((0,), (0,)), ((), ()))
 VMEM_BYTES = 60 << 20
-GRAD_IN_VMEM, SUM_VMEM = 50 << 20, 24 << 20
+GRAD_IN_VMEM, SUM_VMEM, LAST_VMEM = 50 << 20, 24 << 20, 46 << 20
 
 
 def snake(n):
@@ -136,6 +136,7 @@
         scalars=(me, order),
         scratch=[pltpu.VMEM((n * half, feats), BF16), pltpu.VMEM((n * half, tile), BF16)],
         aliases={2 + 2 * n + 2 + i: i for i in range(len(old))},
+        vmem=LAST_VMEM if last else VMEM_BYTES,
         flops=2 * n * half * feats * n_cols,
         bytes_accessed=8 * feats * n_cols,
     )(me, jnp.asarray(order.reshape(-1), jnp.int32), *([attn_all] * n), *[x for x, _ in pieces], *wides, *old)
@@ -298,9 +299,8 @@
         other = lax.ppermute(part, "col", cores)
         shifts = range(2, n_col, 2)
         sums = [pair_sum(me, shifted(tables[0], s), part, other, half) for s in shifts]
-        other, sums = yield other, sums
-        for _ in range(hold):
-            yield ()
+        for _ in range(1 + hold):
+            other, sums = yield other, sums
         received = [send(sums[i], tables[1], s) for i, s in enumerate(shifts)]
         for _ in range(late):
             yield ()
@@ -330,7 +330,7 @@
         2: ([1], 2, 0, 0),
         mid - 1: (list(range(2, mid - 1)), 1, 0, 0),
         mid + 1: ([mid - 1, mid], 0, 0, 0),
-        top - 1: (list(range(mid + 1, top - 1)), 0, 0, 0),
+        top - 1: (list(range(mid + 1, top - 1)), 0, 1, 0),
         top: ([top - 1], 0, 0, 0),
     }
     done, moving = [], []

time: 259 us -> 256 us (0.988)
  transfers between devices with their start and end apart: 35 -> 35, of which waited for: 13 -> 13; matrix products, arithmetic and copies ran while one was open for 3% -> 3% of each run, Pallas kernels for 55% -> 54%
where the time goes in v5:
time: 256 us
  Pallas kernels  148 us (58%)
  waiting for transfers between devices  57.5 us (22%)
  starting transfers between devices  38.6 us (15%)
  other arithmetic  6.53 us (3%)
  local copies, waits for them, and re-layouts  4.2 us (2%)
    pallas_call x2, Pallas kernels, token_pass(): call(functools.partial(pass_kernel, n=n, n_grads=n, last=last, n_old=len(...  58.5 us
    pallas_call x6, Pallas kernels, grad_in_part(): call(kernel, (feats // tile,), specs, out, jax.ShapeDtypeStruct((rows, fe...  57.4 us
    ppermute x14, waiting for transfers between devices, body(): nxt = (lax.ppermute(a, 'row', right), lax.ppermute(b, 'row', left))  36.4 us
    ppermute x12, starting transfers between devices, send(): lax.ppermute(x, ('row', 'col'), route(valid, shift, s))  18.4 us
    ppermute x12, waiting for transfers between devices, send(): lax.ppermute(x, ('row', 'col'), route(valid, shift, s))  13.2 us
    pallas_call x2, Pallas kernels, place(): call(kernel, (n,), specs, spec, jax.ShapeDtypeStruct(shape, BF16), scalar...  11.8 us
    pallas_call x6, Pallas kernels, pair_sum(): call(functools.partial(pair_sum_kernel, n=n), (width // tile,), picked, [...  10.7 us
    ppermute x14, starting transfers between devices, body(): nxt = (lax.ppermute(a, 'row', right), lax.ppermute(b, 'row', left))  10.4 us
  transfers between devices with their start and end apart: 35, of which 13 were waited for; matrix products, arithmetic and copies ran while one was open for 3% of the time, Pallas kernels for 54%

profile of v5, /device:TPU:5, one launch (start us, length us, event | category | flops | bytes accessed | tf_op | source)
XLA Modules:
  0.0 255.8 jit_solution(18368233534461384340)
XLA Ops:
  1.4 1.7 fusion
  4.8 8.2 %shard_map.202.refs_0_.refs_2_ = bf16[256,2048]{1,0:T(8,128)(2,1)S(1)} custom-call(bf16[128,4096]{1,0:T(8,128)(2,1)S(1)} %get-tuple-element.160.refs_0_.refs_6_, bf16[128,4096]{1,0:T(8,128)(2,1)S(1)} %get-tuple-element.159.refs_1_.refs_7_, bf16[2048,4096]{1,0:T(8,128)(2,1)} %refs_21_.1), custom_call_target="tpu_custom_call" | custom-call | flops 4294967296 | bytes 19922944 | tf_op jit(solution)/shard_map/pallas_call | solution.py:76
  13.0 15.1 %collective-permute-done.1.refs_1_.refs_9_ = bf16[128,4096]{1,0:T(8,128)(2,1)} collective-permute-done((bf16[128,4096]{1,0:T(8,128)(2,1)S(1)}, bf16[128,4096]{1,0:T(8,128)(2,1)}, u32[]{:S(2)}, u32[]{:S(2)}) %collective-permute-start.1) | collective-permute-done | bytes 1048608 | tf_op jit(solution)/shard_map/ppermute | solution.py:360
  31.5 9.6 %shard_map.203.refs_0_.refs_4_ = bf16[256,2048]{1,0:T(8,128)(2,1)} custom-call(bf16[128,4096]{1,0:T(8,128)(2,1)} %collective-permute-done.refs_0_.refs_8_, bf16[128,4096]{1,0:T(8,128)(2,1)} %collective-permute-done.1.refs_1_.refs_9_, bf16[2048,4096]{1,0:T(8,128)(2,1)} %refs_21_.1), custom_call_target="tpu_custom_call" | custom-call | flops 4294967296 | bytes 19922944 | tf_op jit(solution)/shard_map/pallas_call | solution.py:76
  41.2 2.5 shard_map.204
  43.7 7.9 %collective-permute-done.5 = bf16[512,2048]{1,0:T(8,128)(2,1)} collective-permute-done((bf16[512,2048]{1,0:T(8,128)(2,1)}, bf16[512,2048]{1,0:T(8,128)(2,1)}, u32[]{:S(2)}, u32[]{:S(2)}) %collective-permute-start.5) | collective-permute-done | bytes 2097184 | tf_op jit(solution)/shard_map/ppermute | solution.py:368
  51.6 3.6 %collective-permute-done.3.refs_0_.refs_10_ = bf16[128,4096]{1,0:T(8,128)(2,1)} collective-permute-done((bf16[128,4096]{1,0:T(8,128)(2,1)}, bf16[128,4096]{1,0:T(8,128)(2,1)}, u32[]{:S(2)}, u32[]{:S(2)}) %collective-permute-start.3) | collective-permute-done | bytes 1048608 | tf_op jit(solution)/shard_map/ppermute | solution.py:360
  58.2 8.8 %shard_map.205.refs_0_.refs_7_ = bf16[256,2048]{1,0:T(8,128)(2,1)S(1)} custom-call(bf16[128,4096]{1,0:T(8,128)(2,1)} %collective-permute-done.3.refs_0_.refs_10_, bf16[128,4096]{1,0:T(8,128)(2,1)} %collective-permute-done.4.refs_1_.refs_11_, bf16[2048,4096]{1,0:T(8,128)(2,1)} %refs_21_.1), custom_call_target="tpu_custom_call" | custom-call | flops 4294967296 | bytes 19922944 | tf_op jit(solution)/shard_map/pallas_call | solution.py:76
  67.1 6.5 %pad_maximum_fusion.refs_0_.refs_1_.refs_2_.refs_3_.refs_4_.refs_5_.refs_6_.refs_7_.refs_8_.refs_9_ = bf16[2048,2048]{1,0:T(8,128)(2,1)} fusion(bf16[512,2048]{1,0:T(8,128)(2,1)S(1)} %collective-permute-done.9, bf16[512,2048]{1,0:T(8,128)(2,1)} %collective-permute-done.2, bf16[512,2048]{1,0:T(8,128)(2,1)} %collective-permute-done.5, ...), kind=kLoop, calls=%fused_computation | loop fusion | flops 33554432 | bytes 16777216 | tf_op jit(solution)/shard_map/concatenate | solution.py:373
  73.6 7.7 %collective-permute-done.7.refs_0_.refs_10_ = bf16[128,4096]{1,0:T(8,128)(2,1)} collective-permute-done((bf16[128,4096]{1,0:T(8,128)(2,1)}, bf16[128,4096]{1,0:T(8,128)(2,1)}, u32[]{:S(2)}, u32[]{:S(2)}) %collective-permute-start.7) | collective-permute-done | bytes 1048608 | tf_op jit(solution)/shard_map/ppermute | solution.py:360
  83.8 1.7 collective-permute-start.17
  85.4 21.8 %shard_map.206.refs_20_ = bf16[2048,4096]{1,0:T(8,128)(2,1)} custom-call(s32[1]{0:T(128)} %bitcast._.me.refs_0_, s32[192]{0:T(256)} %constant.42.clone.__, bf16[2048,2048]{1,0:T(8,128)(2,1)} %pad_maximum_fusion.refs_0_.refs_1_.refs_2_.refs_3_.refs_4_.refs_5_.refs_6_.refs_7_.refs_8_.refs_9_, ...), custom_call_target="tpu_custom_call" | custom-call | flops 12884901888 | bytes 67108864 | tf_op jit(solution)/shard_map/pallas_call | solution.py:130
  107.3 1.3 collective-permute-start.12
  108.8 2.6 %shard_map.208 = bf16[128,2048]{1,0:T(8,128)(2,1)S(1)} custom-call(s32[1]{0:T(128)} %bitcast._.me.refs_0_, s32[32]{0:T(128)S(1)} %copy-done.26, bf16[256,2048]{1,0:T(8,128)(2,1)} %shard_map.203.refs_0_.refs_4_, bf16[256,2048]{1,0:T(8,128)(2,1)S(1)} %collective-permute-done.16.refs_1_.refs_5_), custom_call_target="tpu_custom_call" | custom-call | bytes 1572864 | tf_op jit(solution)/shard_map/pallas_call | solution.py:155
  114.0 13.8 %shard_map.207.refs_0_.refs_2_.refs_4_ = bf16[512,2048]{1,0:T(8,128)(2,1)} custom-call(bf16[128,4096]{1,0:T(8,128)(2,1)} %collective-permute-done.7.refs_0_.refs_10_, bf16[128,4096]{1,0:T(8,128)(2,1)} %collective-permute-done.8.refs_1_.refs_11_, bf16[128,4096]{1,0:T(8,128)(2,1)} %collective-permute-done.10.refs_2_.refs_12_, ...), custom_call_target="tpu_custom_call" | custom-call | flops 8589934592 | bytes 23068672 | tf_op jit(solution)/shard_map/pallas_call | solution.py:76
  127.8 2.2 collective-permute-done.12.refs_0_.refs_14_
  131.0 3.4 %collective-permute-start.22 = (bf16[512,2048]{1,0:T(8,128)(2,1)}, bf16[512,2048]{1,0:T(8,128)(2,1)S(1)}, u32[]{:S(2)}, u32[]{:S(2)}) collective-permute-start(bf16[512,2048]{1,0:T(8,128)(2,1)} %shard_map.207.refs_0_.refs_2_.refs_4_), channel_id=1, source_target_pairs={{0,1},{1,0},{2,3},{3,2},{4,5},{5,4},{6,7},{7,6},{8,9},{9,8},{10,11... | collective-permute-start | bytes 6291464 | tf_op jit(solution)/shard_map/ppermute | solution.py:299
  135.9 2.2 collective-permute-start.20
  139.3 8.2 %shard_map.210.refs_0_.refs_9_ = bf16[256,2048]{1,0:T(8,128)(2,1)S(1)} custom-call(bf16[128,4096]{1,0:T(8,128)(2,1)S(1)} %collective-permute-done.12.refs_0_.refs_14_, bf16[128,4096]{1,0:T(8,128)(2,1)S(1)} %collective-permute-done.13.refs_1_.refs_15_, bf16[2048,4096]{1,0:T(8,128)(2,1)} %refs_21_.1), custom_call_target="tpu_custom_call" | custom-call | flops 4294967296 | bytes 19922944 | tf_op jit(solution)/shard_map/pallas_call | solution.py:76
  147.6 2.8 %shard_map.211 = (bf16[128,2048]{1,0:T(8,128)(2,1)}, bf16[128,2048]{1,0:T(8,128)(2,1)}, bf16[128,2048]{1,0:T(8,128)(2,1)S(1)}) custom-call(s32[1]{0:T(128)} %bitcast._.me.refs_0_, s32[96]{0:T(128)S(1)} %copy-done.24, bf16[512,2048]{1,0:T(8,128)(2,1)S(1)} %copy-done, bf16[512,2048]{1,0:T(8,128)(2,1)S(1)} %collective-permute-done.22.refs_1_.refs_3_.refs_5_, ...), custom_call_target="tpu_custom_call" | custom-call | bytes 4718592 | tf_op jit(solution)/shard_map/pallas_call | solution.py:155
  150.4 4.9 %collective-permute-done.21.refs_9_ = bf16[128,2048]{1,0:T(8,128)(2,1)S(1)} collective-permute-done((bf16[128,2048]{1,0:T(8,128)(2,1)S(1)}, bf16[128,2048]{1,0:T(8,128)(2,1)S(1)}, u32[]{:S(2)}, u32[]{:S(2)}) %collective-permute-start.21) | collective-permute-done | bytes 524320 | tf_op jit(solution)/shard_map/ppermute | solution.py:290
  155.3 4.0 %collective-permute-done.18.refs_0_.refs_16_ = bf16[128,4096]{1,0:T(8,128)(2,1)} collective-permute-done((bf16[128,4096]{1,0:T(8,128)(2,1)S(1)}, bf16[128,4096]{1,0:T(8,128)(2,1)}, u32[]{:S(2)}, u32[]{:S(2)}) %collective-permute-start.18) | collective-permute-done | bytes 1048608 | tf_op jit(solution)/shard_map/ppermute | solution.py:360
  167.7 4.0 %shard_map.213.refs_19_ = bf16[512,2048]{1,0:T(8,128)(2,1)} custom-call(s32[1]{0:T(128)} %bitcast._.me.refs_0_, s32[128]{0:T(128)} %constant.47.clone._, s32[128]{0:T(128)} %constant.48.clone.valid, s32[128]{0:T(128)} %constant.49.clone.__, bf16[256,2048]{1,0:T(8,128)(2,1)} %copy-done.2, bf16[256,2048]{1,0:T(8,128)(2,1)} %copy-done.7, ...), custom_call_target="tpu_custom_call" | custom-call | bytes 8388608 | tf_op jit(solution)/shard_map/pallas_call | solution.py:229
  171.8 8.9 %shard_map.212.refs_0_.refs_12_ = bf16[256,2048]{1,0:T(8,128)(2,1)S(1)} custom-call(bf16[128,4096]{1,0:T(8,128)(2,1)} %collective-permute-done.18.refs_0_.refs_16_, bf16[128,4096]{1,0:T(8,128)(2,1)} %collective-permute-done.19.refs_1_.refs_17_, bf16[2048,4096]{1,0:T(8,128)(2,1)} %refs_21_.1), custom_call_target="tpu_custom_call" | custom-call | flops 4294967296 | bytes 19922944 | tf_op jit(solution)/shard_map/pallas_call | solution.py:76
  181.7 2.9 %collective-permute-done.26.refs_7_ = bf16[128,2048]{1,0:T(8,128)(2,1)} collective-permute-done((bf16[128,2048]{1,0:T(8,128)(2,1)}, bf16[128,2048]{1,0:T(8,128)(2,1)}, u32[]{:S(2)}, u32[]{:S(2)}) %collective-permute-start.26) | collective-permute-done | bytes 524320 | tf_op jit(solution)/shard_map/ppermute | solution.py:290
  184.6 5.3 %collective-permute-done.27.refs_8_ = bf16[128,2048]{1,0:T(8,128)(2,1)} collective-permute-done((bf16[128,2048]{1,0:T(8,128)(2,1)S(1)}, bf16[128,2048]{1,0:T(8,128)(2,1)}, u32[]{:S(2)}, u32[]{:S(2)}) %collective-permute-start.27) | collective-permute-done | bytes 524320 | tf_op jit(solution)/shard_map/ppermute | solution.py:290
  190.0 9.1 %shard_map.215 = (bf16[128,2048]{1,0:T(8,128)(2,1)S(1)}, bf16[128,2048]{1,0:T(8,128)(2,1)S(1)}, bf16[128,2048]{1,0:T(8,128)(2,1)S(1)}, bf16[128,2048]{1,0:T(8,128)(2,1)S(1)}) custom-call(s32[1]{0:T(128)} %bitcast._.me.refs_0_, s32[128]{0:T(128)S(1)} %copy-done.21, bf16[128,4096]{1,0:T(8,128)(2,1)S(1)} %collective-permute-done.23.refs_0_.refs_18_, ...), custom_call_target="tpu_custom_call" | custom-call | flops 4294967296 | bytes 19922944 | tf_op jit(solution)/shard_map/pallas_call | solution.py:81
  201.5 4.0 %collective-permute-start.31 = (bf16[128,2048]{1,0:T(8,128)(2,1)S(1)}, bf16[128,2048]{1,0:T(8,128)(2,1)S(1)}, u32[]{:S(2)}, u32[]{:S(2)}) collective-permute-start(bf16[128,2048]{1,0:T(8,128)(2,1)S(1)} %shard_map.216), channel_id=1, source_target_pairs={{0,2},{3,1},{4,6},{7,5},{9,11},{10,8},{13,15},{14,12},{17,19},{18,... | collective-permute-start | bytes 1572872 | tf_op jit(solution)/shard_map/ppermute | solution.py:290
  205.5 2.0 collective-permute-start.32
  207.5 1.3 collective-permute-start.33
  209.8 36.7 %shard_map.217 = (bf16[2048,4096]{1,0:T(8,128)(2,1)}, bf16[2048,4096]{1,0:T(8,128)(2,1)}) custom-call(s32[1]{0:T(128)} %bitcast._.me.refs_0_, s32[320]{0:T(512)S(1)} %copy-done.20, bf16[2048,2048]{1,0:T(8,128)(2,1)} %pad_maximum_fusion.refs_0_.refs_1_.refs_2_.refs_3_.refs_4_.refs_5_.refs_6_.refs_7_.refs_8_.refs_9_, ...), custom_call_target="tpu_custom_call" | custom-call | flops 21474836480 | bytes 67108864 | tf_op jit(solution)/shard_map/pallas_call | solution.py:130
  248.0 7.8 %shard_map.218 = bf16[512,2048]{1,0:T(8,128)(2,1)} custom-call(s32[1]{0:T(128)} %bitcast._.me.refs_0_, s32[192]{0:T(256)} %constant.53.clone.refs_1_, s32[192]{0:T(256)} %constant.54.clone.refs_2_, s32[192]{0:T(256)} %constant.55.clone.refs_3_, bf16[512,2048]{1,0:T(8,128)(2,1)} %shard_map.207.refs_0_.refs_2_.refs_4_, ...), custom_call_target="tpu_custom_call", output_to_operand_aliasing={{}: (19, {})} | custom-call | bytes 12582912 | tf_op jit(solution)/shard_map/pallas_call | solution.py:229
  (133 shorter events, 32.0 us)
Async XLA Ops:
  0.6 28.3 %collective-permute-start.2 = (bf16[512,2048]{1,0:T(8,128)(2,1)}, bf16[512,2048]{1,0:T(8,128)(2,1)}, u32[]{:S(2)}, u32[]{:S(2)}) collective-permute-start(bf16[512,2048]{1,0:T(8,128)(2,1)} %param.19), channel_id=1, source_target_pairs={{0,1},{1,0},{2,3},{3,2},{4,5},{5,4},{6,7},{7,6},{8,9},{9,8},{10,11... | collective-permute-start | bytes 6291464 | tf_op jit(solution)/shard_map/ppermute | solution.py:369
  3.1 24.9 %collective-permute-start.1 = (bf16[128,4096]{1,0:T(8,128)(2,1)S(1)}, bf16[128,4096]{1,0:T(8,128)(2,1)}, u32[]{:S(2)}, u32[]{:S(2)}) collective-permute-start(bf16[128,4096]{1,0:T(8,128)(2,1)S(1)} %get-tuple-element.159.refs_1_.refs_7_), channel_id=1, source_target_pairs={{8,0},{16,8},{24,16},{28,24},{20,28},{12,20},{4,12},{0,4},{9,1},{1... | collective-permute-start | bytes 3145736 | tf_op jit(solution)/shard_map/ppermute | solution.py:360
  4.4 24.6 %collective-permute-start = (bf16[128,4096]{1,0:T(8,128)(2,1)S(1)}, bf16[128,4096]{1,0:T(8,128)(2,1)}, u32[]{:S(2)}, u32[]{:S(2)}) collective-permute-start(bf16[128,4096]{1,0:T(8,128)(2,1)S(1)} %get-tuple-element.160.refs_0_.refs_6_), channel_id=1, source_target_pairs={{0,8},{8,16},{16,24},{24,28},{28,20},{20,12},{12,4},{4,0},{1,9},{9... | collective-permute-start | bytes 3145736 | tf_op jit(solution)/shard_map/ppermute | solution.py:360
  4.6 46.9 %collective-permute-start.5 = (bf16[512,2048]{1,0:T(8,128)(2,1)}, bf16[512,2048]{1,0:T(8,128)(2,1)}, u32[]{:S(2)}, u32[]{:S(2)}) collective-permute-start(bf16[512,2048]{1,0:T(8,128)(2,1)} %param.19), channel_id=1, source_target_pairs={{0,2},{1,3},{2,0},{3,1},{4,6},{5,7},{6,4},{7,5},{8,10},{9,11},{10,... | collective-permute-start | bytes 6291464 | tf_op jit(solution)/shard_map/ppermute | solution.py:368
  28.9 12.2 %collective-permute-start.6 = (bf16[256,2048]{1,0:T(8,128)(2,1)S(1)}, bf16[256,2048]{1,0:T(8,128)(2,1)S(1)}, u32[]{:S(2)}, u32[]{:S(2)}) collective-permute-start(bf16[256,2048]{1,0:T(8,128)(2,1)S(1)} %shard_map.202.refs_0_.refs_2_), channel_id=1, source_target_pairs={{0,1},{1,0},{2,3},{3,2},{4,5},{5,4},{6,7},{7,6},{8,9},{9,8},{10,11... | collective-permute-start | bytes 3145736 | tf_op jit(solution)/shard_map/ppermute | solution.py:299
  30.1 25.1 %collective-permute-start.3 = (bf16[128,4096]{1,0:T(8,128)(2,1)}, bf16[128,4096]{1,0:T(8,128)(2,1)}, u32[]{:S(2)}, u32[]{:S(2)}) collective-permute-start(bf16[128,4096]{1,0:T(8,128)(2,1)} %collective-permute-done.refs_0_.refs_8_), channel_id=1, source_target_pairs={{0,8},{8,16},{16,24},{24,28},{28,20},{20,12},{12,4},{4,0},{1,9},{9... | collective-permute-start | bytes 3145736 | tf_op jit(solution)/shard_map/ppermute | solution.py:360
  30.3 24.9 %collective-permute-start.4 = (bf16[128,4096]{1,0:T(8,128)(2,1)}, bf16[128,4096]{1,0:T(8,128)(2,1)}, u32[]{:S(2)}, u32[]{:S(2)}) collective-permute-start(bf16[128,4096]{1,0:T(8,128)(2,1)} %collective-permute-done.1.refs_1_.refs_9_), channel_id=1, source_target_pairs={{8,0},{16,8},{24,16},{28,24},{20,28},{12,20},{4,12},{0,4},{9,1},{1... | collective-permute-start | bytes 3145736 | tf_op jit(solution)/shard_map/ppermute | solution.py:360
  56.2 25.1 %collective-permute-start.7 = (bf16[128,4096]{1,0:T(8,128)(2,1)}, bf16[128,4096]{1,0:T(8,128)(2,1)}, u32[]{:S(2)}, u32[]{:S(2)}) collective-permute-start(bf16[128,4096]{1,0:T(8,128)(2,1)} %collective-permute-done.3.refs_0_.refs_10_), channel_id=1, source_target_pairs={{0,8},{8,16},{16,24},{24,28},{28,20},{20,12},{12,4},{4,0},{1,9},{9... | collective-permute-start | bytes 3145736 | tf_op jit(solution)/shard_map/ppermute | solution.py:360
  57.5 24.8 %collective-permute-start.8 = (bf16[128,4096]{1,0:T(8,128)(2,1)}, bf16[128,4096]{1,0:T(8,128)(2,1)}, u32[]{:S(2)}, u32[]{:S(2)}) collective-permute-start(bf16[128,4096]{1,0:T(8,128)(2,1)} %collective-permute-done.4.refs_1_.refs_11_), channel_id=1, source_target_pairs={{8,0},{16,8},{24,16},{28,24},{20,28},{12,20},{4,12},{0,4},{9,1},{1... | collective-permute-start | bytes 3145736 | tf_op jit(solution)/shard_map/ppermute | solution.py:360
  57.7 51.1 %collective-permute-start.16 = (bf16[256,2048]{1,0:T(8,128)(2,1)}, bf16[256,2048]{1,0:T(8,128)(2,1)S(1)}, u32[]{:S(2)}, u32[]{:S(2)}) collective-permute-start(bf16[256,2048]{1,0:T(8,128)(2,1)} %shard_map.203.refs_0_.refs_4_), channel_id=1, source_target_pairs={{0,1},{1,0},{2,3},{3,2},{4,5},{5,4},{6,7},{7,6},{8,9},{9,8},{10,11... | collective-permute-start | bytes 3145736 | tf_op jit(solution)/shard_map/ppermute | solution.py:299
  82.3 24.9 %collective-permute-start.10 = (bf16[128,4096]{1,0:T(8,128)(2,1)}, bf16[128,4096]{1,0:T(8,128)(2,1)}, u32[]{:S(2)}, u32[]{:S(2)}) collective-permute-start(bf16[128,4096]{1,0:T(8,128)(2,1)} %collective-permute-done.7.refs_0_.refs_10_), channel_id=1, source_target_pairs={{0,8},{8,16},{16,24},{24,28},{28,20},{20,12},{12,4},{4,0},{1,9},{9... | collective-permute-start | bytes 3145736 | tf_op jit(solution)/shard_map/ppermute | solution.py:360
  83.6 23.6 %collective-permute-start.11 = (bf16[128,4096]{1,0:T(8,128)(2,1)}, bf16[128,4096]{1,0:T(8,128)(2,1)}, u32[]{:S(2)}, u32[]{:S(2)}) collective-permute-start(bf16[128,4096]{1,0:T(8,128)(2,1)} %collective-permute-done.8.refs_1_.refs_11_), channel_id=1, source_target_pairs={{8,0},{16,8},{24,16},{28,24},{20,28},{12,20},{4,12},{0,4},{9,1},{1... | collective-permute-start | bytes 3145736 | tf_op jit(solution)/shard_map/ppermute | solution.py:360
  83.8 29.2 %collective-permute-start.17 = (bf16[256,2048]{1,0:T(8,128)(2,1)S(1)}, bf16[256,2048]{1,0:T(8,128)(2,1)S(1)}, u32[]{:S(2)}, u32[]{:S(2)}) collective-permute-start(bf16[256,2048]{1,0:T(8,128)(2,1)S(1)} %shard_map.205.refs_0_.refs_7_), channel_id=1, source_target_pairs={{0,1},{1,0},{2,3},{3,2},{4,5},{5,4},{6,7},{7,6},{8,9},{9,8},{10,11... | collective-permute-start | bytes 3145736 | tf_op jit(solution)/shard_map/ppermute | solution.py:299
  107.3 22.7 %collective-permute-start.12 = (bf16[128,4096]{1,0:T(8,128)(2,1)}, bf16[128,4096]{1,0:T(8,128)(2,1)S(1)}, u32[]{:S(2)}, u32[]{:S(2)}) collective-permute-start(bf16[128,4096]{1,0:T(8,128)(2,1)} %collective-permute-done.10.refs_2_.refs_12_), channel_id=1, source_target_pairs={{0,8},{8,16},{16,24},{24,28},{28,20},{20,12},{12,4},{4,0},{1,9},{9... | collective-permute-start | bytes 3145736 | tf_op jit(solution)/shard_map/ppermute | solution.py:360
  108.6 22.4 %collective-permute-start.13 = (bf16[128,4096]{1,0:T(8,128)(2,1)}, bf16[128,4096]{1,0:T(8,128)(2,1)S(1)}, u32[]{:S(2)}, u32[]{:S(2)}) collective-permute-start(bf16[128,4096]{1,0:T(8,128)(2,1)} %collective-permute-done.11.refs_3_.refs_13_), channel_id=1, source_target_pairs={{8,0},{16,8},{24,16},{28,24},{20,28},{12,20},{4,12},{0,4},{9,1},{1... | collective-permute-start | bytes 3145736 | tf_op jit(solution)/shard_map/ppermute | solution.py:360
  111.4 16.4 %collective-permute-start.14 = (bf16[128,2048]{1,0:T(8,128)(2,1)}, bf16[128,2048]{1,0:T(8,128)(2,1)S(1)}, u32[]{:S(2)}, u32[]{:S(2)}) collective-permute-start(bf16[128,2048]{1,0:T(8,128)(2,1)} %get-tuple-element.101), channel_id=1, source_target_pairs={{2,0},{6,4},{11,9},{15,13},{16,18},{20,22},{25,27},{29,31}} | collective-permute-start | bytes 1572872 | tf_op jit(solution)/shard_map/ppermute | solution.py:290
  112.1 15.7 %collective-permute-start.15 = (bf16[128,2048]{1,0:T(8,128)(2,1)}, bf16[128,2048]{1,0:T(8,128)(2,1)S(1)}, u32[]{:S(2)}, u32[]{:S(2)}) collective-permute-start(bf16[128,2048]{1,0:T(8,128)(2,1)} %get-tuple-element.102), channel_id=1, source_target_pairs={{2,0},{6,4},{11,9},{15,13},{16,18},{20,22},{25,27},{29,31}} | collective-permute-start | bytes 1572872 | tf_op jit(solution)/shard_map/ppermute | solution.py:290
  131.0 16.6 %collective-permute-start.22 = (bf16[512,2048]{1,0:T(8,128)(2,1)}, bf16[512,2048]{1,0:T(8,128)(2,1)S(1)}, u32[]{:S(2)}, u32[]{:S(2)}) collective-permute-start(bf16[512,2048]{1,0:T(8,128)(2,1)} %shard_map.207.refs_0_.refs_2_.refs_4_), channel_id=1, source_target_pairs={{0,1},{1,0},{2,3},{3,2},{4,5},{5,4},{6,7},{7,6},{8,9},{9,8},{10,11... | collective-permute-start | bytes 6291464 | tf_op jit(solution)/shard_map/ppermute | solution.py:299
  134.4 24.9 %collective-permute-start.18 = (bf16[128,4096]{1,0:T(8,128)(2,1)S(1)}, bf16[128,4096]{1,0:T(8,128)(2,1)}, u32[]{:S(2)}, u32[]{:S(2)}) collective-permute-start(bf16[128,4096]{1,0:T(8,128)(2,1)S(1)} %collective-permute-done.12.refs_0_.refs_14_), channel_id=1, source_target_pairs={{0,8},{8,16},{16,24},{24,28},{28,20},{20,12},{12,4},{4,0},{1,9},{9... | collective-permute-start | bytes 3145736 | tf_op jit(solution)/shard_map/ppermute | solution.py:360
  135.7 24.6 %collective-permute-start.19 = (bf16[128,4096]{1,0:T(8,128)(2,1)S(1)}, bf16[128,4096]{1,0:T(8,128)(2,1)}, u32[]{:S(2)}, u32[]{:S(2)}) collective-permute-start(bf16[128,4096]{1,0:T(8,128)(2,1)S(1)} %collective-permute-done.13.refs_1_.refs_15_), channel_id=1, source_target_pairs={{8,0},{16,8},{24,16},{28,24},{20,28},{12,20},{4,12},{0,4},{9,1},{1... | collective-permute-start | bytes 3145736 | tf_op jit(solution)/shard_map/ppermute | solution.py:360
  135.9 14.6 %collective-permute-start.20 = (bf16[128,2048]{1,0:T(8,128)(2,1)S(1)}, bf16[128,2048]{1,0:T(8,128)(2,1)S(1)}, u32[]{:S(2)}, u32[]{:S(2)}) collective-permute-start(bf16[128,2048]{1,0:T(8,128)(2,1)S(1)} %shard_map.208), channel_id=1, source_target_pairs={{2,0},{3,1},{6,4},{7,5},{8,10},{10,8},{12,14},{14,12},{17,19},{19,... | collective-permute-start | bytes 1572872 | tf_op jit(solution)/shard_map/ppermute | solution.py:290
  138.0 17.3 %collective-permute-start.21 = (bf16[128,2048]{1,0:T(8,128)(2,1)S(1)}, bf16[128,2048]{1,0:T(8,128)(2,1)S(1)}, u32[]{:S(2)}, u32[]{:S(2)}) collective-permute-start(bf16[128,2048]{1,0:T(8,128)(2,1)S(1)} %shard_map.209), channel_id=1, source_target_pairs={{0,2},{3,1},{4,6},{7,5},{9,11},{10,8},{13,15},{14,12},{17,19},{18,... | collective-permute-start | bytes 1572872 | tf_op jit(solution)/shard_map/ppermute | solution.py:290
  161.4 28.6 %collective-permute-start.23 = (bf16[128,4096]{1,0:T(8,128)(2,1)}, bf16[128,4096]{1,0:T(8,128)(2,1)S(1)}, u32[]{:S(2)}, u32[]{:S(2)}) collective-permute-start(bf16[128,4096]{1,0:T(8,128)(2,1)} %collective-permute-done.18.refs_0_.refs_16_), channel_id=1, source_target_pairs={{0,8},{8,16},{16,24},{24,28},{28,20},{20,12},{12,4},{4,0},{1,9},{9... | collective-permute-start | bytes 3145736 | tf_op jit(solution)/shard_map/ppermute | solution.py:360
  162.6 27.3 %collective-permute-start.24 = (bf16[128,4096]{1,0:T(8,128)(2,1)}, bf16[128,4096]{1,0:T(8,128)(2,1)}, u32[]{:S(2)}, u32[]{:S(2)}) collective-permute-start(bf16[128,4096]{1,0:T(8,128)(2,1)} %collective-permute-done.19.refs_1_.refs_17_), channel_id=1, source_target_pairs={{8,0},{16,8},{24,16},{28,24},{20,28},{12,20},{4,12},{0,4},{9,1},{1... | collective-permute-start | bytes 3145736 | tf_op jit(solution)/shard_map/ppermute | solution.py:360
  162.8 18.8 %collective-permute-start.25 = (bf16[128,2048]{1,0:T(8,128)(2,1)}, bf16[128,2048]{1,0:T(8,128)(2,1)}, u32[]{:S(2)}, u32[]{:S(2)}) collective-permute-start(bf16[128,2048]{1,0:T(8,128)(2,1)} %get-tuple-element.123), channel_id=1, source_target_pairs={{0,2},{1,3},{4,6},{5,7},{8,10},{9,11},{11,9},{12,14},{13,15},{15,1... | collective-permute-start | bytes 1572872 | tf_op jit(solution)/shard_map/ppermute | solution.py:290
  164.1 20.5 %collective-permute-start.26 = (bf16[128,2048]{1,0:T(8,128)(2,1)}, bf16[128,2048]{1,0:T(8,128)(2,1)}, u32[]{:S(2)}, u32[]{:S(2)}) collective-permute-start(bf16[128,2048]{1,0:T(8,128)(2,1)} %get-tuple-element.124), channel_id=1, source_target_pairs={{1,3},{5,7},{8,10},{12,14},{19,17},{23,21},{26,24},{30,28}} | collective-permute-start | bytes 1572872 | tf_op jit(solution)/shard_map/ppermute | solution.py:290
  166.4 23.5 %collective-permute-start.27 = (bf16[128,2048]{1,0:T(8,128)(2,1)S(1)}, bf16[128,2048]{1,0:T(8,128)(2,1)}, u32[]{:S(2)}, u32[]{:S(2)}) collective-permute-start(bf16[128,2048]{1,0:T(8,128)(2,1)S(1)} %get-tuple-element.125), channel_id=1, source_target_pairs={{1,3},{5,7},{26,24},{30,28}} | collective-permute-start | bytes 1572872 | tf_op jit(solution)/shard_map/ppermute | solution.py:290
  200.2 46.3 %collective-permute-start.30 = (bf16[128,2048]{1,0:T(8,128)(2,1)S(1)}, bf16[128,2048]{1,0:T(8,128)(2,1)S(1)}, u32[]{:S(2)}, u32[]{:S(2)}) collective-permute-start(bf16[128,2048]{1,0:T(8,128)(2,1)S(1)} %shard_map.214), channel_id=1, source_target_pairs={{0,2},{1,3},{4,6},{5,7},{9,11},{11,9},{13,15},{15,13},{16,18},{18,... | collective-permute-start | bytes 1572872 | tf_op jit(solution)/shard_map/ppermute | solution.py:290
  201.5 45.1 %collective-permute-start.31 = (bf16[128,2048]{1,0:T(8,128)(2,1)S(1)}, bf16[128,2048]{1,0:T(8,128)(2,1)S(1)}, u32[]{:S(2)}, u32[]{:S(2)}) collective-permute-start(bf16[128,2048]{1,0:T(8,128)(2,1)S(1)} %shard_map.216), channel_id=1, source_target_pairs={{0,2},{3,1},{4,6},{7,5},{9,11},{10,8},{13,15},{14,12},{17,19},{18,... | collective-permute-start | bytes 1572872 | tf_op jit(solution)/shard_map/ppermute | solution.py:290
  205.5 41.0 %collective-permute-start.32 = (bf16[128,2048]{1,0:T(8,128)(2,1)S(1)}, bf16[128,2048]{1,0:T(8,128)(2,1)S(1)}, u32[]{:S(2)}, u32[]{:S(2)}) collective-permute-start(bf16[128,2048]{1,0:T(8,128)(2,1)S(1)} %get-tuple-element.146), channel_id=1, source_target_pairs={{0,1},{3,0},{4,5},{7,4},{9,10},{11,8},{13,14},{15,12},{16,17},{18,... | collective-permute-start | bytes 1572872 | tf_op jit(solution)/shard_map/ppermute | solution.py:290
  207.5 39.1 %collective-permute-start.33 = (bf16[128,2048]{1,0:T(8,128)(2,1)S(1)}, bf16[128,2048]{1,0:T(8,128)(2,1)S(1)}, u32[]{:S(2)}, u32[]{:S(2)}) collective-permute-start(bf16[128,2048]{1,0:T(8,128)(2,1)S(1)} %get-tuple-element.147), channel_id=1, source_target_pairs={{2,0},{3,1},{6,4},{7,5},{8,10},{10,8},{12,14},{14,12},{17,19},{19,... | collective-permute-start | bytes 1572872 | tf_op jit(solution)/shard_map/ppermute | solution.py:290
  208.9 37.8 %collective-permute-start.34 = (bf16[128,2048]{1,0:T(8,128)(2,1)S(1)}, bf16[128,2048]{1,0:T(8,128)(2,1)S(1)}, u32[]{:S(2)}, u32[]{:S(2)}) collective-permute-start(bf16[128,2048]{1,0:T(8,128)(2,1)S(1)} %get-tuple-element.148), channel_id=1, source_target_pairs={{1,0},{2,1},{5,4},{6,5},{9,8},{11,10},{13,12},{15,14},{16,19},{18,... | collective-permute-start | bytes 1572872 | tf_op jit(solution)/shard_map/ppermute | solution.py:290
  (41 other events, 703.3 us)

commit v6 on v5

--- a/solution.py
+++ b/solution.py
@@ -136,7 +136,7 @@
         scalars=(me, order),
         scratch=[pltpu.VMEM((n * half, feats), BF16), pltpu.VMEM((n * half, tile), BF16)],
         aliases={2 + 2 * n + 2 + i: i for i in range(len(old))},
-        vmem=LAST_VMEM if last else VMEM_BYTES,
+        vmem=LAST_VMEM,
         flops=2 * n * half * feats * n_cols,
         bytes_accessed=8 * feats * n_cols,
     )(me, jnp.asarray(order.reshape(-1), jnp.int32), *([attn_all] * n), *[x for x, _ in pieces], *wides, *old)

time: 256 us -> 255 us (level)
  Pallas kernels: 148 us -> 143 us
  transfers between devices with their start and end apart: 35 -> 35, of which waited for: 13 -> 14; matrix products, arithmetic and copies ran while one was open for 3% -> 3% of each run, Pallas kernels for 54% -> 53%
where the time goes in v6:
time: 255 us
  Pallas kernels  143 us (56%)
  waiting for transfers between devices  59.2 us (23%)
  starting transfers between devices  38.7 us (15%)
  other arithmetic  7.01 us (3%)
  local copies, waits for them, and re-layouts  5.23 us (2%)
    pallas_call x2, Pallas kernels, token_pass(): call(functools.partial(pass_kernel, n=n, n_grads=n, last=last, n_old=len(...  57.1 us
    pallas_call x6, Pallas kernels, grad_in_part(): call(kernel, (feats // tile,), specs, out, jax.ShapeDtypeStruct((rows, fe...  55.5 us
    ppermute x14, waiting for transfers between devices, body(): nxt = (lax.ppermute(a, 'row', right), lax.ppermute(b, 'row', left))  37.9 us
    ppermute x12, starting transfers between devices, send(): lax.ppermute(x, ('row', 'col'), route(valid, shift, s))  18.4 us
    ppermute x12, waiting for transfers between devices, send(): lax.ppermute(x, ('row', 'col'), route(valid, shift, s))  13.1 us
    pallas_call x2, Pallas kernels, place(): call(kernel, (n,), specs, spec, jax.ShapeDtypeStruct(shape, BF16), scalar...  11.8 us
    ppermute x14, starting transfers between devices, body(): nxt = (lax.ppermute(a, 'row', right), lax.ppermute(b, 'row', left))  10.3 us
    pallas_call x6, Pallas kernels, pair_sum(): call(functools.partial(pair_sum_kernel, n=n), (width // tile,), picked, [...  9.66 us
  transfers between devices with their start and end apart: 35, of which 14 were waited for; matrix products, arithmetic and copies ran while one was open for 3% of the time, Pallas kernels for 53%

profile of v6, /device:TPU:5, one launch (start us, length us, event | category | flops | bytes accessed | tf_op | source)
XLA Modules:
  0.0 254.8 jit_solution(11699029687928921679)
XLA Ops:
  1.4 1.7 fusion
  4.7 8.2 %shard_map.202.refs_0_.refs_2_ = bf16[256,2048]{1,0:T(8,128)(2,1)S(1)} custom-call(bf16[128,4096]{1,0:T(8,128)(2,1)S(1)} %get-tuple-element.160.refs_0_.refs_6_, bf16[128,4096]{1,0:T(8,128)(2,1)S(1)} %get-tuple-element.159.refs_1_.refs_7_, bf16[2048,4096]{1,0:T(8,128)(2,1)} %refs_21_.1), custom_call_target="tpu_custom_call" | custom-call | flops 4294967296 | bytes 19922944 | tf_op jit(solution)/shard_map/pallas_call | solution.py:76
  12.9 15.1 %collective-permute-done.1.refs_1_.refs_9_ = bf16[128,4096]{1,0:T(8,128)(2,1)} collective-permute-done((bf16[128,4096]{1,0:T(8,128)(2,1)S(1)}, bf16[128,4096]{1,0:T(8,128)(2,1)}, u32[]{:S(2)}, u32[]{:S(2)}) %collective-permute-start.1) | collective-permute-done | bytes 1048608 | tf_op jit(solution)/shard_map/ppermute | solution.py:360
  31.5 8.8 %shard_map.203.refs_0_.refs_4_ = bf16[256,2048]{1,0:T(8,128)(2,1)S(1)} custom-call(bf16[128,4096]{1,0:T(8,128)(2,1)} %collective-permute-done.refs_0_.refs_8_, bf16[128,4096]{1,0:T(8,128)(2,1)} %collective-permute-done.1.refs_1_.refs_9_, bf16[2048,4096]{1,0:T(8,128)(2,1)} %refs_21_.1), custom_call_target="tpu_custom_call" | custom-call | flops 4294967296 | bytes 19922944 | tf_op jit(solution)/shard_map/pallas_call | solution.py:76
  40.3 3.0 %shard_map.204 = (bf16[128,2048]{1,0:T(8,128)(2,1)S(1)}, bf16[128,2048]{1,0:T(8,128)(2,1)S(1)}) custom-call(s32[1]{0:T(128)} %bitcast._.me.refs_0_, s32[64]{0:T(128)S(1)} %copy-done.34, bf16[256,2048]{1,0:T(8,128)(2,1)S(1)} %shard_map.202.refs_0_.refs_2_, bf16[256,2048]{1,0:T(8,128)(2,1)} %collective-permute-done.6.refs_1_.refs_3_, ...), custom_call_target="tpu_custom_call" | custom-call | bytes 3145728 | tf_op jit(solution)/shard_map/pallas_call | solution.py:155
  43.4 8.2 %collective-permute-done.5 = bf16[512,2048]{1,0:T(8,128)(2,1)} collective-permute-done((bf16[512,2048]{1,0:T(8,128)(2,1)}, bf16[512,2048]{1,0:T(8,128)(2,1)}, u32[]{:S(2)}, u32[]{:S(2)}) %collective-permute-start.5) | collective-permute-done | bytes 2097184 | tf_op jit(solution)/shard_map/ppermute | solution.py:368
  51.5 3.6 %collective-permute-done.3.refs_0_.refs_10_ = bf16[128,4096]{1,0:T(8,128)(2,1)} collective-permute-done((bf16[128,4096]{1,0:T(8,128)(2,1)}, bf16[128,4096]{1,0:T(8,128)(2,1)}, u32[]{:S(2)}, u32[]{:S(2)}) %collective-permute-start.3) | collective-permute-done | bytes 1048608 | tf_op jit(solution)/shard_map/ppermute | solution.py:360
  58.2 8.8 %shard_map.205.refs_0_.refs_7_ = bf16[256,2048]{1,0:T(8,128)(2,1)S(1)} custom-call(bf16[128,4096]{1,0:T(8,128)(2,1)} %collective-permute-done.3.refs_0_.refs_10_, bf16[128,4096]{1,0:T(8,128)(2,1)} %collective-permute-done.4.refs_1_.refs_11_, bf16[2048,4096]{1,0:T(8,128)(2,1)} %refs_21_.1), custom_call_target="tpu_custom_call" | custom-call | flops 4294967296 | bytes 19922944 | tf_op jit(solution)/shard_map/pallas_call | solution.py:76
  67.1 7.0 %pad_maximum_fusion.refs_0_.refs_1_.refs_2_.refs_3_.refs_4_.refs_5_.refs_6_.refs_7_.refs_8_.refs_9_ = bf16[2048,2048]{1,0:T(8,128)(2,1)} fusion(bf16[512,2048]{1,0:T(8,128)(2,1)} %collective-permute-done.9, bf16[512,2048]{1,0:T(8,128)(2,1)} %collective-permute-done.2, bf16[512,2048]{1,0:T(8,128)(2,1)} %collective-permute-done.5, bf16[512,2048]{1,0:T(8,128)(2,1)S(1)} %copy-done.35), kind=kLoop, calls=%fused_computation | loop fusion | flops 33554432 | bytes 16777216 | tf_op jit(solution)/shard_map/concatenate | solution.py:373
  74.1 7.1 %collective-permute-done.7.refs_0_.refs_10_ = bf16[128,4096]{1,0:T(8,128)(2,1)S(1)} collective-permute-done((bf16[128,4096]{1,0:T(8,128)(2,1)}, bf16[128,4096]{1,0:T(8,128)(2,1)S(1)}, u32[]{:S(2)}, u32[]{:S(2)}) %collective-permute-start.7) | collective-permute-done | bytes 1048608 | tf_op jit(solution)/shard_map/ppermute | solution.py:360
  82.2 1.3 collective-permute-start.10
  83.6 1.7 collective-permute-start.17
  85.3 20.9 %shard_map.206.refs_20_ = bf16[2048,4096]{1,0:T(8,128)(2,1)} custom-call(s32[1]{0:T(128)} %bitcast._.me.refs_0_, s32[192]{0:T(256)S(1)} %copy-done.27, bf16[2048,2048]{1,0:T(8,128)(2,1)} %pad_maximum_fusion.refs_0_.refs_1_.refs_2_.refs_3_.refs_4_.refs_5_.refs_6_.refs_7_.refs_8_.refs_9_, ...), custom_call_target="tpu_custom_call" | custom-call | flops 12884901888 | bytes 67108864 | tf_op jit(solution)/shard_map/pallas_call | solution.py:130
  112.9 12.8 %shard_map.207.refs_0_.refs_2_.refs_4_ = bf16[512,2048]{1,0:T(8,128)(2,1)} custom-call(bf16[128,4096]{1,0:T(8,128)(2,1)S(1)} %collective-permute-done.7.refs_0_.refs_10_, bf16[128,4096]{1,0:T(8,128)(2,1)S(1)} %collective-permute-done.8.refs_1_.refs_11_, bf16[128,4096]{1,0:T(8,128)(2,1)S(1)} %collective-permute-done.10.refs_2_.refs_12_, ...), custom_call_target="tpu_custom_call" | custom-call | flops 8589934592 | bytes 23068672 | tf_op jit(solution)/shard_map/pallas_call | solution.py:76
  125.7 3.5 %collective-permute-done.12.refs_0_.refs_14_ = bf16[128,4096]{1,0:T(8,128)(2,1)S(1)} collective-permute-done((bf16[128,4096]{1,0:T(8,128)(2,1)S(1)}, bf16[128,4096]{1,0:T(8,128)(2,1)S(1)}, u32[]{:S(2)}, u32[]{:S(2)}) %collective-permute-start.12) | collective-permute-done | bytes 1048608 | tf_op jit(solution)/shard_map/ppermute | solution.py:360
  130.4 3.5 %collective-permute-start.22 = (bf16[512,2048]{1,0:T(8,128)(2,1)}, bf16[512,2048]{1,0:T(8,128)(2,1)S(1)}, u32[]{:S(2)}, u32[]{:S(2)}) collective-permute-start(bf16[512,2048]{1,0:T(8,128)(2,1)} %shard_map.207.refs_0_.refs_2_.refs_4_), channel_id=1, source_target_pairs={{0,1},{1,0},{2,3},{3,2},{4,5},{5,4},{6,7},{7,6},{8,9},{9,8},{10,11... | collective-permute-start | bytes 6291464 | tf_op jit(solution)/shard_map/ppermute | solution.py:299
  135.4 2.2 collective-permute-start.20
  137.6 1.3 collective-permute-start.21
  138.9 8.2 %shard_map.210.refs_0_.refs_9_ = bf16[256,2048]{1,0:T(8,128)(2,1)S(1)} custom-call(bf16[128,4096]{1,0:T(8,128)(2,1)S(1)} %collective-permute-done.12.refs_0_.refs_14_, bf16[128,4096]{1,0:T(8,128)(2,1)S(1)} %collective-permute-done.13.refs_1_.refs_15_, bf16[2048,4096]{1,0:T(8,128)(2,1)} %refs_21_.1), custom_call_target="tpu_custom_call" | custom-call | flops 4294967296 | bytes 19922944 | tf_op jit(solution)/shard_map/pallas_call | solution.py:76
  147.2 2.8 %shard_map.211 = (bf16[128,2048]{1,0:T(8,128)(2,1)}, bf16[128,2048]{1,0:T(8,128)(2,1)}, bf16[128,2048]{1,0:T(8,128)(2,1)S(1)}) custom-call(s32[1]{0:T(128)} %bitcast._.me.refs_0_, s32[96]{0:T(128)S(1)} %copy-done.31, bf16[512,2048]{1,0:T(8,128)(2,1)S(1)} %copy-done, bf16[512,2048]{1,0:T(8,128)(2,1)S(1)} %collective-permute-done.22.refs_1_.refs_3_.refs_5_, ...), custom_call_target="tpu_custom_call" | custom-call | bytes 4718592 | tf_op jit(solution)/shard_map/pallas_call | solution.py:155
  150.0 4.9 %collective-permute-done.21.refs_9_ = bf16[128,2048]{1,0:T(8,128)(2,1)S(1)} collective-permute-done((bf16[128,2048]{1,0:T(8,128)(2,1)S(1)}, bf16[128,2048]{1,0:T(8,128)(2,1)S(1)}, u32[]{:S(2)}, u32[]{:S(2)}) %collective-permute-start.21) | collective-permute-done | bytes 524320 | tf_op jit(solution)/shard_map/ppermute | solution.py:290
  154.9 4.0 %collective-permute-done.18.refs_0_.refs_16_ = bf16[128,4096]{1,0:T(8,128)(2,1)} collective-permute-done((bf16[128,4096]{1,0:T(8,128)(2,1)S(1)}, bf16[128,4096]{1,0:T(8,128)(2,1)}, u32[]{:S(2)}, u32[]{:S(2)}) %collective-permute-start.18) | collective-permute-done | bytes 1048608 | tf_op jit(solution)/shard_map/ppermute | solution.py:360
  167.2 4.0 %shard_map.213.refs_19_ = bf16[512,2048]{1,0:T(8,128)(2,1)} custom-call(s32[1]{0:T(128)} %bitcast._.me.refs_0_, s32[128]{0:T(128)} %constant.47.clone._, s32[128]{0:T(128)} %constant.48.clone.valid, s32[128]{0:T(128)} %constant.49.clone.__, bf16[256,2048]{1,0:T(8,128)(2,1)} %copy-done.2, bf16[256,2048]{1,0:T(8,128)(2,1)} %collective-permute-done.6.refs_1_.refs_3_, ...), custom_call_target="tpu_custom_call" | custom-call | bytes 8388608 | tf_op jit(solution)/shard_map/pallas_call | solution.py:229
  171.2 8.9 %shard_map.212.refs_0_.refs_12_ = bf16[256,2048]{1,0:T(8,128)(2,1)S(1)} custom-call(bf16[128,4096]{1,0:T(8,128)(2,1)} %collective-permute-done.18.refs_0_.refs_16_, bf16[128,4096]{1,0:T(8,128)(2,1)} %collective-permute-done.19.refs_1_.refs_17_, bf16[2048,4096]{1,0:T(8,128)(2,1)} %refs_21_.1), custom_call_target="tpu_custom_call" | custom-call | flops 4294967296 | bytes 19922944 | tf_op jit(solution)/shard_map/pallas_call | solution.py:76
  181.2 2.9 %collective-permute-done.26.refs_7_ = bf16[128,2048]{1,0:T(8,128)(2,1)} collective-permute-done((bf16[128,2048]{1,0:T(8,128)(2,1)}, bf16[128,2048]{1,0:T(8,128)(2,1)}, u32[]{:S(2)}, u32[]{:S(2)}) %collective-permute-start.26) | collective-permute-done | bytes 524320 | tf_op jit(solution)/shard_map/ppermute | solution.py:290
  184.1 5.3 %collective-permute-done.27.refs_8_ = bf16[128,2048]{1,0:T(8,128)(2,1)} collective-permute-done((bf16[128,2048]{1,0:T(8,128)(2,1)S(1)}, bf16[128,2048]{1,0:T(8,128)(2,1)}, u32[]{:S(2)}, u32[]{:S(2)}) %collective-permute-start.27) | collective-permute-done | bytes 524320 | tf_op jit(solution)/shard_map/ppermute | solution.py:290
  189.5 9.1 %shard_map.215 = (bf16[128,2048]{1,0:T(8,128)(2,1)S(1)}, bf16[128,2048]{1,0:T(8,128)(2,1)S(1)}, bf16[128,2048]{1,0:T(8,128)(2,1)S(1)}, bf16[128,2048]{1,0:T(8,128)(2,1)S(1)}) custom-call(s32[1]{0:T(128)} %bitcast._.me.refs_0_, s32[128]{0:T(128)S(1)} %copy-done.28, bf16[128,4096]{1,0:T(8,128)(2,1)S(1)} %collective-permute-done.23.refs_0_.refs_18_, ...), custom_call_target="tpu_custom_call" | custom-call | flops 4294967296 | bytes 19922944 | tf_op jit(solution)/shard_map/pallas_call | solution.py:81
  201.0 4.0 %collective-permute-start.31 = (bf16[128,2048]{1,0:T(8,128)(2,1)S(1)}, bf16[128,2048]{1,0:T(8,128)(2,1)S(1)}, u32[]{:S(2)}, u32[]{:S(2)}) collective-permute-start(bf16[128,2048]{1,0:T(8,128)(2,1)S(1)} %shard_map.216), channel_id=1, source_target_pairs={{0,2},{3,1},{4,6},{7,5},{9,11},{10,8},{13,15},{14,12},{17,19},{18,... | collective-permute-start | bytes 1572872 | tf_op jit(solution)/shard_map/ppermute | solution.py:290
  205.0 2.0 collective-permute-start.32
  207.0 1.3 collective-permute-start.33
  209.3 36.2 %shard_map.217 = (bf16[2048,4096]{1,0:T(8,128)(2,1)}, bf16[2048,4096]{1,0:T(8,128)(2,1)}) custom-call(s32[1]{0:T(128)} %bitcast._.me.refs_0_, s32[320]{0:T(512)S(1)} %copy-done.26, bf16[2048,2048]{1,0:T(8,128)(2,1)} %pad_maximum_fusion.refs_0_.refs_1_.refs_2_.refs_3_.refs_4_.refs_5_.refs_6_.refs_7_.refs_8_.refs_9_, ...), custom_call_target="tpu_custom_call" | custom-call | flops 21474836480 | bytes 67108864 | tf_op jit(solution)/shard_map/pallas_call | solution.py:130
  247.0 7.8 %shard_map.218 = bf16[512,2048]{1,0:T(8,128)(2,1)} custom-call(s32[1]{0:T(128)} %bitcast._.me.refs_0_, s32[192]{0:T(256)} %constant.53.clone.refs_1_, s32[192]{0:T(256)} %constant.54.clone.refs_2_, s32[192]{0:T(256)} %constant.55.clone.refs_3_, bf16[512,2048]{1,0:T(8,128)(2,1)} %shard_map.207.refs_0_.refs_2_.refs_4_, ...), custom_call_target="tpu_custom_call", output_to_operand_aliasing={{}: (19, {})} | custom-call | bytes 12582912 | tf_op jit(solution)/shard_map/pallas_call | solution.py:229
  (147 shorter events, 33.4 us)
Async XLA Ops:
  0.6 28.3 %collective-permute-start.2 = (bf16[512,2048]{1,0:T(8,128)(2,1)}, bf16[512,2048]{1,0:T(8,128)(2,1)}, u32[]{:S(2)}, u32[]{:S(2)}) collective-permute-start(bf16[512,2048]{1,0:T(8,128)(2,1)} %param.19), channel_id=1, source_target_pairs={{0,1},{1,0},{2,3},{3,2},{4,5},{5,4},{6,7},{7,6},{8,9},{9,8},{10,11... | collective-permute-start | bytes 6291464 | tf_op jit(solution)/shard_map/ppermute | solution.py:369
  3.1 24.9 %collective-permute-start.1 = (bf16[128,4096]{1,0:T(8,128)(2,1)S(1)}, bf16[128,4096]{1,0:T(8,128)(2,1)}, u32[]{:S(2)}, u32[]{:S(2)}) collective-permute-start(bf16[128,4096]{1,0:T(8,128)(2,1)S(1)} %get-tuple-element.159.refs_1_.refs_7_), channel_id=1, source_target_pairs={{8,0},{16,8},{24,16},{28,24},{20,28},{12,20},{4,12},{0,4},{9,1},{1... | collective-permute-start | bytes 3145736 | tf_op jit(solution)/shard_map/ppermute | solution.py:360
  4.4 24.6 %collective-permute-start = (bf16[128,4096]{1,0:T(8,128)(2,1)S(1)}, bf16[128,4096]{1,0:T(8,128)(2,1)}, u32[]{:S(2)}, u32[]{:S(2)}) collective-permute-start(bf16[128,4096]{1,0:T(8,128)(2,1)S(1)} %get-tuple-element.160.refs_0_.refs_6_), channel_id=1, source_target_pairs={{0,8},{8,16},{16,24},{24,28},{28,20},{20,12},{12,4},{4,0},{1,9},{9... | collective-permute-start | bytes 3145736 | tf_op jit(solution)/shard_map/ppermute | solution.py:360
  4.6 46.9 %collective-permute-start.5 = (bf16[512,2048]{1,0:T(8,128)(2,1)}, bf16[512,2048]{1,0:T(8,128)(2,1)}, u32[]{:S(2)}, u32[]{:S(2)}) collective-permute-start(bf16[512,2048]{1,0:T(8,128)(2,1)} %param.19), channel_id=1, source_target_pairs={{0,2},{1,3},{2,0},{3,1},{4,6},{5,7},{6,4},{7,5},{8,10},{9,11},{10,... | collective-permute-start | bytes 6291464 | tf_op jit(solution)/shard_map/ppermute | solution.py:368
  30.1 25.1 %collective-permute-start.3 = (bf16[128,4096]{1,0:T(8,128)(2,1)}, bf16[128,4096]{1,0:T(8,128)(2,1)}, u32[]{:S(2)}, u32[]{:S(2)}) collective-permute-start(bf16[128,4096]{1,0:T(8,128)(2,1)} %collective-permute-done.refs_0_.refs_8_), channel_id=1, source_target_pairs={{0,8},{8,16},{16,24},{24,28},{28,20},{20,12},{12,4},{4,0},{1,9},{9... | collective-permute-start | bytes 3145736 | tf_op jit(solution)/shard_map/ppermute | solution.py:360
  30.3 24.9 %collective-permute-start.4 = (bf16[128,4096]{1,0:T(8,128)(2,1)}, bf16[128,4096]{1,0:T(8,128)(2,1)}, u32[]{:S(2)}, u32[]{:S(2)}) collective-permute-start(bf16[128,4096]{1,0:T(8,128)(2,1)} %collective-permute-done.1.refs_1_.refs_9_), channel_id=1, source_target_pairs={{8,0},{16,8},{24,16},{28,24},{20,28},{12,20},{4,12},{0,4},{9,1},{1... | collective-permute-start | bytes 3145736 | tf_op jit(solution)/shard_map/ppermute | solution.py:360
  55.2 11.9 %collective-permute-start.9 = (bf16[512,2048]{1,0:T(8,128)(2,1)}, bf16[512,2048]{1,0:T(8,128)(2,1)}, u32[]{:S(2)}, u32[]{:S(2)}) collective-permute-start(bf16[512,2048]{1,0:T(8,128)(2,1)} %collective-permute-done.5), channel_id=1, source_target_pairs={{0,1},{1,0},{2,3},{3,2},{4,5},{5,4},{6,7},{7,6},{8,9},{9,8},{10,11... | collective-permute-start | bytes 6291464 | tf_op jit(solution)/shard_map/ppermute | solution.py:373
  56.2 25.0 %collective-permute-start.7 = (bf16[128,4096]{1,0:T(8,128)(2,1)}, bf16[128,4096]{1,0:T(8,128)(2,1)S(1)}, u32[]{:S(2)}, u32[]{:S(2)}) collective-permute-start(bf16[128,4096]{1,0:T(8,128)(2,1)} %collective-permute-done.3.refs_0_.refs_10_), channel_id=1, source_target_pairs={{0,8},{8,16},{16,24},{24,28},{28,20},{20,12},{12,4},{4,0},{1,9},{9... | collective-permute-start | bytes 3145736 | tf_op jit(solution)/shard_map/ppermute | solution.py:360
  57.5 24.7 %collective-permute-start.8 = (bf16[128,4096]{1,0:T(8,128)(2,1)}, bf16[128,4096]{1,0:T(8,128)(2,1)S(1)}, u32[]{:S(2)}, u32[]{:S(2)}) collective-permute-start(bf16[128,4096]{1,0:T(8,128)(2,1)} %collective-permute-done.4.refs_1_.refs_11_), channel_id=1, source_target_pairs={{8,0},{16,8},{24,16},{28,24},{20,28},{12,20},{4,12},{0,4},{9,1},{1... | collective-permute-start | bytes 3145736 | tf_op jit(solution)/shard_map/ppermute | solution.py:360
  57.7 50.7 %collective-permute-start.16 = (bf16[256,2048]{1,0:T(8,128)(2,1)S(1)}, bf16[256,2048]{1,0:T(8,128)(2,1)S(1)}, u32[]{:S(2)}, u32[]{:S(2)}) collective-permute-start(bf16[256,2048]{1,0:T(8,128)(2,1)S(1)} %shard_map.203.refs_0_.refs_4_), channel_id=1, source_target_pairs={{0,1},{1,0},{2,3},{3,2},{4,5},{5,4},{6,7},{7,6},{8,9},{9,8},{10,11... | collective-permute-start | bytes 3145736 | tf_op jit(solution)/shard_map/ppermute | solution.py:299
  82.2 24.0 %collective-permute-start.10 = (bf16[128,4096]{1,0:T(8,128)(2,1)S(1)}, bf16[128,4096]{1,0:T(8,128)(2,1)S(1)}, u32[]{:S(2)}, u32[]{:S(2)}) collective-permute-start(bf16[128,4096]{1,0:T(8,128)(2,1)S(1)} %collective-permute-done.7.refs_0_.refs_10_), channel_id=1, source_target_pairs={{0,8},{8,16},{16,24},{24,28},{28,20},{20,12},{12,4},{4,0},{1,9},{9... | collective-permute-start | bytes 3145736 | tf_op jit(solution)/shard_map/ppermute | solution.py:360
  83.5 23.4 %collective-permute-start.11 = (bf16[128,4096]{1,0:T(8,128)(2,1)S(1)}, bf16[128,4096]{1,0:T(8,128)(2,1)}, u32[]{:S(2)}, u32[]{:S(2)}) collective-permute-start(bf16[128,4096]{1,0:T(8,128)(2,1)S(1)} %collective-permute-done.8.refs_1_.refs_11_), channel_id=1, source_target_pairs={{8,0},{16,8},{24,16},{28,24},{20,28},{12,20},{4,12},{0,4},{9,1},{1... | collective-permute-start | bytes 3145736 | tf_op jit(solution)/shard_map/ppermute | solution.py:360
  83.6 27.2 %collective-permute-start.17 = (bf16[256,2048]{1,0:T(8,128)(2,1)S(1)}, bf16[256,2048]{1,0:T(8,128)(2,1)S(1)}, u32[]{:S(2)}, u32[]{:S(2)}) collective-permute-start(bf16[256,2048]{1,0:T(8,128)(2,1)S(1)} %shard_map.205.refs_0_.refs_7_), channel_id=1, source_target_pairs={{0,1},{1,0},{2,3},{3,2},{4,5},{5,4},{6,7},{7,6},{8,9},{9,8},{10,11... | collective-permute-start | bytes 3145736 | tf_op jit(solution)/shard_map/ppermute | solution.py:299
  106.9 22.3 %collective-permute-start.12 = (bf16[128,4096]{1,0:T(8,128)(2,1)S(1)}, bf16[128,4096]{1,0:T(8,128)(2,1)S(1)}, u32[]{:S(2)}, u32[]{:S(2)}) collective-permute-start(bf16[128,4096]{1,0:T(8,128)(2,1)S(1)} %collective-permute-done.10.refs_2_.refs_12_), channel_id=1, source_target_pairs={{0,8},{8,16},{16,24},{24,28},{28,20},{20,12},{12,4},{4,0},{1,9},{9... | collective-permute-start | bytes 3145736 | tf_op jit(solution)/shard_map/ppermute | solution.py:360
  108.2 22.3 %collective-permute-start.13 = (bf16[128,4096]{1,0:T(8,128)(2,1)}, bf16[128,4096]{1,0:T(8,128)(2,1)S(1)}, u32[]{:S(2)}, u32[]{:S(2)}) collective-permute-start(bf16[128,4096]{1,0:T(8,128)(2,1)} %collective-permute-done.11.refs_3_.refs_13_), channel_id=1, source_target_pairs={{8,0},{16,8},{24,16},{28,24},{20,28},{12,20},{4,12},{0,4},{9,1},{1... | collective-permute-start | bytes 3145736 | tf_op jit(solution)/shard_map/ppermute | solution.py:360
  109.3 16.4 %collective-permute-start.14 = (bf16[128,2048]{1,0:T(8,128)(2,1)S(1)}, bf16[128,2048]{1,0:T(8,128)(2,1)S(1)}, u32[]{:S(2)}, u32[]{:S(2)}) collective-permute-start(bf16[128,2048]{1,0:T(8,128)(2,1)S(1)} %get-tuple-element.101), channel_id=1, source_target_pairs={{2,0},{6,4},{11,9},{15,13},{16,18},{20,22},{25,27},{29,31}} | collective-permute-start | bytes 1572872 | tf_op jit(solution)/shard_map/ppermute | solution.py:290
  110.0 15.7 %collective-permute-start.15 = (bf16[128,2048]{1,0:T(8,128)(2,1)S(1)}, bf16[128,2048]{1,0:T(8,128)(2,1)S(1)}, u32[]{:S(2)}, u32[]{:S(2)}) collective-permute-start(bf16[128,2048]{1,0:T(8,128)(2,1)S(1)} %get-tuple-element.102), channel_id=1, source_target_pairs={{2,0},{6,4},{11,9},{15,13},{16,18},{20,22},{25,27},{29,31}} | collective-permute-start | bytes 1572872 | tf_op jit(solution)/shard_map/ppermute | solution.py:290
  130.4 16.7 %collective-permute-start.22 = (bf16[512,2048]{1,0:T(8,128)(2,1)}, bf16[512,2048]{1,0:T(8,128)(2,1)S(1)}, u32[]{:S(2)}, u32[]{:S(2)}) collective-permute-start(bf16[512,2048]{1,0:T(8,128)(2,1)} %shard_map.207.refs_0_.refs_2_.refs_4_), channel_id=1, source_target_pairs={{0,1},{1,0},{2,3},{3,2},{4,5},{5,4},{6,7},{7,6},{8,9},{9,8},{10,11... | collective-permute-start | bytes 6291464 | tf_op jit(solution)/shard_map/ppermute | solution.py:299
  133.9 24.9 %collective-permute-start.18 = (bf16[128,4096]{1,0:T(8,128)(2,1)S(1)}, bf16[128,4096]{1,0:T(8,128)(2,1)}, u32[]{:S(2)}, u32[]{:S(2)}) collective-permute-start(bf16[128,4096]{1,0:T(8,128)(2,1)S(1)} %collective-permute-done.12.refs_0_.refs_14_), channel_id=1, source_target_pairs={{0,8},{8,16},{16,24},{24,28},{28,20},{20,12},{12,4},{4,0},{1,9},{9... | collective-permute-start | bytes 3145736 | tf_op jit(solution)/shard_map/ppermute | solution.py:360
  135.2 24.6 %collective-permute-start.19 = (bf16[128,4096]{1,0:T(8,128)(2,1)S(1)}, bf16[128,4096]{1,0:T(8,128)(2,1)}, u32[]{:S(2)}, u32[]{:S(2)}) collective-permute-start(bf16[128,4096]{1,0:T(8,128)(2,1)S(1)} %collective-permute-done.13.refs_1_.refs_15_), channel_id=1, source_target_pairs={{8,0},{16,8},{24,16},{28,24},{20,28},{12,20},{4,12},{0,4},{9,1},{1... | collective-permute-start | bytes 3145736 | tf_op jit(solution)/shard_map/ppermute | solution.py:360
  135.4 14.6 %collective-permute-start.20 = (bf16[128,2048]{1,0:T(8,128)(2,1)S(1)}, bf16[128,2048]{1,0:T(8,128)(2,1)S(1)}, u32[]{:S(2)}, u32[]{:S(2)}) collective-permute-start(bf16[128,2048]{1,0:T(8,128)(2,1)S(1)} %shard_map.208), channel_id=1, source_target_pairs={{2,0},{3,1},{6,4},{7,5},{8,10},{10,8},{12,14},{14,12},{17,19},{19,... | collective-permute-start | bytes 1572872 | tf_op jit(solution)/shard_map/ppermute | solution.py:290
  137.6 17.3 %collective-permute-start.21 = (bf16[128,2048]{1,0:T(8,128)(2,1)S(1)}, bf16[128,2048]{1,0:T(8,128)(2,1)S(1)}, u32[]{:S(2)}, u32[]{:S(2)}) collective-permute-start(bf16[128,2048]{1,0:T(8,128)(2,1)S(1)} %shard_map.209), channel_id=1, source_target_pairs={{0,2},{3,1},{4,6},{7,5},{9,11},{10,8},{13,15},{14,12},{17,19},{18,... | collective-permute-start | bytes 1572872 | tf_op jit(solution)/shard_map/ppermute | solution.py:290
  160.8 28.6 %collective-permute-start.23 = (bf16[128,4096]{1,0:T(8,128)(2,1)}, bf16[128,4096]{1,0:T(8,128)(2,1)S(1)}, u32[]{:S(2)}, u32[]{:S(2)}) collective-permute-start(bf16[128,4096]{1,0:T(8,128)(2,1)} %collective-permute-done.18.refs_0_.refs_16_), channel_id=1, source_target_pairs={{0,8},{8,16},{16,24},{24,28},{28,20},{20,12},{12,4},{4,0},{1,9},{9... | collective-permute-start | bytes 3145736 | tf_op jit(solution)/shard_map/ppermute | solution.py:360
  161.6 27.8 %collective-permute-start.24 = (bf16[128,4096]{1,0:T(8,128)(2,1)}, bf16[128,4096]{1,0:T(8,128)(2,1)}, u32[]{:S(2)}, u32[]{:S(2)}) collective-permute-start(bf16[128,4096]{1,0:T(8,128)(2,1)} %collective-permute-done.19.refs_1_.refs_17_), channel_id=1, source_target_pairs={{8,0},{16,8},{24,16},{28,24},{20,28},{12,20},{4,12},{0,4},{9,1},{1... | collective-permute-start | bytes 3145736 | tf_op jit(solution)/shard_map/ppermute | solution.py:360
  162.3 18.9 %collective-permute-start.25 = (bf16[128,2048]{1,0:T(8,128)(2,1)}, bf16[128,2048]{1,0:T(8,128)(2,1)}, u32[]{:S(2)}, u32[]{:S(2)}) collective-permute-start(bf16[128,2048]{1,0:T(8,128)(2,1)} %get-tuple-element.123), channel_id=1, source_target_pairs={{0,2},{1,3},{4,6},{5,7},{8,10},{9,11},{11,9},{12,14},{13,15},{15,1... | collective-permute-start | bytes 1572872 | tf_op jit(solution)/shard_map/ppermute | solution.py:290
  163.6 20.5 %collective-permute-start.26 = (bf16[128,2048]{1,0:T(8,128)(2,1)}, bf16[128,2048]{1,0:T(8,128)(2,1)}, u32[]{:S(2)}, u32[]{:S(2)}) collective-permute-start(bf16[128,2048]{1,0:T(8,128)(2,1)} %get-tuple-element.124), channel_id=1, source_target_pairs={{1,3},{5,7},{8,10},{12,14},{19,17},{23,21},{26,24},{30,28}} | collective-permute-start | bytes 1572872 | tf_op jit(solution)/shard_map/ppermute | solution.py:290
  165.9 23.5 %collective-permute-start.27 = (bf16[128,2048]{1,0:T(8,128)(2,1)S(1)}, bf16[128,2048]{1,0:T(8,128)(2,1)}, u32[]{:S(2)}, u32[]{:S(2)}) collective-permute-start(bf16[128,2048]{1,0:T(8,128)(2,1)S(1)} %get-tuple-element.125), channel_id=1, source_target_pairs={{1,3},{5,7},{26,24},{30,28}} | collective-permute-start | bytes 1572872 | tf_op jit(solution)/shard_map/ppermute | solution.py:290
  199.7 45.9 %collective-permute-start.30 = (bf16[128,2048]{1,0:T(8,128)(2,1)S(1)}, bf16[128,2048]{1,0:T(8,128)(2,1)S(1)}, u32[]{:S(2)}, u32[]{:S(2)}) collective-permute-start(bf16[128,2048]{1,0:T(8,128)(2,1)S(1)} %shard_map.214), channel_id=1, source_target_pairs={{0,2},{1,3},{4,6},{5,7},{9,11},{11,9},{13,15},{15,13},{16,18},{18,... | collective-permute-start | bytes 1572872 | tf_op jit(solution)/shard_map/ppermute | solution.py:290
  201.0 44.6 %collective-permute-start.31 = (bf16[128,2048]{1,0:T(8,128)(2,1)S(1)}, bf16[128,2048]{1,0:T(8,128)(2,1)S(1)}, u32[]{:S(2)}, u32[]{:S(2)}) collective-permute-start(bf16[128,2048]{1,0:T(8,128)(2,1)S(1)} %shard_map.216), channel_id=1, source_target_pairs={{0,2},{3,1},{4,6},{7,5},{9,11},{10,8},{13,15},{14,12},{17,19},{18,... | collective-permute-start | bytes 1572872 | tf_op jit(solution)/shard_map/ppermute | solution.py:290
  205.0 40.6 %collective-permute-start.32 = (bf16[128,2048]{1,0:T(8,128)(2,1)S(1)}, bf16[128,2048]{1,0:T(8,128)(2,1)S(1)}, u32[]{:S(2)}, u32[]{:S(2)}) collective-permute-start(bf16[128,2048]{1,0:T(8,128)(2,1)S(1)} %get-tuple-element.146), channel_id=1, source_target_pairs={{0,1},{3,0},{4,5},{7,4},{9,10},{11,8},{13,14},{15,12},{16,17},{18,... | collective-permute-start | bytes 1572872 | tf_op jit(solution)/shard_map/ppermute | solution.py:290
  207.0 38.6 %collective-permute-start.33 = (bf16[128,2048]{1,0:T(8,128)(2,1)S(1)}, bf16[128,2048]{1,0:T(8,128)(2,1)S(1)}, u32[]{:S(2)}, u32[]{:S(2)}) collective-permute-start(bf16[128,2048]{1,0:T(8,128)(2,1)S(1)} %get-tuple-element.147), channel_id=1, source_target_pairs={{2,0},{3,1},{6,4},{7,5},{8,10},{10,8},{12,14},{14,12},{17,19},{19,... | collective-permute-start | bytes 1572872 | tf_op jit(solution)/shard_map/ppermute | solution.py:290
  208.3 37.3 %collective-permute-start.34 = (bf16[128,2048]{1,0:T(8,128)(2,1)S(1)}, bf16[128,2048]{1,0:T(8,128)(2,1)S(1)}, u32[]{:S(2)}, u32[]{:S(2)}) collective-permute-start(bf16[128,2048]{1,0:T(8,128)(2,1)S(1)} %get-tuple-element.148), channel_id=1, source_target_pairs={{1,0},{2,1},{5,4},{6,5},{9,8},{11,10},{13,12},{15,14},{16,19},{18,... | collective-permute-start | bytes 1572872 | tf_op jit(solution)/shard_map/ppermute | solution.py:290
  (48 other events, 933.3 us)
